TPU v7x, 32 devices: a whole 2x2x4 slice. The times are simulated.
32 devices in a mesh: dp: 4 (over y, x), expert: 8 (over z, core).
Axes of the slice: x: 2, y: 2, z: 4, core: 2. Of those that a mesh axis runs over, the one named last changes fastest.
Arguments:
- layer_input: bfloat16 [32768, 1024], P(('dp', 'expert')), may hold values from -6 to 6
- segments: int32 [32, 1024], P(('dp', 'expert')), may hold values from 0 to 7, never falling along the last dimension, each value on 1 to 256 neighbouring positions
- keep_mask: int32 [32, 1024], P(('dp', 'expert')), may hold values 0 or 1
- att_routes: int32 [32768, 8, 2], P(('dp', 'expert')), may hold values from 0 to 4, all different within a row
- moe_routes: int32 [32768, 16], P(('dp', 'expert')), may hold values from 0 to 47, all different within a row; in each aligned block of 1024 rows (0 to 1023, 1024 to 2047, ...) at most 488 rows name the same one
- expert_counts: int32 [48], P('expert'), may hold values from 0 to 2729
- norm_gain: float32 [1024], replicated, may hold values from 0.5 to 1.5
- w_query: bfloat16 [1024, 512], replicated, may hold values from -0.25 to 0.25
- w_key: bfloat16 [1024, 512], replicated, may hold values from -0.1875 to 0.1875
- w_select: bfloat16 [1024, 40], replicated, may hold values from -0.125 to 0.125
- w_value: bfloat16 [1024, 2560], replicated, may hold values from -0.1875 to 0.1875
- w_output: bfloat16 [2560, 1024], replicated, may hold values from -3 to 3
- w_router: bfloat16 [48, 1024], P('expert'), may hold values from -0.09375 to 0.09375
- w_in: bfloat16 [48, 1024, 128], P('expert'), may hold values from -0.1875 to 0.1875
- w_out: bfloat16 [48, 128, 1024], P('expert'), may hold values from -0.25 to 0.25
- cotangent: bfloat16 [32768, 1024], P(('dp', 'expert')), may hold values from -6 to 6
Outputs:
- layer_output: bfloat16 [32768, 1024], P(('dp', 'expert'))
- grad_input: bfloat16 [32768, 1024], P(('dp', 'expert'))
- grad_gain: float32 [1024], P(('dp', 'expert'))
- grad_query: float32 [1024, 512], P(('dp', 'expert'))
- grad_key: float32 [1024, 512], P(('dp', 'expert'))
- grad_select: float32 [1024, 40], P(('dp', 'expert'))
- grad_value: float32 [1024, 2560], P(('dp', 'expert'))
- grad_output: float32 [2560, 1024], P(None, ('dp', 'expert'))
- grad_router: float32 [48, 1024], P('expert')
- grad_w_in: float32 [48, 1024, 128], P('expert')
- grad_w_out: float32 [48, 128, 1024], P('expert')
- counts_out: int32 [48], P('expert')
Inputs may be any that keep to these rules, and one draw needn't show every extreme that they name: `moe_routes`: in each aligned block of 1024 rows (the tokens of one device), no expert is named by more than 488 pairs, a bound that some block reaches; a row names 16 different experts. `att_routes`: each row names two different experts. `segments`: never falling along a sequence; each document holds 1 to 256 tokens.
All inputs are finite; a program needn't handle non-finite values. No bound on the sum of `keep_mask` on one device may be relied on, other than what follows from the above.
Results may differ from a plain program's by a relative error of at most 0.015.
The roundings to bfloat16 on the way count: a program that leaves them out, or rounds other values in their place, can miss the bound.
Values may be sent and summed in bfloat16 or wider, within the bound.
A program may use at most 576 MiB of HBM per device.

v0:
```python
import jax
import jax.numpy as jnp
from jax import lax
from jax.sharding import PartitionSpec as P

DH = 128
VEXP = 5


NORM_EPS = 1e-05
ROPE_BASE = 10000.0
MASK_FILL = -1e30
HIGHEST = lax.Precision.HIGHEST


def layer_norm(values, gain_vec):
    center = values - jnp.mean(values, axis=-1, keepdims=True)
    spread = jnp.mean(center * center, axis=-1, keepdims=True)
    return center * lax.rsqrt(spread + NORM_EPS) * gain_vec


def rope_tables(position, width_dh):
    half_dh = width_dh // 2
    freq_row = jnp.power(ROPE_BASE, jnp.arange(half_dh, dtype=jnp.float32) * (-2.0 / width_dh))
    angle_tab = position.astype(jnp.float32)[:, None] * freq_row[None, :]
    return (jnp.cos(angle_tab), jnp.sin(angle_tab))


def rotate(values, cos_tab, sin_tab):
    half_dh = values.shape[-1] // 2
    first_half = values[..., :half_dh]
    second_half = values[..., half_dh:]
    cos_b = cos_tab[:, None, :]
    sin_b = sin_tab[:, None, :]
    return jnp.concatenate(
        [first_half * cos_b - second_half * sin_b, second_half * cos_b + first_half * sin_b],
        axis=-1,
    )


def rotate_back(grad_rot, cos_tab, sin_tab):
    half_dh = grad_rot.shape[-1] // 2
    grad_first = grad_rot[..., :half_dh]
    grad_second = grad_rot[..., half_dh:]
    cos_b = cos_tab[:, None, :]
    sin_b = sin_tab[:, None, :]
    return jnp.concatenate(
        [grad_first * cos_b + grad_second * sin_b, grad_second * cos_b - grad_first * sin_b],
        axis=-1,
    )


def doc_layout(seg_row, keep_row):
    length_s = seg_row.shape[0]
    column = jnp.arange(length_s, dtype=jnp.int32)
    new_doc = jnp.concatenate([jnp.ones((1,), dtype=jnp.bool_), seg_row[1:] != seg_row[:-1]])
    doc_start = lax.cummax(jnp.where(new_doc, column, jnp.zeros_like(column)), axis=0)
    position = column - doc_start
    same_doc = seg_row[:, None] == seg_row[None, :]
    causal = column[None, :] <= column[:, None]
    visible = (keep_row[None, :] == 1) | (column[None, :] == column[:, None])
    return (position, same_doc & causal & visible)


def slot_table(routes, exp_total, capacity):
    flat_ids = routes.reshape(-1)
    pair_count = flat_ids.shape[0]
    top_k = routes.shape[1]
    sort_order = jnp.argsort(flat_ids, stable=True)
    ranked = flat_ids[sort_order]
    first_slot = jnp.searchsorted(ranked, jnp.arange(exp_total, dtype=jnp.int32), side="left")
    slot_rank = jnp.arange(pair_count, dtype=jnp.int32) - first_slot[ranked]
    slot_dest = ranked * capacity + slot_rank
    owner = jnp.zeros((exp_total * capacity,), jnp.int32).at[slot_dest].set(sort_order // top_k)
    filled = jnp.zeros((exp_total * capacity,), jnp.float32).at[slot_dest].set(1.0)
    slot_of = (
        jnp.zeros((pair_count,), jnp.int32).at[sort_order].set(slot_dest).reshape(routes.shape)
    )
    return (owner, filled, slot_of)


def block_scores(q_blk, k_rows, allowed_blk):
    scores = jnp.einsum("qhd,khd->hqk", q_blk, k_rows, preferred_element_type=jnp.float32)
    return jnp.where(allowed_blk[None, :, :], scores, MASK_FILL)


def attend_forward(pieces):
    q_rows, k_rows, v_rows, allowed = pieces
    length_s = q_rows.shape[0]
    block_len = min(512, length_s)
    outs_list = []
    lse_list = []
    for begin_at in range(0, length_s, block_len):
        scores = block_scores(
            q_rows[begin_at : begin_at + block_len],
            k_rows,
            allowed[begin_at : begin_at + block_len],
        )
        row_max = jnp.max(scores, axis=-1, keepdims=True)
        exp_terms = jnp.exp(scores - row_max)
        row_sum = jnp.sum(exp_terms, axis=-1, keepdims=True)
        probs_bf = (exp_terms / row_sum).astype(jnp.bfloat16)
        outs_list.append(
            jnp.einsum("hqk,khd->qhd", probs_bf, v_rows, preferred_element_type=jnp.float32)
        )
        lse_list.append((row_max + jnp.log(row_sum))[..., 0])
    return (jnp.concatenate(outs_list, axis=0), jnp.concatenate(lse_list, axis=1))


def attend_backward(pieces):
    q_rows, k_rows, v_rows, allowed, log_total, grad_rows = pieces
    length_s = q_rows.shape[0]
    block_len = min(512, length_s)
    grad_q_list = []
    grad_k = jnp.zeros(k_rows.shape, jnp.float32)
    grad_v = jnp.zeros(v_rows.shape, jnp.float32)
    for begin_at in range(0, length_s, block_len):
        q_blk = q_rows[begin_at : begin_at + block_len]
        grad_blk = grad_rows[begin_at : begin_at + block_len]
        scores = block_scores(q_blk, k_rows, allowed[begin_at : begin_at + block_len])
        probs_f = jnp.exp(scores - log_total[:, begin_at : begin_at + block_len, None])
        grad_prob = jnp.einsum("qhd,khd->hqk", grad_blk, v_rows, preferred_element_type=jnp.float32)
        grad_score = (
            probs_f * (grad_prob - jnp.sum(probs_f * grad_prob, axis=-1, keepdims=True))
        ).astype(jnp.bfloat16)
        grad_v = grad_v + jnp.einsum(
            "hqk,qhd->khd",
            probs_f.astype(jnp.bfloat16),
            grad_blk,
            preferred_element_type=jnp.float32,
        )
        grad_q_list.append(
            jnp.einsum("hqk,khd->qhd", grad_score, k_rows, preferred_element_type=jnp.float32)
        )
        grad_k = grad_k + jnp.einsum(
            "hqk,qhd->khd", grad_score, q_blk, preferred_element_type=jnp.float32
        )
    return (jnp.concatenate(grad_q_list, axis=0), grad_k, grad_v)


def local(
    layer_input,
    segments,
    keep_mask,
    att_routes,
    moe_routes,
    expert_counts,
    norm_gain,
    w_query,
    w_key,
    w_select,
    w_value,
    w_output,
    w_router,
    w_in,
    w_out,
    cotangent,
):
    tok_rows, model_dim = layer_input.shape
    seq_count, seq_len = segments.shape
    head_count = w_query.shape[1] // DH
    score_scale = DH ** (-0.5)
    inputs_f = layer_input.astype(jnp.float32)
    normed, norm_pull = jax.vjp(layer_norm, inputs_f, norm_gain)
    normed_bf = normed.astype(jnp.bfloat16)
    query_rows = jnp.dot(normed_bf, w_query, preferred_element_type=jnp.float32).reshape(
        tok_rows, head_count, DH
    )
    key_rows = jnp.dot(normed_bf, w_key, preferred_element_type=jnp.float32).reshape(
        tok_rows, head_count, DH
    )
    logits = jnp.dot(layer_input, w_select, preferred_element_type=jnp.float32)
    named_mask = jnp.sum(
        (att_routes[..., None] == jnp.arange(VEXP, dtype=jnp.int32)).astype(jnp.float32), axis=2
    )
    select_sig = jax.nn.sigmoid(logits).reshape(tok_rows, 2 * head_count, VEXP)
    head_gates = select_sig * named_mask
    value_all = jnp.dot(layer_input, w_value, preferred_element_type=jnp.float32).reshape(
        tok_rows, head_count, VEXP, DH
    )
    value_bf = jnp.sum(head_gates[:, :head_count, :, None] * value_all, axis=2).astype(jnp.bfloat16)
    position, allowed = jax.vmap(doc_layout)(segments, keep_mask)
    cos_tab, sin_tab = rope_tables(position.reshape(-1), DH)
    q_rot = (rotate(query_rows, cos_tab, sin_tab) * score_scale).astype(jnp.bfloat16)
    k_rot = rotate(key_rows, cos_tab, sin_tab).astype(jnp.bfloat16)
    seq_shape = (seq_count, seq_len, head_count, DH)
    attended, log_total = lax.map(
        attend_forward,
        (q_rot.reshape(seq_shape), k_rot.reshape(seq_shape), value_bf.reshape(seq_shape), allowed),
    )
    attended = attended.reshape(tok_rows, head_count, DH)
    mixed_bf = (
        (head_gates[:, head_count:, :, None] * attended[:, :, None, :])
        .astype(jnp.bfloat16)
        .reshape(tok_rows, head_count * VEXP * DH)
    )
    hidden = inputs_f + jnp.dot(mixed_bf, w_output, preferred_element_type=jnp.float32)
    dev_count = lax.axis_size("expert")
    exp_local = w_in.shape[0]
    exp_total = dev_count * exp_local
    top_k = moe_routes.shape[1]
    capacity = 10 * tok_rows * top_k // (7 * exp_total) + 1
    owner, filled, slot_of = slot_table(moe_routes, exp_total, capacity)
    keep_slot = filled[:, None] > 0
    zero_bf = jnp.zeros((), jnp.bfloat16)
    hidden_bf = hidden.astype(jnp.bfloat16)
    send_rows = jnp.where(keep_slot, hidden_bf[owner], zero_bf).reshape(
        dev_count, exp_local * capacity, model_dim
    )
    rows_in = lax.all_to_all(send_rows, "expert", split_axis=0, concat_axis=0, tiled=True)
    histogram = jnp.zeros((exp_total,), jnp.float32).at[moe_routes.reshape(-1)].add(1.0)
    tally = lax.psum_scatter(histogram, "expert", scatter_dimension=0, tiled=True)
    slot_shape = (dev_count, exp_local, capacity, model_dim)
    rows_four = rows_in.reshape(slot_shape)
    pre_act = jnp.einsum("necd,edf->necf", rows_four, w_in, preferred_element_type=jnp.float32)
    gelu_out, gelu_pull = jax.vjp(jax.nn.gelu, pre_act)
    act_bf = gelu_out.astype(jnp.bfloat16)
    router_logit = jnp.einsum(
        "necd,ed->nec", rows_four, w_router, preferred_element_type=jnp.float32
    )
    gate_moe = jax.nn.sigmoid(router_logit)
    expert_out = jnp.einsum("necf,efd->necd", act_bf, w_out, preferred_element_type=jnp.float32)
    reply = (
        (gate_moe[..., None] * expert_out)
        .astype(jnp.bfloat16)
        .reshape(dev_count, exp_local * capacity, model_dim)
    )
    returned = lax.all_to_all(reply, "expert", split_axis=0, concat_axis=0, tiled=True)
    moe_sum = jnp.sum(returned.reshape(-1, model_dim)[slot_of].astype(jnp.float32), axis=1)
    layer_output = (hidden + moe_sum).astype(jnp.bfloat16)
    cot_f = cotangent.astype(jnp.float32)
    send_cot = jnp.where(keep_slot, cotangent[owner], zero_bf).reshape(
        dev_count, exp_local * capacity, model_dim
    )
    cot_in, rows_again = (
        lax.all_to_all(send_cot, "expert", split_axis=0, concat_axis=0, tiled=True),
        lax.all_to_all(send_rows, "expert", split_axis=0, concat_axis=0, tiled=True),
    )
    rows_grad = rows_again.reshape(slot_shape)
    cot_bf = cot_in.reshape(slot_shape)
    raw_back = jnp.einsum("necd,efd->necf", cot_bf, w_out, preferred_element_type=jnp.float32)
    dgate = jnp.sum(act_bf.astype(jnp.float32) * raw_back, axis=-1)
    dlogit = dgate * gate_moe * (1.0 - gate_moe)
    dexpert = (gate_moe[..., None] * cot_bf.astype(jnp.float32)).astype(jnp.bfloat16)
    grad_w_out = jnp.einsum("necf,necd->efd", act_bf, dexpert, preferred_element_type=jnp.float32)
    dact = jnp.einsum("necd,efd->necf", dexpert, w_out, preferred_element_type=jnp.float32)
    dpre_bf = gelu_pull(dact)[0].astype(jnp.bfloat16)
    grad_w_in = jnp.einsum("necd,necf->edf", rows_grad, dpre_bf, preferred_element_type=jnp.float32)
    grad_router = jnp.einsum(
        "nec,necd->ed",
        dlogit,
        rows_grad.astype(jnp.float32),
        preferred_element_type=jnp.float32,
        precision=HIGHEST,
    )
    dsent = jnp.einsum("necf,edf->necd", dpre_bf, w_in, preferred_element_type=jnp.float32)
    dsent = (dsent + dlogit[..., None] * w_router[None, :, None, :].astype(jnp.float32)).astype(
        jnp.bfloat16
    )
    grad_back = lax.all_to_all(
        dsent.reshape(dev_count, exp_local * capacity, model_dim),
        "expert",
        split_axis=0,
        concat_axis=0,
        tiled=True,
    )
    dhidden = cot_f + jnp.sum(grad_back.reshape(-1, model_dim)[slot_of].astype(jnp.float32), axis=1)
    dy_bf = dhidden.astype(jnp.bfloat16)
    grad_output = jnp.einsum("tk,td->kd", mixed_bf, dy_bf, preferred_element_type=jnp.float32)
    dmixed = jnp.einsum("td,kd->tk", dy_bf, w_output, preferred_element_type=jnp.float32).reshape(
        tok_rows, head_count, VEXP, DH
    )
    dgate_out = jnp.sum(dmixed * attended[:, :, None, :], axis=-1)
    dattend = jnp.sum(head_gates[:, head_count:, :, None] * dmixed, axis=2).astype(jnp.bfloat16)
    grad_q, grad_k, grad_v = lax.map(
        attend_backward,
        (
            q_rot.reshape(seq_shape),
            k_rot.reshape(seq_shape),
            value_bf.reshape(seq_shape),
            allowed,
            log_total,
            dattend.reshape(seq_shape),
        ),
    )
    dquery = (
        (rotate_back(grad_q.reshape(tok_rows, head_count, DH), cos_tab, sin_tab) * score_scale)
        .astype(jnp.bfloat16)
        .reshape(tok_rows, head_count * DH)
    )
    dkey = (
        rotate_back(grad_k.reshape(tok_rows, head_count, DH), cos_tab, sin_tab)
        .astype(jnp.bfloat16)
        .reshape(tok_rows, head_count * DH)
    )
    grad_query = jnp.einsum("td,tk->dk", normed_bf, dquery, preferred_element_type=jnp.float32)
    grad_key = jnp.einsum("td,tk->dk", normed_bf, dkey, preferred_element_type=jnp.float32)
    dnormed = jnp.einsum(
        "tk,dk->td", dquery, w_query, preferred_element_type=jnp.float32
    ) + jnp.einsum("tk,dk->td", dkey, w_key, preferred_element_type=jnp.float32)
    dx_norm, grad_gain = norm_pull(dnormed)
    dvalue = grad_v.reshape(tok_rows, head_count, DH)
    dgate_val = jnp.sum(dvalue[:, :, None, :] * value_all, axis=-1)
    dvalue_all = (
        (head_gates[:, :head_count, :, None] * dvalue[:, :, None, :])
        .astype(jnp.bfloat16)
        .reshape(tok_rows, head_count * VEXP * DH)
    )
    grad_value = jnp.einsum(
        "td,tk->dk", layer_input, dvalue_all, preferred_element_type=jnp.float32
    )
    dgates = jnp.concatenate([dgate_val, dgate_out], axis=1)
    dlogits = (
        (dgates * named_mask * select_sig * (1.0 - select_sig))
        .astype(jnp.bfloat16)
        .reshape(tok_rows, 2 * head_count * VEXP)
    )
    grad_select = jnp.einsum("td,tk->dk", layer_input, dlogits, preferred_element_type=jnp.float32)
    grad_input = (
        dhidden
        + dx_norm
        + jnp.einsum("tk,dk->td", dvalue_all, w_value, preferred_element_type=jnp.float32)
    )
    grad_input = (
        grad_input + jnp.einsum("tk,dk->td", dlogits, w_select, preferred_element_type=jnp.float32)
    ).astype(jnp.bfloat16)
    expert_sums = (
        lax.psum(grad_w_in.astype(jnp.bfloat16), "dp").astype(jnp.float32),
        lax.psum(grad_w_out.astype(jnp.bfloat16), "dp").astype(jnp.float32),
        lax.psum(grad_router.astype(jnp.bfloat16), "dp").astype(jnp.float32),
        lax.psum(tally.astype(jnp.bfloat16), "dp").astype(jnp.float32),
    )
    dense_sums = (
        lax.psum_scatter(grad_gain, ("dp", "expert"), scatter_dimension=0, tiled=True),
        lax.psum_scatter(grad_query, ("dp", "expert"), scatter_dimension=0, tiled=True),
        lax.psum_scatter(grad_key, ("dp", "expert"), scatter_dimension=0, tiled=True),
        lax.psum_scatter(grad_select, ("dp", "expert"), scatter_dimension=0, tiled=True),
        lax.psum_scatter(grad_value, ("dp", "expert"), scatter_dimension=0, tiled=True),
        lax.psum_scatter(grad_output, ("dp", "expert"), scatter_dimension=1, tiled=True),
    )
    counts_out = expert_counts + expert_sums[3].astype(jnp.int32)
    return (
        layer_output,
        grad_input,
        dense_sums[0],
        dense_sums[1],
        dense_sums[2],
        dense_sums[3],
        dense_sums[4],
        dense_sums[5],
        expert_sums[2],
        expert_sums[0],
        expert_sums[1],
        counts_out,
    )


def solution(mesh):
    placed = (
        P(("dp", "expert"), None),
        P(("dp", "expert"), None),
        P(("dp", "expert"), None),
        P(("dp", "expert"), None, None),
        P(("dp", "expert"), None),
        P("expert"),
        P(),
        P(),
        P(),
        P(),
        P(),
        P(),
        P("expert", None),
        P("expert", None, None),
        P("expert", None, None),
        P(("dp", "expert"), None),
    )
    return jax.shard_map(
        local,
        mesh=mesh,
        in_specs=placed,
        out_specs=(
            P(("dp", "expert"), None),
            P(("dp", "expert"), None),
            P(("dp", "expert")),
            P(("dp", "expert"), None),
            P(("dp", "expert"), None),
            P(("dp", "expert"), None),
            P(("dp", "expert"), None),
            P(None, ("dp", "expert")),
            P("expert", None),
            P("expert", None, None),
            P("expert", None, None),
            P("expert"),
        ),
        check_vma=False,
    )
```

profile of v0, /device:TPU:0, one launch (start us, length us, event | category | flops | bytes accessed | tf_op | source)
XLA Modules:
  0.0 5416.4 jit_solution(12257327168857357902)
XLA Ops:
  9.4 7.8 sort.17
  17.9 90.5 %gather_fusion.1 = s32[16384]{0:T(1024)S(1)} fusion(s32[16384]{0:T(1024)S(1)} %reshape.567, s32[16384]{0:T(1024)S(1)} %get-tuple-element.295), kind=kCustom, calls=%fused_computation.1 | custom fusion | bytes 196608 | tf_op jit(solution)/shard_map/gather | solution.py:70
  108.4 12.4 while.35
  137.7 10.3 compare_reduce_fusion.40
  148.0 26.6 subtract_add_fusion
  174.7 60.4 %scatter_custom_fusion.1 = s32[23424]{0:T(1024)S(1)} fusion(s32[16384]{0:T(1024)S(1)} %bitcast.282, s32[16384]{0:T(1024)S(1)} %get-tuple-element.296, s32[]{:T(128)} %constant.127.clone.1), kind=kCustom, calls=%fused_computation.242 | custom fusion | bytes 93700 | tf_op jit(solution)/shard_map/scatter | solution.py:74
  235.1 60.4 %scatter_custom_fusion = f32[23424]{0:T(1024)S(1)} fusion(s32[16384]{0:T(1024)S(1)} %bitcast.283, f32[16384]{0:T(1024)S(1)} %broadcast.462, f32[]{:T(128)} %constant.121.clone.1), kind=kCustom, calls=%fused_computation.245 | custom fusion | bytes 93700 | tf_op jit(solution)/shard_map/scatter | solution.py:75
  336.9 13.9 fusion.128
  371.8 11.1 fusion.62
  382.9 102.2 %gather_fusion.2 = bf16[23424,1024]{1,0:T(8,128)(2,1)} fusion(bf16[1024,1024]{1,0:T(8,128)(2,1)} %get-tuple-element.353, s32[23552]{0:T(1024)S(1)} %copy-done.42), kind=kCustom, calls=%fused_computation.2 | custom fusion | bytes 96038400 | tf_op jit(solution)/shard_map/gather | solution.py:207
  485.1 102.2 %gather_fusion.4 = bf16[23424,1024]{1,0:T(8,128)(2,1)} fusion(bf16[1024,1024]{1,0:T(8,128)(2,1)} %param.33, s32[23552]{0:T(1024)S(1)} %copy-done.42), kind=kCustom, calls=%fused_computation.4 | custom fusion | bytes 96038400 | tf_op jit(solution)/shard_map/gather | solution.py:232
  587.3 61.6 %broadcast_select_fusion.2 = (bf16[8,2928,1024]{2,1,0:T(8,128)(2,1)}, bf16[8,2928,1024]{2,1,0:T(8,128)(2,1)}) fusion(bf16[8,2928,1024]{2,1,0:T(8,128)(2,1)} %bitcast.261, pred[8,2928]{1,0:T(8,128)(4,1)S(1)} %copy-done.54, bf16[8,2928,1024]{2,1,0:T(8,128)(2,1)} %bitcast.260), kind=kLoop, calls=%fused_computation.25 | loop fusion | flops 47972352 | bytes 191912832 | tf_op jit(solution)/shard_map/jit(_where)/select_n | solution.py:232
  648.9 1047.2 %all_to_all.21 = bf16[8,2928,1024]{2,1,0:T(8,128)(2,1)} all-to-all(bf16[8,2928,1024]{2,1,0:T(8,128)(2,1)} %get-tuple-element.298), channel_id=1, replica_groups=mesh['dp'=4,'expert'=8] {'expert'}, dimensions={0} | all-to-all | bytes 95944704 | tf_op jit(solution)/shard_map/all_to_all | solution.py:210
  1696.1 8.5 all-to-all-start.2
  1704.7 19.2 fusion.10
  1723.9 25.4 fusion.12
  1749.2 987.6 %all-to-all-done.2 = bf16[8,2928,1024]{2,1,0:T(8,128)(2,1)} async-done(((bf16[8,2928,1024]{2,1,0:T(8,128)(2,1)}), bf16[8,2928,1024]{2,1,0:T(8,128)(2,1)}, u32[]{:S(2)}, u32[]{:S(2)}) %all-to-all-start.2) | async-done | bytes 47972384 | tf_op jit(solution)/shard_map/all_to_all | solution.py:236
  2736.8 22.6 fusion.23
  2759.5 27.0 fusion.22
  2786.5 21.5 fusion.4
  2808.0 32.1 copy.172
  2840.1 8.3 all-to-all-start.3
  2848.4 22.8 fusion.5
  2871.3 32.0 copy.169
  2903.3 977.3 %all-to-all-done.3 = bf16[8,2928,1024]{2,1,0:T(8,128)(2,1)} async-done(((bf16[8,2928,1024]{2,1,0:T(8,128)(2,1)}), bf16[8,2928,1024]{2,1,0:T(8,128)(2,1)}, u32[]{:S(2)}, u32[]{:S(2)}) %all-to-all-start.3) | async-done | bytes 47972384 | tf_op jit(solution)/shard_map/all_to_all | solution.py:260
  3880.6 8.5 all-to-all-start.1
  3889.2 60.7 %scatter_custom_fusion.2 = s32[16384]{0:T(1024)S(1)} fusion(s32[16384]{0:T(1024)} %get-tuple-element.294, s32[16384]{0:T(1024)} %get-tuple-element.265, s32[]{:T(128)} %constant.127.clone.1), kind=kCustom, calls=%fused_computation.250 | custom fusion | bytes 66048 | tf_op jit(solution)/shard_map/scatter | solution.py:77
  3951.6 23.4 bitcast_convert_fusion.1
  3975.0 24.5 bitcast_convert_fusion
  3999.6 301.1 %gather_fusion.5 = bf16[16384,1024]{1,0:T(8,128)(2,1)} fusion(bf16[23424,1024]{1,0:T(8,128)(2,1)} %bitcast.86, s32[16384]{0:T(1024)S(1)} %broadcast_clamp_fusion), kind=kCustom, calls=%fused_computation.5 | custom fusion | bytes 67174400 | tf_op jit(solution)/shard_map/gather | solution.py:267
  4300.7 17.6 convert_reduce_fusion
  4318.4 11.5 fusion.117
  4330.0 7.2 multiply_reduce_fusion
  4359.4 9.6 multiply_convert_fusion.5
  4369.0 8.4 multiply_reduce_fusion.1
  4406.2 11.7 fusion.115
  4417.9 11.0 convolution_bitcast_fusion
  4428.9 11.5 copy.223
  4442.4 113.7 %scatter_custom_fusion.3 = f32[48]{0:T(128)S(1)} fusion(s32[16384]{0:T(1024)S(1)} %bitcast.284, f32[16384]{0:T(1024)} %copy-done.67, f32[]{:T(128)} %constant.121.clone.1), kind=kCustom, calls=%fused_computation.272 | custom fusion | flops 16384 | bytes 704 | tf_op jit(solution)/shard_map/scatter-add | solution.py:211
  4556.7 117.0 %all-reduce.1 = bf16[48]{0:T(256)(128)(2,1)S(1)} all-reduce(f32[48]{0:T(128)S(1)} %scatter_custom_fusion.3), channel_id=8, replica_groups=mesh['dp'=4,'expert'=8] {'expert'}, use_global_device_ids=true, to_apply=%region_37.38.clone | all-reduce | flops 48 | bytes 288
  4673.8 28.5 fusion.8
  4702.4 20.1 all-reduce.2
  4729.1 219.7 %all-to-all-done.1 = bf16[8,2928,1024]{2,1,0:T(8,128)(2,1)} async-done(((bf16[8,2928,1024]{2,1,0:T(8,128)(2,1)}), bf16[8,2928,1024]{2,1,0:T(8,128)(2,1)}, u32[]{:S(2)}, u32[]{:S(2)}) %all-to-all-start.1) | async-done | bytes 47972384 | tf_op jit(solution)/shard_map/all_to_all | solution.py:228
  4948.7 302.1 %gather_fusion.3 = bf16[16384,1024]{1,0:T(8,128)(2,1)} fusion(bf16[23424,1024]{1,0:T(8,128)(2,1)} %bitcast.76, s32[16384]{0:T(1024)S(1)} %broadcast_clamp_fusion), kind=kCustom, calls=%fused_computation.3 | custom fusion | bytes 67174400 | tf_op jit(solution)/shard_map/gather | solution.py:229
  5257.9 17.5 convert_reduce_fusion.1
  5282.6 100.5 %all-reduce = f32[1024]{0:T(1024)S(1)} all-reduce(f32[1024]{0:T(1024)S(1)} %get-tuple-element.210), channel_id=2, replica_groups=mesh['dp'=4,'expert'=8] {'dp','expert'}, use_global_device_ids=true, to_apply=%region_27.28.clone | all-reduce | flops 1024 | bytes 8192
  5383.8 9.4 fusion.132
  5396.8 11.8 reduce-scatter.18.cloned.1.call-done
  (352 shorter events, 172.6 us)
Async XLA Ops:
  8.0 2728.8 %copy-start = (bf16[6,128,1024]{2,1,0:T(8,128)(2,1)S(1)}, bf16[6,128,1024]{2,1,0:T(8,128)(2,1)}, u32[]{:S(2)}) copy-start(bf16[6,128,1024]{2,1,0:T(8,128)(2,1)} %param.32) | copy-start | bytes 4718596
  17.9 105.1 %copy-start.73 = (s32[1,1024]{1,0:T(1,128)S(1)}, s32[1,1024]{1,0:T(1,128)}, u32[]{:S(2)}) copy-start(s32[1,1024]{1,0:T(1,128)} %param.20) | copy-start | bytes 12292
  17.9 105.1 %copy-start.65 = (s32[1,1024]{1,0:T(1,128)S(1)}, s32[1,1024]{1,0:T(1,128)}, u32[]{:S(2)}) copy-start(s32[1,1024]{1,0:T(1,128)} %param.19) | copy-start | bytes 12292
  108.4 19.8 copy-start.66
  108.4 20.4 copy-start.55
  125.8 173.4 %copy-start.49 = (f32[1024]{0:T(1024)}, f32[1024]{0:T(1024)S(1)}, u32[]{:S(2)}) copy-start(f32[1024]{0:T(1024)S(1)} %broadcast_multiply_fusion) | copy-start | bytes 12292
  128.2 171.1 %copy-start.63 = (f32[1024]{0:T(1024)}, f32[1024]{0:T(1024)S(1)}, u32[]{:S(2)}) copy-start(f32[1024]{0:T(1024)S(1)} %fusion.108) | copy-start | bytes 12292
  128.8 170.5 %copy-start.36 = (f32[1024,8,5]{0,1,2:T(8,128)}, f32[1024,8,5]{0,1,2:T(8,128)S(1)}, u32[]{:S(2)}) copy-start(f32[1024,8,5]{0,1,2:T(8,128)S(1)} %convert_reduce_fusion.3) | copy-start | bytes 491524
  128.8 170.5 %copy-start.61 = (f32[1024]{0:T(1024)S(1)}, f32[1024]{0:T(1024)}, u32[]{:S(2)}) copy-start(f32[1024]{0:T(1024)} %param.24) | copy-start | bytes 12292
  131.2 170.8 %copy-start.45 = (f32[1024,40]{0,1:T(8,128)}, f32[1024,40]{0,1:T(8,128)S(1)}, u32[]{:S(2)}) copy-start(f32[1024,40]{0,1:T(8,128)S(1)} %fusion.78) | copy-start | bytes 491524
  235.1 70.3 %copy-start.67 = (f32[16384]{0:T(1024)}, f32[16384]{0:T(1024)S(1)}, u32[]{:S(2)}) copy-start(f32[16384]{0:T(1024)S(1)} %broadcast.462) | copy-start | bytes 196612
  299.3 63.3 %copy-start.13 = (pred[512,1024]{1,0:T(8,128)(4,1)}, pred[512,1024]{1,0:T(8,128)(4,1)S(1)}, u32[]{:S(2)}) copy-start(pred[512,1024]{1,0:T(8,128)(4,1)S(1)} %get-tuple-element.289) | copy-start | bytes 1572868
  299.3 67.3 %copy-start.11 = (pred[512,1024]{1,0:T(8,128)(4,1)}, pred[512,1024]{1,0:T(8,128)(4,1)S(1)}, u32[]{:S(2)}) copy-start(pred[512,1024]{1,0:T(8,128)(4,1)S(1)} %get-tuple-element.288) | copy-start | bytes 1572868
  333.7 28.9 copy-start.4
  333.7 28.9 copy-start.57
  336.9 29.7 copy-start.5
  336.9 29.7 copy-start.59
  355.9 10.7 copy-start.70
  369.6 13.2 copy-start.15
  370.9 12.0 copy-start.27
  371.8 11.1 copy-start.42
  485.1 102.2 %copy-start.54 = (pred[8,2928]{1,0:T(8,128)(4,1)S(1)}, pred[8,2928]{1,0:T(8,128)(4,1)}, u32[]{:S(2)}) copy-start(pred[8,2928]{1,0:T(8,128)(4,1)} %broadcast_in_dim.194) | copy-start | bytes 70276
  1696.1 1040.7 %all-to-all-start.2 = ((bf16[8,2928,1024]{2,1,0:T(8,128)(2,1)}), bf16[8,2928,1024]{2,1,0:T(8,128)(2,1)}, u32[]{:S(2)}, u32[]{:S(2)}) async-start(bf16[8,2928,1024]{2,1,0:T(8,128)(2,1)} %get-tuple-element.297), calls=%async_computation.2 | async-start | bytes 95944704 | tf_op jit(solution)/shard_map/all_to_all | solution.py:236
  2759.5 27.0 copy-start.47
  2840.1 1040.5 %all-to-all-start.3 = ((bf16[8,2928,1024]{2,1,0:T(8,128)(2,1)}), bf16[8,2928,1024]{2,1,0:T(8,128)(2,1)}, u32[]{:S(2)}, u32[]{:S(2)}) async-start(bf16[8,2928,1024]{2,1,0:T(8,128)(2,1)} %bitcast.259), calls=%async_computation.3 | async-start | bytes 95944704 | tf_op jit(solution)/shard_map/all_to_all | solution.py:260
  3880.6 69.7 %copy-start.58 = (f32[4,512]{1,0:T(4,128)S(1)}, f32[4,512]{1,0:T(4,128)}, u32[]{:S(2)}) copy-start(f32[4,512]{1,0:T(4,128)} %copy-done.57) | copy-start | bytes 24580
  3880.6 69.7 %copy-start.72 = (f32[4,512]{1,0:T(4,128)S(1)}, f32[4,512]{1,0:T(4,128)}, u32[]{:S(2)}) copy-start(f32[4,512]{1,0:T(4,128)} %fusion.29) | copy-start | bytes 24580
  3880.6 70.3 %copy-start.60 = (f32[4,512]{1,0:T(4,128)S(1)}, f32[4,512]{1,0:T(4,128)}, u32[]{:S(2)}) copy-start(f32[4,512]{1,0:T(4,128)} %copy-done.59) | copy-start | bytes 24580
  3880.6 70.3 %copy-start.71 = (f32[4,512]{1,0:T(4,128)S(1)}, f32[4,512]{1,0:T(4,128)}, u32[]{:S(2)}) copy-start(f32[4,512]{1,0:T(4,128)} %copy-done.70) | copy-start | bytes 24580
  3880.6 1068.1 %all-to-all-start.1 = ((bf16[8,2928,1024]{2,1,0:T(8,128)(2,1)}), bf16[8,2928,1024]{2,1,0:T(8,128)(2,1)}, u32[]{:S(2)}, u32[]{:S(2)}) async-start(bf16[8,2928,1024]{2,1,0:T(8,128)(2,1)} %bitcast.258), calls=%async_computation.1 | async-start | bytes 95944704 | tf_op jit(solution)/shard_map/all_to_all | solution.py:228
  3889.1 834.5 %all-reduce.6.cloned.1.call-start = ((), (), s32[]{:S(2)}) async-start(), calls=%async_computation.14 | async-start | bytes 6291456 | tf_op jit(solution)/shard_map/psum | solution.py:328
  3999.6 1397.3 %reduce-scatter.16.cloned.1.call-start = ((), (), s32[]{:S(2)}) async-start(), calls=%async_computation.12 | async-start | bytes 540672
  4300.7 17.6 copy-start.2
  4318.4 11.6 copy-start.16
  4318.4 11.6 copy-start.40
  4338.9 12.5 slice-start
  4344.2 10.0 slice-start.2
  4359.4 9.6 copy-start.26
  4359.4 9.6 copy-start.38
  4392.9 1003.9 %reduce-scatter.12.cloned.1.call-start = ((), (), s32[]{:S(2)}) async-start(), calls=%async_computation.10 | async-start | bytes 2162688 | tf_op jit(solution)/shard_map/reduce_scatter | solution.py:336
  4397.2 999.6 %reduce-scatter.10.cloned.1.call-start = ((), (), s32[]{:S(2)}) async-start(), calls=%async_computation.9 | async-start | bytes 2162688 | tf_op jit(solution)/shard_map/reduce_scatter | solution.py:335
  4406.1 990.7 %reduce-scatter.14.cloned.1.call-start = ((), (), s32[]{:S(2)}) async-start(), calls=%async_computation.11 | async-start | bytes 10813440 | tf_op jit(solution)/shard_map/reduce_scatter | solution.py:339
  4417.9 990.8 %reduce-scatter.18.cloned.1.call-start = ((), (), s32[]{:S(2)}) async-start(), calls=%async_computation.13 | async-start | bytes 10813440
  4440.4 233.4 %copy-start.48 = (f32[8,6,488]{2,0,1:T(8,128)S(1)}, f32[8,6,488]{2,0,1:T(8,128)}, u32[]{:S(2)}) copy-start(f32[8,6,488]{2,0,1:T(8,128)} %copy-done.47) | copy-start | bytes 281092
  4673.8 49.3 copy-start.74
  5257.9 17.5 copy-start.64
  5383.7 9.4 copy-start.19
  5383.8 24.9 copy-start.1
  (41 other events, 212.1 us)
Sparse Core Ops, SparseCore 0:
  3999.7 91.8 all-reduce.5
Sparse Core Ops, SparseCore 1:
  4393.0 384.8 reduce-scatter.15
  4780.6 170.3 reduce-scatter.11
  4953.7 139.8 reduce-scatter.9
  5096.5 153.4 reduce-scatter.13
  5252.9 155.7 reduce-scatter.17
where the time goes:
time: 5440 us; the launch traced here: 5420 us
  waiting for transfers between devices  2200 us (40%)
  blocking collectives  1280 us (24%)
  local copies, waits for them, and re-layouts  1200 us (22%)
  matrix products  352 us (6%)
  other arithmetic  340 us (6%)
    all_to_all x1, blocking collectives, local(): lax.all_to_all(send_rows, 'expert', split_axis=0, concat_axis=0, tiled=True)  1050 us
    all_to_all x1, waiting for transfers between devices, local(): lax.all_to_all(send_cot, 'expert', split_axis=0, concat_axis=0, tiled=True)  988 us
    all_to_all x1, waiting for transfers between devices, local(): lax.all_to_all(dsent.reshape(dev_count, exp_local * capacity, model_dim),...  977 us
    gather x1, local copies, waits for them, and re-layouts, local(): returned.reshape(-1, model_dim)[slot_of].astype(jnp.float32)  302 us
    gather x1, local copies, waits for them, and re-layouts, local(): grad_back.reshape(-1, model_dim)[slot_of].astype(jnp.float32)  301 us
    all_to_all x1, waiting for transfers between devices, local(): lax.all_to_all(reply, 'expert', split_axis=0, concat_axis=0, tiled=True)  220 us
    unnamed x2, blocking collectives  217 us
    scatter-add x1, other arithmetic, local(): jnp.zeros((exp_total,), jnp.float32).at[moe_routes.reshape(-1)].add(1.0)  114 us
  transfers between devices with their start and end apart: 9, of which 4 were waited for; matrix products, arithmetic and copies ran while one was open for 21% of the time, Pallas kernels for 0%

commit v1 on v0

--- a/solution.py
+++ b/solution.py
@@ -138,6 +138,128 @@
     return (jnp.concatenate(grad_q_list, axis=0), grad_k, grad_v)
 
 
+def moe_dispatched(hidden, moe_routes, w_router, w_in, w_out, cotangent, capacity):
+    dev_count = lax.axis_size("expert")
+    exp_local = w_in.shape[0]
+    exp_total = dev_count * exp_local
+    tok_rows, model_dim = hidden.shape
+    owner, filled, slot_of = slot_table(moe_routes, exp_total, capacity)
+    keep_slot = filled[:, None] > 0
+    zero_bf = jnp.zeros((), jnp.bfloat16)
+    hidden_bf = hidden.astype(jnp.bfloat16)
+    send_rows = jnp.where(keep_slot, hidden_bf[owner], zero_bf).reshape(
+        dev_count, exp_local * capacity, model_dim
+    )
+    rows_in = lax.all_to_all(send_rows, "expert", split_axis=0, concat_axis=0, tiled=True)
+    histogram = jnp.zeros((exp_total,), jnp.float32).at[moe_routes.reshape(-1)].add(1.0)
+    tally = lax.psum_scatter(histogram, "expert", scatter_dimension=0, tiled=True)
+    slot_shape = (dev_count, exp_local, capacity, model_dim)
+    rows_four = rows_in.reshape(slot_shape)
+    pre_act = jnp.einsum("necd,edf->necf", rows_four, w_in, preferred_element_type=jnp.float32)
+    gelu_out, gelu_pull = jax.vjp(jax.nn.gelu, pre_act)
+    act_bf = gelu_out.astype(jnp.bfloat16)
+    router_logit = jnp.einsum(
+        "necd,ed->nec", rows_four, w_router, preferred_element_type=jnp.float32
+    )
+    gate_moe = jax.nn.sigmoid(router_logit)
+    expert_out = jnp.einsum("necf,efd->necd", act_bf, w_out, preferred_element_type=jnp.float32)
+    reply = (
+        (gate_moe[..., None] * expert_out)
+        .astype(jnp.bfloat16)
+        .reshape(dev_count, exp_local * capacity, model_dim)
+    )
+    returned = lax.all_to_all(reply, "expert", split_axis=0, concat_axis=0, tiled=True)
+    moe_sum = jnp.sum(returned.reshape(-1, model_dim)[slot_of].astype(jnp.float32), axis=1)
+    layer_output = (hidden + moe_sum).astype(jnp.bfloat16)
+    cot_f = cotangent.astype(jnp.float32)
+    send_cot = jnp.where(keep_slot, cotangent[owner], zero_bf).reshape(
+        dev_count, exp_local * capacity, model_dim
+    )
+    cot_in, rows_again = (
+        lax.all_to_all(send_cot, "expert", split_axis=0, concat_axis=0, tiled=True),
+        lax.all_to_all(send_rows, "expert", split_axis=0, concat_axis=0, tiled=True),
+    )
+    rows_grad = rows_again.reshape(slot_shape)
+    cot_bf = cot_in.reshape(slot_shape)
+    raw_back = jnp.einsum("necd,efd->necf", cot_bf, w_out, preferred_element_type=jnp.float32)
+    dgate = jnp.sum(act_bf.astype(jnp.float32) * raw_back, axis=-1)
+    dlogit = dgate * gate_moe * (1.0 - gate_moe)
+    dexpert = (gate_moe[..., None] * cot_bf.astype(jnp.float32)).astype(jnp.bfloat16)
+    grad_w_out = jnp.einsum("necf,necd->efd", act_bf, dexpert, preferred_element_type=jnp.float32)
+    dact = jnp.einsum("necd,efd->necf", dexpert, w_out, preferred_element_type=jnp.float32)
+    dpre_bf = gelu_pull(dact)[0].astype(jnp.bfloat16)
+    grad_w_in = jnp.einsum("necd,necf->edf", rows_grad, dpre_bf, preferred_element_type=jnp.float32)
+    grad_router = jnp.einsum(
+        "nec,necd->ed",
+        dlogit,
+        rows_grad.astype(jnp.float32),
+        preferred_element_type=jnp.float32,
+        precision=HIGHEST,
+    )
+    dsent = jnp.einsum("necf,edf->necd", dpre_bf, w_in, preferred_element_type=jnp.float32)
+    dsent = (dsent + dlogit[..., None] * w_router[None, :, None, :].astype(jnp.float32)).astype(
+        jnp.bfloat16
+    )
+    grad_back = lax.all_to_all(
+        dsent.reshape(dev_count, exp_local * capacity, model_dim),
+        "expert",
+        split_axis=0,
+        concat_axis=0,
+        tiled=True,
+    )
+    dhidden = cot_f + jnp.sum(grad_back.reshape(-1, model_dim)[slot_of].astype(jnp.float32), axis=1)
+    return (layer_output, dhidden, grad_w_in, grad_w_out, grad_router, tally)
+
+
+def moe_dense(hidden, moe_routes, w_router, w_in, w_out, cotangent, capacity):
+    exp_local = w_in.shape[0]
+    exp_total = lax.axis_size("expert") * exp_local
+    win_all = lax.all_gather(w_in, "expert", axis=0, tiled=True)
+    wout_all = lax.all_gather(w_out, "expert", axis=0, tiled=True)
+    router_all = lax.all_gather(w_router, "expert", axis=0, tiled=True)
+    hidden_bf = hidden.astype(jnp.bfloat16)
+    named_exp = jnp.sum(
+        (moe_routes[..., None] == jnp.arange(exp_total, dtype=jnp.int32)).astype(jnp.float32), axis=1
+    )
+    tally = lax.psum_scatter(jnp.sum(named_exp, axis=0), "expert", scatter_dimension=0, tiled=True)
+    router_logit = jnp.einsum("td,ed->te", hidden_bf, router_all, preferred_element_type=jnp.float32)
+    gate_sig = jax.nn.sigmoid(router_logit)
+    gate_moe = gate_sig * named_exp
+    pre_act = jnp.einsum("td,edf->tef", hidden_bf, win_all, preferred_element_type=jnp.float32)
+    gelu_out, gelu_pull = jax.vjp(jax.nn.gelu, pre_act)
+    act_bf = gelu_out.astype(jnp.bfloat16)
+    gated_bf = (gate_moe[..., None] * act_bf.astype(jnp.float32)).astype(jnp.bfloat16)
+    moe_sum = jnp.einsum("tef,efd->td", gated_bf, wout_all, preferred_element_type=jnp.float32)
+    layer_output = (hidden + moe_sum).astype(jnp.bfloat16)
+    cot_f = cotangent.astype(jnp.float32)
+    raw_back = jnp.einsum("td,efd->tef", cotangent, wout_all, preferred_element_type=jnp.float32)
+    dgate = jnp.sum(act_bf.astype(jnp.float32) * raw_back, axis=-1)
+    dlogit = dgate * gate_moe * (1.0 - gate_sig)
+    dpre_bf = gelu_pull(gate_moe[..., None] * raw_back)[0].astype(jnp.bfloat16)
+    grad_w_out = jnp.einsum("tef,td->efd", gated_bf, cotangent, preferred_element_type=jnp.float32)
+    grad_w_in = jnp.einsum("td,tef->edf", hidden_bf, dpre_bf, preferred_element_type=jnp.float32)
+    grad_router = jnp.einsum(
+        "te,td->ed",
+        dlogit,
+        hidden_bf.astype(jnp.float32),
+        preferred_element_type=jnp.float32,
+        precision=HIGHEST,
+    )
+    dsent = jnp.einsum("tef,edf->td", dpre_bf, win_all, preferred_element_type=jnp.float32)
+    dsent = dsent + jnp.einsum(
+        "te,ed->td",
+        dlogit,
+        router_all.astype(jnp.float32),
+        preferred_element_type=jnp.float32,
+        precision=HIGHEST,
+    )
+    dhidden = cot_f + dsent
+    grad_w_in = lax.psum_scatter(grad_w_in.astype(jnp.bfloat16), "expert", scatter_dimension=0, tiled=True)
+    grad_w_out = lax.psum_scatter(grad_w_out.astype(jnp.bfloat16), "expert", scatter_dimension=0, tiled=True)
+    grad_router = lax.psum_scatter(grad_router, "expert", scatter_dimension=0, tiled=True)
+    return (layer_output, dhidden, grad_w_in, grad_w_out, grad_router, tally)
+
+
 def local(
     layer_input,
     segments,
@@ -195,76 +317,13 @@
         .reshape(tok_rows, head_count * VEXP * DH)
     )
     hidden = inputs_f + jnp.dot(mixed_bf, w_output, preferred_element_type=jnp.float32)
-    dev_count = lax.axis_size("expert")
-    exp_local = w_in.shape[0]
-    exp_total = dev_count * exp_local
     top_k = moe_routes.shape[1]
+    exp_total = lax.axis_size("expert") * w_in.shape[0]
     capacity = 10 * tok_rows * top_k // (7 * exp_total) + 1
-    owner, filled, slot_of = slot_table(moe_routes, exp_total, capacity)
-    keep_slot = filled[:, None] > 0
-    zero_bf = jnp.zeros((), jnp.bfloat16)
-    hidden_bf = hidden.astype(jnp.bfloat16)
-    send_rows = jnp.where(keep_slot, hidden_bf[owner], zero_bf).reshape(
-        dev_count, exp_local * capacity, model_dim
-    )
-    rows_in = lax.all_to_all(send_rows, "expert", split_axis=0, concat_axis=0, tiled=True)
-    histogram = jnp.zeros((exp_total,), jnp.float32).at[moe_routes.reshape(-1)].add(1.0)
-    tally = lax.psum_scatter(histogram, "expert", scatter_dimension=0, tiled=True)
-    slot_shape = (dev_count, exp_local, capacity, model_dim)
-    rows_four = rows_in.reshape(slot_shape)
-    pre_act = jnp.einsum("necd,edf->necf", rows_four, w_in, preferred_element_type=jnp.float32)
-    gelu_out, gelu_pull = jax.vjp(jax.nn.gelu, pre_act)
-    act_bf = gelu_out.astype(jnp.bfloat16)
-    router_logit = jnp.einsum(
-        "necd,ed->nec", rows_four, w_router, preferred_element_type=jnp.float32
-    )
-    gate_moe = jax.nn.sigmoid(router_logit)
-    expert_out = jnp.einsum("necf,efd->necd", act_bf, w_out, preferred_element_type=jnp.float32)
-    reply = (
-        (gate_moe[..., None] * expert_out)
-        .astype(jnp.bfloat16)
-        .reshape(dev_count, exp_local * capacity, model_dim)
-    )
-    returned = lax.all_to_all(reply, "expert", split_axis=0, concat_axis=0, tiled=True)
-    moe_sum = jnp.sum(returned.reshape(-1, model_dim)[slot_of].astype(jnp.float32), axis=1)
-    layer_output = (hidden + moe_sum).astype(jnp.bfloat16)
-    cot_f = cotangent.astype(jnp.float32)
-    send_cot = jnp.where(keep_slot, cotangent[owner], zero_bf).reshape(
-        dev_count, exp_local * capacity, model_dim
-    )
-    cot_in, rows_again = (
-        lax.all_to_all(send_cot, "expert", split_axis=0, concat_axis=0, tiled=True),
-        lax.all_to_all(send_rows, "expert", split_axis=0, concat_axis=0, tiled=True),
-    )
-    rows_grad = rows_again.reshape(slot_shape)
-    cot_bf = cot_in.reshape(slot_shape)
-    raw_back = jnp.einsum("necd,efd->necf", cot_bf, w_out, preferred_element_type=jnp.float32)
-    dgate = jnp.sum(act_bf.astype(jnp.float32) * raw_back, axis=-1)
-    dlogit = dgate * gate_moe * (1.0 - gate_moe)
-    dexpert = (gate_moe[..., None] * cot_bf.astype(jnp.float32)).astype(jnp.bfloat16)
-    grad_w_out = jnp.einsum("necf,necd->efd", act_bf, dexpert, preferred_element_type=jnp.float32)
-    dact = jnp.einsum("necd,efd->necf", dexpert, w_out, preferred_element_type=jnp.float32)
-    dpre_bf = gelu_pull(dact)[0].astype(jnp.bfloat16)
-    grad_w_in = jnp.einsum("necd,necf->edf", rows_grad, dpre_bf, preferred_element_type=jnp.float32)
-    grad_router = jnp.einsum(
-        "nec,necd->ed",
-        dlogit,
-        rows_grad.astype(jnp.float32),
-        preferred_element_type=jnp.float32,
-        precision=HIGHEST,
-    )
-    dsent = jnp.einsum("necf,edf->necd", dpre_bf, w_in, preferred_element_type=jnp.float32)
-    dsent = (dsent + dlogit[..., None] * w_router[None, :, None, :].astype(jnp.float32)).astype(
-        jnp.bfloat16
-    )
-    grad_back = lax.all_to_all(
-        dsent.reshape(dev_count, exp_local * capacity, model_dim),
-        "expert",
-        split_axis=0,
-        concat_axis=0,
-        tiled=True,
-    )
-    dhidden = cot_f + jnp.sum(grad_back.reshape(-1, model_dim)[slot_of].astype(jnp.float32), axis=1)
+    moe_layer = moe_dense if 4 * capacity > tok_rows else moe_dispatched
+    layer_output, dhidden, grad_w_in, grad_w_out, grad_router, tally = moe_layer(
+        hidden, moe_routes, w_router, w_in, w_out, cotangent, capacity
+    )
     dy_bf = dhidden.astype(jnp.bfloat16)
     grad_output = jnp.einsum("tk,td->kd", mixed_bf, dy_bf, preferred_element_type=jnp.float32)
     dmixed = jnp.einsum("td,kd->tk", dy_bf, w_output, preferred_element_type=jnp.float32).reshape(

time: 5440 us -> 1390 us (0.26)
  waiting for transfers between devices: 2200 us -> 831 us
  blocking collectives: 1280 us -> 100 us
  local copies, waits for them, and re-layouts: 1200 us -> 74.1 us
  other arithmetic: 340 us -> 70 us
  matrix products: 352 us -> 285 us
    all_to_all x3 -> x0, waiting for transfers between devices: 2180 us -> none  [the longest x1 988 us: local(): lax.all_to_all(send_cot, 'expert', split_axis=0, concat_axis=0, tiled=True)]
    all_to_all x1 -> x0, blocking collectives: 1050 us -> none  [local(): lax.all_to_all(send_rows, 'expert', split_axis=0, concat_axis=0, tiled=True)]
    gather x23 -> x0, local copies, waits for them, and re-layouts: 912 us -> none  [the longest x1 302 us: local(): returned.reshape(-1, model_dim)[slot_of].astype(jnp.float32)]
    scatter x3 -> x0, local copies, waits for them, and re-layouts: 181 us -> none  [the longest x1 60.7 us: slot_table(): jnp.zeros((pair_count,), jnp.int32).at[sort_order].set(slot_dest)]
    reduce_scatter x0 -> x2, waiting for transfers between devices: none -> 161 us  [the longest x1 130 us: moe_dense(): lax.psum_scatter(grad_w_out.astype(jnp.bfloat16), 'expert', scatter_dimen...]
    reduce_scatter x1, waiting for transfers between devices: 0.01 us -> 157 us  [local(): lax.psum_scatter(grad_output, ('dp', 'expert'), scatter_dimension=1, tile...]
    unnamed x2 -> x3, blocking collectives: 217 us -> 68.1 us
    unnamed x8 -> x14, waiting for transfers between devices: 11.9 us -> 159 us
  transfers between devices with their start and end apart: 9 -> 12, of which waited for: 4 -> 8; matrix products, arithmetic and copies ran while one was open for 21% -> 27% of each run, Pallas kernels for 0% -> 0%
where the time goes in v1:
time: 1390 us; the launch traced here: 1380 us
  waiting for transfers between devices  831 us (60%)
  matrix products  285 us (21%)
  blocking collectives  100 us (7%)
  local copies, waits for them, and re-layouts  74.1 us (5%)
  other arithmetic  70 us (5%)
  between operations  16.8 us (1%)
    unnamed x14, waiting for transfers between devices  159 us
    reduce_scatter x1, waiting for transfers between devices, local(): lax.psum_scatter(grad_output, ('dp', 'expert'), scatter_dimension=1, tile...  157 us
    reduce_scatter x1, waiting for transfers between devices, local(): lax.psum_scatter(grad_query, ('dp', 'expert'), scatter_dimension=0, tiled...  136 us
    reduce_scatter x1, waiting for transfers between devices, moe_dense(): lax.psum_scatter(grad_w_out.astype(jnp.bfloat16), 'expert', scatter_dimen...  130 us
    reduce_scatter x1, waiting for transfers between devices, local(): lax.psum_scatter(grad_key, ('dp', 'expert'), scatter_dimension=0, tiled=T...  126 us
    all_gather x1, waiting for transfers between devices, moe_dense(): wout_all = lax.all_gather(w_out, 'expert', axis=0, tiled=True)  79.1 us
    unnamed x3, blocking collectives  68.1 us
    unnamed x170, local copies, waits for them, and re-layouts  44.4 us
  transfers between devices with their start and end apart: 12, of which 8 were waited for; matrix products, arithmetic and copies ran while one was open for 27% of the time, Pallas kernels for 0%

profile of v1, /device:TPU:0, one launch (start us, length us, event | category | flops | bytes accessed | tf_op | source)
XLA Modules:
  0.0 1382.2 jit_solution(7413300847584423367)
XLA Ops:
  11.8 16.0 %all-gather = bf16[8,6,1024]{2,1,0:T(8,128)(2,1)S(1)} all-gather(bf16[1,6,1024]{2,1,0:T(8,128)(2,1)} %bitcast.147), channel_id=1, replica_groups=mesh['dp'=4,'expert'=8] {'expert'}, dimensions={0}, use_global_device_ids=true | all-gather | bytes 110592 | tf_op jit(solution)/shard_map/all_gather | solution.py:219
  27.9 3.1 fusion.66
  41.3 3.2 copy.215
  44.5 3.2 fusion.99
  49.1 3.2 copy.214
  52.3 3.2 copy.213
  57.5 4.4 multiply_subtract_fusion.1
  70.1 14.0 %fusion.98 = f32[1024,2560]{0,1:T(8,128)} fusion(bf16[1024,1024]{1,0:T(8,128)(2,1)S(1)} %copy-done.4, bf16[1024,2560]{1,0:T(8,128)(2,1)} %param.26), kind=kOutput, calls=%fused_computation.174 | convolution fusion | flops 5368709120 | bytes 17825792 | tf_op jit(solution)/shard_map/dot_general | solution.py:300
  84.0 6.8 multiply_reduce_fusion.3
  104.4 10.9 fusion.48
  116.7 12.6 all-gather.4.cloned.1.call-done
  129.3 16.6 %copy.164 = bf16[48,1024,128]{1,2,0:T(8,128)(2,1)} copy(bf16[48,1024,128]{2,1,0:T(8,128)(2,1)} %all-gather.4.cloned.1.call-done) | data formatting | bytes 25165824 | tf_op jit(solution)/shard_map/all_gather | solution.py:217
  146.0 20.9 %fusion.101 = f32[1024,6144]{0,1} fusion(bf16[1024,1024]{1,0:T(8,128)(2,1)S(1)} %get-tuple-element.165, bf16[1024,6144]{0,1:T(8,128)(2,1)} %bitcast.132), kind=kOutput, calls=%fused_computation.177 | convolution fusion | flops 12884901888 | bytes 39845888
  166.8 79.1 %all-gather.6.cloned.1.call-done = bf16[48,128,1024]{2,1,0:T(8,128)(2,1)} async-done(((bf16[6,128,1024]{2,1,0:T(8,128)(2,1)}), bf16[48,128,1024]{2,1,0:T(8,128)(2,1)}) %all-gather.6.cloned.1.call-update) | async-done | bytes 12582928 | tf_op jit(solution)/shard_map/all_gather | solution.py:218
  245.9 38.6 %fusion.2 = (f32[1024,48]{0,1:T(8,128)}, bf16[1024,48,128]{0,2,1:T(8,128)(2,1)}) fusion(f32[1024,48,128]{0,2,1:T(8,128)} %bitcast.152, f32[1024,48]{0,1:T(8,128)S(1)} %get-tuple-element.167, bf16[48,128,1024]{2,1,0:T(8,128)(2,1)} %all-gather.6.cloned.1.call-done, bf16[1024,1024]{1,0:T(8,128)(2,1)} %param.31), kind=kOutput, calls=%fused_computation.5 | convolution fusion | flops 13048430592 | bytes 52822016 | tf_op jit(solution)/shard_map/td,efd->tef/dot_general | solution.py:235
  284.5 20.2 %convert_bitcast_fusion = bf16[48,1024,128]{1,2,0:T(8,128)(2,1)} fusion(bf16[1024,48,128]{0,2,1:T(8,128)(2,1)} %get-tuple-element.134, bf16[1024,1024]{1,0:T(8,128)(2,1)S(1)} %get-tuple-element.165), kind=kOutput, calls=%fused_computation.14 | convolution fusion | flops 12891193344 | bytes 27262976 | tf_op jit(solution)/shard_map/td,tef->edf/dot_general | solution.py:240
  306.3 23.8 %fusion.16 = bf16[48,128,1024]{2,1,0:T(8,128)(2,1)} fusion(f32[1024,48]{0,1:T(8,128)S(1)} %get-tuple-element.167, bf16[1024,1024]{1,0:T(8,128)(2,1)S(1)} %copy-done.31, f32[1024,48,128]{0,2,1:T(8,128)} %bitcast.153), kind=kOutput, calls=%fused_computation.35 | convolution fusion | flops 12966690816 | bytes 40042496 | tf_op jit(solution)/shard_map/tef,td->efd/dot_general | solution.py:239
  330.9 17.4 %fusion.102 = f32[1024,1024,1]{1,0,2:T(8,128)S(1)} fusion(bf16[1024,48,128]{0,2,1:T(8,128)(2,1)} %get-tuple-element.134, bf16[48,1024,128]{2,1,0:T(8,128)(2,1)} %all-gather.4.cloned.1.call-done), kind=kOutput, calls=%fused_computation.178 | convolution fusion | flops 12884901888 | bytes 29360128 | tf_op jit(solution)/shard_map/tef,edf->td/dot_general | solution.py:248
  350.5 12.7 fusion.69
  363.2 7.4 multiply_reduce_fusion
  372.2 5.0 fusion.29
  377.2 7.1 add_bitcast_fusion
  387.2 5.0 multiply_reduce_fusion.5
  392.2 9.3 multiply_convert_fusion.3
  401.5 30.9 %reduce-scatter.20.cloned.1.call-done = bf16[6,1024,128]{1,2,0:T(8,128)(2,1)} async-done(((bf16[48,1024,128]{1,2,0:T(8,128)(2,1)}), bf16[6,1024,128]{1,2,0:T(8,128)(2,1)}) %reduce-scatter.20.cloned.1.call-update) | async-done | bytes 1572880 | tf_op jit(solution)/shard_map/reduce_scatter | solution.py:257
  432.3 129.8 %reduce-scatter.22.cloned.1.call-done = bf16[6,128,1024]{2,1,0:T(8,128)(2,1)} async-done(((bf16[48,128,1024]{2,1,0:T(8,128)(2,1)}), bf16[6,128,1024]{2,1,0:T(8,128)(2,1)}) %reduce-scatter.22.cloned.1.call-update) | async-done | bytes 1572880 | tf_op jit(solution)/shard_map/reduce_scatter | solution.py:258
  562.4 9.0 multiply_reduce_fusion.1
  578.8 4.1 fusion.80
  594.7 4.6 fusion.106
  599.7 3.9 fusion.52
  605.9 4.6 fusion.105
  610.5 11.4 fusion.67
  622.0 11.0 convolution_bitcast_fusion
  633.0 11.7 copy.211
  647.3 13.6 all-reduce.2
  661.4 3.5 fusion.91
  665.0 16.1 %fusion = f32[8,1024]{1,0:T(8,128)S(1)} fusion(f32[48,1024]{1,0:T(8,128)} %fusion.91), kind=kCustom, calls=%all-reduce-scatter | all-reduce-scatter fusion | flops 65537 | bytes 229888
  693.4 3.0 fusion.28
  697.1 7.2 fusion.104
  704.3 23.6 %fusion.36 = bf16[1024,1024]{1,0:T(8,128)(2,1)} fusion(f32[1024,1024]{1,0:T(8,128)} %get-tuple-element.166, bf16[1024,1024]{1,0:T(8,128)(2,1)S(1)} %copy-done.6, bf16[48,128,1024]{2,1,0:T(8,128)(2,1)} %all-gather.6.cloned.1.call-done, f32[1024,48]{0,1:T(8,128)S(1)} %get-tuple-element.167, f32[1024,48,128]{0,2,1:T(8,128)} %bitcast.154), kind=kOutput, calls=%fused_computation.62 | convolution fusion | flops 12964593664 | bytes 46333952 | tf_op jit(solution)/shard_map/tef,efd->td/dot_general | solution.py:232
  727.9 6.8 add_convert_fusion
  734.7 38.4 %all-reduce = f32[1024]{0:T(1024)S(1)} all-reduce(f32[1024]{0:T(1024)S(1)} %copy-done.64), channel_id=2, replica_groups=mesh['dp'=4,'expert'=8] {'dp','expert'}, use_global_device_ids=true, to_apply=%region_20.21.clone | all-reduce | flops 1024 | bytes 8192
  775.4 16.2 %all-reduce.4 = (bf16[6,1024]{1,0:T(8,128)(2,1)S(1)}, bf16[6]{0:T(256)(128)(2,1)S(1)}) all-reduce(bf16[6,1024]{1,0:T(8,128)(2,1)S(1)} %dynamic-slice_convert_fusion, bf16[6]{0:T(256)(128)(2,1)S(1)} %copy-done.68), channel_id=1, replica_groups=mesh['dp'=4,'expert'=8] {'dp'}, use_global_device_ids=true, to_apply=%region_27.28 | all-reduce | flops 6150 | bytes 24600 | tf_op jit(solution)/shard_map/psum | solution.py:389
  792.7 3.2 copy.190
  797.9 125.9 %reduce-scatter.16.cloned.1.call-done = f32[32,512]{1,0:T(8,128)} async-done(((f32[1024,512]{1,0:T(8,128)}), f32[32,512]{1,0:T(8,128)}) %reduce-scatter.16.cloned.1.call-update) | async-done | bytes 65552 | tf_op jit(solution)/shard_map/reduce_scatter | solution.py:395
  923.9 136.0 %reduce-scatter.14.cloned.1.call-done = f32[32,512]{1,0:T(8,128)} async-done(((f32[1024,512]{1,0:T(8,128)}), f32[32,512]{1,0:T(8,128)}) %reduce-scatter.14.cloned.1.call-update) | async-done | bytes 65552 | tf_op jit(solution)/shard_map/reduce_scatter | solution.py:394
  1059.9 157.5 %reduce-scatter.18.cloned.1.call-done = f32[2560,32]{0,1:T(8,128)} async-done(((f32[2560,1024]{0,1:T(8,128)}), f32[2560,32]{0,1:T(8,128)}) %reduce-scatter.18.cloned.1.call-update) | async-done | bytes 327696 | tf_op jit(solution)/shard_map/reduce_scatter | solution.py:398
  1217.3 157.8 %reduce-scatter.26.cloned.1.call-done = f32[32,2560]{1,0:T(8,128)} async-done(((f32[1024,2560]{1,0:T(8,128)}), f32[32,2560]{1,0:T(8,128)}) %reduce-scatter.26.cloned.1.call-update) | async-done | bytes 327696
  (263 shorter events, 92.4 us)
Async XLA Ops:
  7.2 29.5 %copy-start = (bf16[1024,512]{1,0:T(8,128)(2,1)S(1)}, bf16[1024,512]{1,0:T(8,128)(2,1)}, u32[]{:S(2)}) copy-start(bf16[1024,512]{1,0:T(8,128)(2,1)} %param.24) | copy-start | bytes 3145732
  7.2 26.5 %copy-start.3 = (bf16[1024,1024]{1,0:T(8,128)(2,1)S(1)}, bf16[1024,1024]{1,0:T(8,128)(2,1)}, u32[]{:S(2)}) copy-start(bf16[1024,1024]{1,0:T(8,128)(2,1)} %param.16) | copy-start | bytes 6291460
  7.2 122.1 %all-gather.4.cloned.1.call-start = ((), (), s32[]{:S(2)}) async-start(), calls=%async_computation.7 | async-start | bytes 14155776 | tf_op jit(solution)/shard_map/all_gather | solution.py:217
  7.9 238.0 %all-gather.6.cloned.1.call-start = ((), (), s32[]{:S(2)}) async-start(), calls=%async_computation.8 | async-start | bytes 14155776 | tf_op jit(solution)/shard_map/all_gather | solution.py:218
  8.7 423.6 %reduce-scatter.20.cloned.1.call-start = ((), (), s32[]{:S(2)}) async-start(), calls=%async_computation.12 | async-start | bytes 14155776 | tf_op jit(solution)/shard_map/reduce_scatter | solution.py:257
  27.8 87.4 %copy-start.39 = (bf16[48,1024]{1,0:T(8,128)(2,1)}, bf16[48,1024]{1,0:T(8,128)(2,1)S(1)}, u32[]{:S(2)}) copy-start(bf16[48,1024]{1,0:T(8,128)(2,1)S(1)} %reshape.425) | copy-start | bytes 294916
  27.9 8.1 copy-start.54
  33.6 69.5 %copy-start.37 = (f32[1024,4,5]{0,2,1:T(8,128)}, f32[1024,4,5]{0,2,1:T(8,128)S(1)}, u32[]{:S(2)}) copy-start(f32[1024,4,5]{0,2,1:T(8,128)S(1)} %copy.157) | copy-start | bytes 245764
  33.7 50.3 %copy-start.36 = (f32[1024,4,5]{0,2,1:T(8,128)}, f32[1024,4,5]{0,2,1:T(8,128)S(1)}, u32[]{:S(2)}) copy-start(f32[1024,4,5]{0,2,1:T(8,128)S(1)} %copy.158) | copy-start | bytes 245764
  65.4 30.0 %copy-start.10 = (pred[512,1024]{1,0:T(8,128)(4,1)}, pred[512,1024]{1,0:T(8,128)(4,1)S(1)}, u32[]{:S(2)}) copy-start(pred[512,1024]{1,0:T(8,128)(4,1)S(1)} %get-tuple-element.152) | copy-start | bytes 1572868
  65.4 33.0 %copy-start.8 = (pred[512,1024]{1,0:T(8,128)(4,1)}, pred[512,1024]{1,0:T(8,128)(4,1)S(1)}, u32[]{:S(2)}) copy-start(pred[512,1024]{1,0:T(8,128)(4,1)S(1)} %get-tuple-element.151) | copy-start | bytes 1572868
  66.8 28.6 %copy-start.1 = (f32[4,512,1024]{2,1,0:T(8,128)}, f32[4,512,1024]{2,1,0:T(8,128)S(1)}, u32[]{:S(2)}) copy-start(f32[4,512,1024]{2,1,0:T(8,128)S(1)} %get-tuple-element.162) | copy-start | bytes 25165828
  66.8 28.6 %copy-start.48 = (f32[4,512]{1,0:T(4,128)}, f32[4,512]{1,0:T(4,128)S(1)}, u32[]{:S(2)}) copy-start(f32[4,512]{1,0:T(4,128)S(1)} %get-tuple-element.161) | copy-start | bytes 24580
  70.1 28.4 %copy-start.2 = (f32[4,512,1024]{2,1,0:T(8,128)}, f32[4,512,1024]{2,1,0:T(8,128)S(1)}, u32[]{:S(2)}) copy-start(f32[4,512,1024]{2,1,0:T(8,128)S(1)} %get-tuple-element.164) | copy-start | bytes 25165828
  70.1 28.4 %copy-start.50 = (f32[4,512]{1,0:T(4,128)}, f32[4,512]{1,0:T(4,128)S(1)}, u32[]{:S(2)}) copy-start(f32[4,512]{1,0:T(4,128)S(1)} %get-tuple-element.163) | copy-start | bytes 24580
  102.0 13.2 copy-start.12
  104.4 10.9 copy-start.24
  115.3 169.2 %copy-start.23 = (bf16[1024,1024]{1,0:T(8,128)(2,1)}, bf16[1024,1024]{1,0:T(8,128)(2,1)S(1)}, u32[]{:S(2)}) copy-start(bf16[1024,1024]{1,0:T(8,128)(2,1)S(1)} %get-tuple-element.165) | copy-start | bytes 6291460
  304.7 257.4 %reduce-scatter.22.cloned.1.call-start = ((), (), s32[]{:S(2)}) async-start(), calls=%async_computation.13 | async-start | bytes 14155776 | tf_op jit(solution)/shard_map/reduce_scatter | solution.py:258
  330.1 462.6 %all-reduce.8.cloned.1.call-start = ((), (), s32[]{:S(2)}) async-start(), calls=%async_computation.16 | async-start | bytes 6291456 | tf_op jit(solution)/shard_map/psum | solution.py:387
  330.8 17.4 %copy-start.32 = (f32[1024,48]{0,1:T(8,128)S(1)}, f32[1024,48]{0,1:T(8,128)}, u32[]{:S(2)}) copy-start(f32[1024,48]{0,1:T(8,128)} %get-tuple-element.168) | copy-start | bytes 589828
  330.9 17.4 %copy-start.40 = (bf16[48,1024]{1,0:T(8,128)(2,1)S(1)}, bf16[48,1024]{1,0:T(8,128)(2,1)}, u32[]{:S(2)}) copy-start(bf16[48,1024]{1,0:T(8,128)(2,1)} %copy-done.39) | copy-start | bytes 294916
  330.9 17.4 %copy-start.41 = (f32[1024,48]{0,1:T(8,128)S(1)}, f32[1024,48]{0,1:T(8,128)}, u32[]{:S(2)}) copy-start(f32[1024,48]{0,1:T(8,128)} %get-tuple-element.133) | copy-start | bytes 589828
  350.4 12.7 copy-start.16
  350.4 12.7 copy-start.13
  350.4 12.7 copy-start.38
  363.2 9.0 copy-start.11
  372.2 12.1 slice-start
  377.2 7.1 slice-start.1
  377.2 9.9 slice-start.2
  562.1 13.6 copy-start.6
  562.1 235.8 %reduce-scatter.24.cloned.1.call-start = ((), (), s32[]{:S(2)}) async-start(), calls=%async_computation.14 | async-start | bytes 540672
  562.4 9.1 copy-start.44
  562.4 9.2 copy-start.35
  594.6 329.3 %reduce-scatter.16.cloned.1.call-start = ((), (), s32[]{:S(2)}) async-start(), calls=%async_computation.10 | async-start | bytes 2162688 | tf_op jit(solution)/shard_map/reduce_scatter | solution.py:395
  599.3 460.6 %reduce-scatter.14.cloned.1.call-start = ((), (), s32[]{:S(2)}) async-start(), calls=%async_computation.9 | async-start | bytes 2162688 | tf_op jit(solution)/shard_map/reduce_scatter | solution.py:394
  610.5 606.8 %reduce-scatter.18.cloned.1.call-start = ((), (), s32[]{:S(2)}) async-start(), calls=%async_computation.11 | async-start | bytes 10813440 | tf_op jit(solution)/shard_map/reduce_scatter | solution.py:398
  622.0 753.2 %reduce-scatter.26.cloned.1.call-start = ((), (), s32[]{:S(2)}) async-start(), calls=%async_computation.15 | async-start | bytes 10813440
  682.3 91.3 %collective-permute-start = (bf16[8,1024]{1,0:T(8,128)(2,1)}, bf16[8,1024]{1,0:T(8,128)(2,1)}, u32[]{:S(2)}, u32[]{:S(2)}) collective-permute-start(bf16[8,1024]{1,0:T(8,128)(2,1)} %convert.20), channel_id=1, source_target_pairs={{0,1},{1,2},{2,3},{3,4},{4,5},{5,6},{6,7},{8,9},{9,10},{10,11},{11... | collective-permute-start | bytes 49160
  684.3 89.3 %collective-permute-start.1 = (bf16[6,1024]{1,0:T(8,128)(2,1)}, bf16[6,1024]{1,0:T(8,128)(2,1)}, u32[]{:S(2)}, u32[]{:S(2)}) collective-permute-start(bf16[6,1024]{1,0:T(8,128)(2,1)} %slice.120), channel_id=1, source_target_pairs={{0,2},{1,3},{2,4},{3,5},{4,6},{5,7},{8,10},{9,11},{10,12},{11,13},... | collective-permute-start | bytes 36872
  686.2 10.8 slice-start.4
  686.2 10.8 slice-start.6
  689.2 7.8 slice-start.5
  689.3 7.8 slice-start.7
  704.3 23.6 %copy-start.43 = (bf16[1024,40]{0,1:T(8,128)(2,1)S(1)}, bf16[1024,40]{0,1:T(8,128)(2,1)}, u32[]{:S(2)}) copy-start(bf16[1024,40]{0,1:T(8,128)(2,1)} %copy-done.42) | copy-start | bytes 245764
  704.3 23.6 %copy-start.47 = (bf16[1024,40]{0,1:T(8,128)(2,1)S(1)}, bf16[1024,40]{0,1:T(8,128)(2,1)}, u32[]{:S(2)}) copy-start(bf16[1024,40]{0,1:T(8,128)(2,1)} %param.25) | copy-start | bytes 245764
  727.9 47.5 %copy-start.68 = (bf16[6]{0:T(256)(128)(2,1)S(1)}, bf16[6]{0:T(256)(128)(2,1)}, u32[]{:S(2)}) copy-start(bf16[6]{0:T(256)(128)(2,1)} %dynamic-slice.16) | copy-start | bytes 40
  727.9 64.3 %copy-start.69 = (s32[6]{0:T(128)S(1)}, s32[6]{0:T(128)}, u32[]{:S(2)}) copy-start(s32[6]{0:T(128)} %param.21) | copy-start | bytes 76
  (42 other events, 122.5 us)
Sparse Core Ops, SparseCore 0:
  9.7 119.5 all-gather.3
  131.0 114.9 all-gather.5
  304.9 127.4 reduce-scatter.19
  434.5 127.5 reduce-scatter.21
  565.1 85.7 all-reduce.7
  653.6 134.1 reduce-scatter.23
  790.6 133.2 reduce-scatter.15
  926.8 133.0 reduce-scatter.13
  1062.8 154.5 reduce-scatter.17
  1220.1 155.0 reduce-scatter.25

commit v2 on v1

--- a/solution.py
+++ b/solution.py
@@ -11,6 +11,9 @@
 ROPE_BASE = 10000.0
 MASK_FILL = -1e30
 HIGHEST = lax.Precision.HIGHEST
+ROUTER_ROWS = 64
+DIGITS = 5
+LANE = 128
 
 
 def layer_norm(values, gain_vec):
@@ -208,55 +211,161 @@
         tiled=True,
     )
     dhidden = cot_f + jnp.sum(grad_back.reshape(-1, model_dim)[slot_of].astype(jnp.float32), axis=1)
-    return (layer_output, dhidden, grad_w_in, grad_w_out, grad_router, tally)
+    expert_sums = (
+        lax.psum(grad_w_in.astype(jnp.bfloat16), "dp").astype(jnp.float32),
+        lax.psum(grad_w_out.astype(jnp.bfloat16), "dp").astype(jnp.float32),
+        lax.psum(grad_router.astype(jnp.bfloat16), "dp").astype(jnp.float32),
+        lax.psum(tally, "dp").astype(jnp.int32),
+    )
+    return (layer_output, dhidden) + expert_sums
+
+
+def core_swap(arr):
+    size = lax.axis_size("expert")
+    return lax.ppermute(arr, "expert", [(i, i ^ 1) for i in range(size)])
+
+
+def chip_shift(arr, hop):
+    size = lax.axis_size("expert")
+    chips = size // 2
+    return lax.ppermute(
+        arr, "expert", [(i, (i // 2 + hop) % chips * 2 + i % 2) for i in range(size)]
+    )
+
+
+def dp_swap(arr, flip):
+    return lax.ppermute(arr, "dp", [(i, i ^ flip) for i in range(lax.axis_size("dp"))])
+
+
+def row_part(arr, index, count):
+    return lax.dynamic_slice_in_dim(arr, index * (arr.shape[0] // count), arr.shape[0] // count, 0)
+
+
+def dp_gather(part):
+    mine = lax.axis_index("dp")
+    rows = part.shape[0]
+    whole = jnp.zeros((4 * rows,) + part.shape[1:], part.dtype)
+    for flip in range(4):
+        piece = part if flip == 0 else dp_swap(part, flip)
+        whole = lax.dynamic_update_slice_in_dim(whole, piece, (mine ^ flip) * rows, 0)
+    return whole
+
+
+def dp_scatter(whole):
+    mine = lax.axis_index("dp")
+    total = row_part(whole, mine, 4).astype(jnp.float32)
+    for flip in range(1, 4):
+        total = total + dp_swap(row_part(whole, mine ^ flip, 4), flip).astype(jnp.float32)
+    return total
+
+
+def scatter_rows(whole):
+    dev_count = lax.axis_size("expert")
+    chips = dev_count // 2
+    rows, width = whole.shape
+    mine = lax.axis_index("expert")
+    chip, core = mine // 2, mine % 2
+    by_core = whole.reshape(4 * chips, 2, rows // (8 * chips), width)
+    kept = lax.dynamic_index_in_dim(by_core, core, 1, keepdims=False)
+    given = lax.dynamic_index_in_dim(by_core, 1 - core, 1, keepdims=False)
+    pair = (kept.astype(jnp.float32) + core_swap(given).astype(jnp.float32)).astype(jnp.bfloat16)
+    quarter = dp_scatter(pair.reshape(rows // 2, width)).astype(jnp.bfloat16)
+    total = row_part(quarter, chip, chips).astype(jnp.float32)
+    for hop in range(1, chips):
+        piece = row_part(quarter, (chip + hop) % chips, chips)
+        total = total + chip_shift(piece, hop).astype(jnp.float32)
+    return total
+
+
+def gather_weights(w_router, w_in, w_out):
+    exp_local, model_dim, ff_dim = w_in.shape
+    chips = lax.axis_size("expert") // 2
+    router_rows = jnp.zeros((ROUTER_ROWS, model_dim), jnp.bfloat16).at[:exp_local].set(w_router)
+    own = jnp.concatenate(
+        [
+            jnp.swapaxes(w_in, 1, 2).reshape(exp_local * ff_dim, model_dim),
+            router_rows,
+            w_out.reshape(exp_local * ff_dim, model_dim),
+        ]
+    )
+    quarter = row_part(own, lax.axis_index("dp"), 4)
+    chunks = [own] + [None] * (chips - 1)
+    for hop in range(2, chips):
+        chunks[hop] = dp_gather(chip_shift(quarter, -hop))
+    if chips > 1:
+        chunks[1] = chip_shift(own, -1)
+    return chunks
 
 
 def moe_dense(hidden, moe_routes, w_router, w_in, w_out, cotangent, capacity):
-    exp_local = w_in.shape[0]
-    exp_total = lax.axis_size("expert") * exp_local
-    win_all = lax.all_gather(w_in, "expert", axis=0, tiled=True)
-    wout_all = lax.all_gather(w_out, "expert", axis=0, tiled=True)
-    router_all = lax.all_gather(w_router, "expert", axis=0, tiled=True)
+    tok_rows, model_dim = hidden.shape
+    exp_local, _, ff_dim = w_in.shape
+    dev_count = lax.axis_size("expert")
+    chips = dev_count // 2
+    wide = exp_local * ff_dim
+    mine = lax.axis_index("expert")
+    chip, core = mine // 2, mine % 2
+    chunks = gather_weights(w_router, w_in, w_out)
+    named = jnp.sum(
+        (moe_routes[..., None] == jnp.arange(dev_count * exp_local, dtype=jnp.int32)).astype(
+            jnp.bfloat16
+        ),
+        axis=1,
+    )
+    named = jnp.concatenate([named, core_swap(named)])
+    cot_two = jnp.concatenate([cotangent, core_swap(cotangent)])
     hidden_bf = hidden.astype(jnp.bfloat16)
-    named_exp = jnp.sum(
-        (moe_routes[..., None] == jnp.arange(exp_total, dtype=jnp.int32)).astype(jnp.float32), axis=1
-    )
-    tally = lax.psum_scatter(jnp.sum(named_exp, axis=0), "expert", scatter_dimension=0, tiled=True)
-    router_logit = jnp.einsum("td,ed->te", hidden_bf, router_all, preferred_element_type=jnp.float32)
-    gate_sig = jax.nn.sigmoid(router_logit)
-    gate_moe = gate_sig * named_exp
-    pre_act = jnp.einsum("td,edf->tef", hidden_bf, win_all, preferred_element_type=jnp.float32)
-    gelu_out, gelu_pull = jax.vjp(jax.nn.gelu, pre_act)
-    act_bf = gelu_out.astype(jnp.bfloat16)
-    gated_bf = (gate_moe[..., None] * act_bf.astype(jnp.float32)).astype(jnp.bfloat16)
-    moe_sum = jnp.einsum("tef,efd->td", gated_bf, wout_all, preferred_element_type=jnp.float32)
-    layer_output = (hidden + moe_sum).astype(jnp.bfloat16)
-    cot_f = cotangent.astype(jnp.float32)
-    raw_back = jnp.einsum("td,efd->tef", cotangent, wout_all, preferred_element_type=jnp.float32)
-    dgate = jnp.sum(act_bf.astype(jnp.float32) * raw_back, axis=-1)
-    dlogit = dgate * gate_moe * (1.0 - gate_sig)
-    dpre_bf = gelu_pull(gate_moe[..., None] * raw_back)[0].astype(jnp.bfloat16)
-    grad_w_out = jnp.einsum("tef,td->efd", gated_bf, cotangent, preferred_element_type=jnp.float32)
-    grad_w_in = jnp.einsum("td,tef->edf", hidden_bf, dpre_bf, preferred_element_type=jnp.float32)
-    grad_router = jnp.einsum(
-        "te,td->ed",
-        dlogit,
-        hidden_bf.astype(jnp.float32),
-        preferred_element_type=jnp.float32,
-        precision=HIGHEST,
-    )
-    dsent = jnp.einsum("tef,edf->td", dpre_bf, win_all, preferred_element_type=jnp.float32)
-    dsent = dsent + jnp.einsum(
-        "te,ed->td",
-        dlogit,
-        router_all.astype(jnp.float32),
-        preferred_element_type=jnp.float32,
-        precision=HIGHEST,
-    )
-    dhidden = cot_f + dsent
-    grad_w_in = lax.psum_scatter(grad_w_in.astype(jnp.bfloat16), "expert", scatter_dimension=0, tiled=True)
-    grad_w_out = lax.psum_scatter(grad_w_out.astype(jnp.bfloat16), "expert", scatter_dimension=0, tiled=True)
-    grad_router = lax.psum_scatter(grad_router, "expert", scatter_dimension=0, tiled=True)
+    sent_two = jnp.concatenate([hidden_bf, core_swap(hidden_bf)])
+    out_two = jnp.zeros((2 * tok_rows, model_dim), jnp.float32)
+    grad_two = jnp.zeros((2 * tok_rows, model_dim), jnp.float32)
+    grads = [None] * chips
+    for hop in [0] + list(range(2, chips)) + [1]:
+        w_ext = chunks[hop][: wide + ROUTER_ROWS]
+        w_back = chunks[hop][wide + ROUTER_ROWS :]
+        first = ((chip + hop) % chips * 2 + core) * exp_local
+        mask = lax.dynamic_slice_in_dim(named, first, exp_local, 1).astype(jnp.float32)
+        pre_ext = jnp.einsum("td,fd->tf", sent_two, w_ext, preferred_element_type=jnp.float32)
+        gate_sig = jax.nn.sigmoid(pre_ext[:, wide : wide + exp_local])
+        gate = gate_sig * mask
+        gate_wide = jnp.repeat(gate, ff_dim, axis=1)
+        gelu_out, gelu_pull = jax.vjp(jax.nn.gelu, pre_ext[:, :wide])
+        act_f = gelu_out.astype(jnp.bfloat16).astype(jnp.float32)
+        gated_bf = (gate_wide * act_f).astype(jnp.bfloat16)
+        raw_back = jnp.einsum("td,fd->tf", cot_two, w_back, preferred_element_type=jnp.float32)
+        dgate = jnp.sum((act_f * raw_back).reshape(-1, exp_local, ff_dim), axis=-1)
+        dlogit = dgate * gate * (1.0 - gate_sig)
+        dpre = gelu_pull(gate_wide * raw_back)[0]
+        dpre_ext = jnp.concatenate(
+            [dpre, jnp.pad(dlogit, ((0, 0), (0, ROUTER_ROWS - exp_local)))], axis=1
+        ).astype(jnp.bfloat16)
+        out_two = out_two + jnp.dot(gated_bf, w_back, preferred_element_type=jnp.float32)
+        grad_two = grad_two + jnp.dot(dpre_ext, w_ext, preferred_element_type=jnp.float32)
+        grad_ext = jnp.einsum("tf,td->fd", dpre_ext, sent_two, preferred_element_type=jnp.float32)
+        grad_back = jnp.einsum("tf,td->fd", gated_bf, cot_two, preferred_element_type=jnp.float32)
+        chunk_grad = jnp.concatenate([grad_ext, grad_back]).astype(jnp.bfloat16)
+        counts = jnp.sum(mask, axis=0).astype(jnp.int32)
+        digits = jnp.stack([(counts >> (2 * place)) & 3 for place in range(DIGITS)])
+        grads[hop] = chunk_grad.at[
+            wide + exp_local : wide + exp_local + DIGITS, :exp_local
+        ].set(digits.astype(jnp.bfloat16))
+    back = core_swap(grad_two[tok_rows:].astype(jnp.bfloat16))
+    dhidden = cotangent.astype(jnp.float32) + grad_two[:tok_rows] + back.astype(jnp.float32)
+    back = core_swap(out_two[tok_rows:].astype(jnp.bfloat16))
+    layer_output = (hidden + out_two[:tok_rows] + back.astype(jnp.float32)).astype(jnp.bfloat16)
+    near = grads[0].astype(jnp.float32)
+    if chips > 1:
+        near = near + chip_shift(grads[1], 1).astype(jnp.float32)
+    total = 0.0
+    for hop in range(2, chips):
+        part = dp_scatter(grads[hop]).astype(jnp.bfloat16)
+        total = total + chip_shift(part, hop).astype(jnp.float32)
+    total = total + dp_scatter(near.astype(jnp.bfloat16))
+    summed = dp_gather(total.astype(jnp.bfloat16)).astype(jnp.float32)
+    grad_w_in = jnp.swapaxes(summed[:wide].reshape(exp_local, ff_dim, model_dim), 1, 2)
+    grad_router = summed[wide : wide + exp_local]
+    digits = summed[wide + exp_local : wide + exp_local + DIGITS, :exp_local].astype(jnp.int32)
+    tally = sum(digits[place] << (2 * place) for place in range(DIGITS))
+    grad_w_out = summed[wide + ROUTER_ROWS :].reshape(exp_local, ff_dim, model_dim)
     return (layer_output, dhidden, grad_w_in, grad_w_out, grad_router, tally)
 
 
@@ -320,7 +429,8 @@
     top_k = moe_routes.shape[1]
     exp_total = lax.axis_size("expert") * w_in.shape[0]
     capacity = 10 * tok_rows * top_k // (7 * exp_total) + 1
-    moe_layer = moe_dense if 4 * capacity > tok_rows else moe_dispatched
+    dense = 4 * capacity > tok_rows
+    moe_layer = moe_dense if dense else moe_dispatched
     layer_output, dhidden, grad_w_in, grad_w_out, grad_router, tally = moe_layer(
         hidden, moe_routes, w_router, w_in, w_out, cotangent, capacity
     )
@@ -383,33 +493,39 @@
     grad_input = (
         grad_input + jnp.einsum("tk,dk->td", dlogits, w_select, preferred_element_type=jnp.float32)
     ).astype(jnp.bfloat16)
-    expert_sums = (
-        lax.psum(grad_w_in.astype(jnp.bfloat16), "dp").astype(jnp.float32),
-        lax.psum(grad_w_out.astype(jnp.bfloat16), "dp").astype(jnp.float32),
-        lax.psum(grad_router.astype(jnp.bfloat16), "dp").astype(jnp.float32),
-        lax.psum(tally.astype(jnp.bfloat16), "dp").astype(jnp.float32),
-    )
-    dense_sums = (
-        lax.psum_scatter(grad_gain, ("dp", "expert"), scatter_dimension=0, tiled=True),
-        lax.psum_scatter(grad_query, ("dp", "expert"), scatter_dimension=0, tiled=True),
-        lax.psum_scatter(grad_key, ("dp", "expert"), scatter_dimension=0, tiled=True),
-        lax.psum_scatter(grad_select, ("dp", "expert"), scatter_dimension=0, tiled=True),
-        lax.psum_scatter(grad_value, ("dp", "expert"), scatter_dimension=0, tiled=True),
-        lax.psum_scatter(grad_output, ("dp", "expert"), scatter_dimension=1, tiled=True),
-    )
-    counts_out = expert_counts + expert_sums[3].astype(jnp.int32)
+    if dense:
+        wide, narrow, few = head_count * VEXP * DH, head_count * DH, 2 * head_count * VEXP
+        filler = jnp.zeros((model_dim, -(few + 1) % LANE), jnp.float32)
+        joined = jnp.concatenate(
+            [grad_value, grad_query, grad_key, grad_select, grad_gain[:, None], filler], axis=1
+        ).astype(jnp.bfloat16)
+        summed = scatter_rows(joined)
+        out_sum = scatter_rows(grad_output.T.astype(jnp.bfloat16)).T
+        cuts = [0, wide, wide + narrow, wide + 2 * narrow, wide + 2 * narrow + few]
+        value_sum, query_sum, key_sum, select_sum = [
+            summed[:, cuts[i] : cuts[i + 1]] for i in range(4)
+        ]
+        gain_sum = summed[:, cuts[4]]
+    else:
+        both = ("dp", "expert")
+        gain_sum, query_sum, key_sum, select_sum, value_sum = [
+            lax.psum_scatter(grad, both, scatter_dimension=0, tiled=True)
+            for grad in (grad_gain, grad_query, grad_key, grad_select, grad_value)
+        ]
+        out_sum = lax.psum_scatter(grad_output, both, scatter_dimension=1, tiled=True)
+    counts_out = expert_counts + tally
     return (
         layer_output,
         grad_input,
-        dense_sums[0],
-        dense_sums[1],
-        dense_sums[2],
-        dense_sums[3],
-        dense_sums[4],
-        dense_sums[5],
-        expert_sums[2],
-        expert_sums[0],
-        expert_sums[1],
+        gain_sum,
+        query_sum,
+        key_sum,
+        select_sum,
+        value_sum,
+        out_sum,
+        grad_router,
+        grad_w_in,
+        grad_w_out,
         counts_out,
     )
 

time: 1390 us -> 809 us (0.58)
  waiting for transfers between devices: 831 us -> 174 us
  blocking collectives: 100 us -> 0 us
  other arithmetic: 70 us -> 162 us
  local copies, waits for them, and re-layouts: 74.1 us -> 123 us
  starting transfers between devices: 4.87 us -> 48.5 us
  between operations: 16.8 us -> 2.88 us
    reduce_scatter x5 -> x0, waiting for transfers between devices: 580 us -> none  [the longest x1 157 us: local(): lax.psum_scatter(grad_output, ('dp', 'expert'), scatter_dimension=1, tile...]
    ppermute x0 -> x43, waiting for transfers between devices: none -> 174 us  [the longest x24 161 us: dp_swap(): lax.ppermute(arr, 'dp', [(i, i ^ flip) for i in range(lax.axis_size('dp'))])]
    unnamed x14 -> x0, waiting for transfers between devices: 159 us -> none
    all_gather x2 -> x0, waiting for transfers between devices: 91.7 us -> none  [the longest x1 79.1 us: moe_dense(): wout_all = lax.all_gather(w_out, 'expert', axis=0, tiled=True)]
    unnamed x3 -> x0, blocking collectives: 68.1 us -> none
    ppermute x0 -> x43, starting transfers between devices: none -> 48.5 us  [the longest x24 28.9 us: dp_swap(): lax.ppermute(arr, 'dp', [(i, i ^ flip) for i in range(lax.axis_size('dp'))])]
    convert_element_type x3 -> x13, other arithmetic: 3.36 us -> 45.4 us  [the longest x1 11.5 us: local(): grad_input = (grad_input + jnp.einsum('tk,dk->td', dlogits, w_select, pre...]
    dot_general x8 -> x24, matrix products: 131 us -> 169 us  [the longest x4 39 us: moe_dense(): jnp.dot(dpre_ext, w_ext, preferred_element_type=jnp.float32)]
  transfers between devices with their start and end apart: 12 -> 43, of which waited for: 8 -> 15; matrix products, arithmetic and copies ran while one was open for 27% -> 69% of each run, Pallas kernels for 0% -> 0%
where the time goes in v2:
time: 809 us; the launch traced here: 795 us
  matrix products  284 us (35%)
  waiting for transfers between devices  174 us (22%)
  other arithmetic  162 us (20%)
  local copies, waits for them, and re-layouts  123 us (15%)
  starting transfers between devices  48.5 us (6%)
    ppermute x24, waiting for transfers between devices, dp_swap(): lax.ppermute(arr, 'dp', [(i, i ^ flip) for i in range(lax.axis_size('dp'))])  161 us
    dot_general x4, matrix products, moe_dense(): jnp.dot(dpre_ext, w_ext, preferred_element_type=jnp.float32)  39 us
    another operation x10, other arithmetic  36 us
    dot_general x4, matrix products, moe_dense(): jnp.einsum('td,fd->tf', cot_two, w_back, preferred_element_type=jnp.float32)  33.9 us
    dot_general x4, matrix products, moe_dense(): jnp.dot(gated_bf, w_back, preferred_element_type=jnp.float32)  32.9 us
    ppermute x24, starting transfers between devices, dp_swap(): lax.ppermute(arr, 'dp', [(i, i ^ flip) for i in range(lax.axis_size('dp'))])  28.9 us
    unnamed x245, local copies, waits for them, and re-layouts  28.8 us
    dot_general x4, matrix products, moe_dense(): jnp.einsum('td,fd->tf', sent_two, w_ext, preferred_element_type=jnp.float32)  25.5 us
  transfers between devices with their start and end apart: 43, of which 15 were waited for; matrix products, arithmetic and copies ran while one was open for 69% of the time, Pallas kernels for 0%

profile of v2, /device:TPU:0, one launch (start us, length us, event | category | flops | bytes accessed | tf_op | source)
XLA Modules:
  0.0 795.1 jit_solution(11485399461124240999)
XLA Ops:
  42.5 11.0 %fusion.191 = f32[1024,2560]{0,1:T(8,128)} fusion(bf16[1024,1024]{1,0:T(8,128)(2,1)S(1)} %copy-done.3, bf16[1024,2560]{1,0:T(8,128)(2,1)} %param.36), kind=kOutput, calls=%fused_computation.391 | convolution fusion | flops 5368709120 | bytes 17825792 | tf_op jit(solution)/shard_map/dot_general | solution.py:409
  63.5 7.8 multiply_reduce_fusion.3
  83.1 7.6 fusion.75
  105.1 9.9 %collective-permute-done.3 = bf16[400,1024]{1,0:T(8,128)(2,1)} collective-permute-done((bf16[400,1024]{1,0:T(8,128)(2,1)}, bf16[400,1024]{1,0:T(8,128)(2,1)}, u32[]{:S(2)}, u32[]{:S(2)}) %collective-permute-start.3) | collective-permute-done | bytes 819232 | tf_op jit(solution)/shard_map/ppermute | solution.py:237
  119.3 13.3 %collective-permute-done.7 = bf16[400,1024]{1,0:T(8,128)(2,1)} collective-permute-done((bf16[400,1024]{1,0:T(8,128)(2,1)}, bf16[400,1024]{1,0:T(8,128)(2,1)}, u32[]{:S(2)}, u32[]{:S(2)}) %collective-permute-start.7) | collective-permute-done | bytes 819232 | tf_op jit(solution)/shard_map/ppermute | solution.py:237
  145.4 25.6 %collective-permute-done.8 = bf16[400,1024]{1,0:T(8,128)(2,1)} collective-permute-done((bf16[400,1024]{1,0:T(8,128)(2,1)}, bf16[400,1024]{1,0:T(8,128)(2,1)}, u32[]{:S(2)}, u32[]{:S(2)}) %collective-permute-start.8) | collective-permute-done | bytes 819232 | tf_op jit(solution)/shard_map/ppermute | solution.py:237
  177.7 6.3 fusion.99
  187.4 7.0 convert_multiply_fusion.2
  198.6 7.9 fusion.20
  215.8 7.3 fusion.87
  223.1 5.9 convolution_convert_fusion.5
  240.2 6.4 fusion.96
  246.6 9.7 %convert_multiply_fusion.1 = (f32[2048,768]{0,1:T(8,128)}, f32[2048,768]{0,1:T(8,128)}) fusion(f32[2048,832]{0,1:T(8,128)S(1)} %fusion.96, bf16[2048,1024]{1,0:T(8,128)(2,1)S(1)} %copy-done.70, bf16[1600,1024]{1,0:T(8,128)(2,1)} %constant_dynamic-update-slice_fusion.4), kind=kOutput, calls=%fused_computation.35 | convolution fusion | flops 3238526976 | bytes 24641536 | tf_op jit(solution)/shard_map/td,fd->tf/dot_general | solution.py:334
  260.6 8.1 %fusion.27 = (bf16[2048,768]{0,1:T(8,128)(2,1)S(1)}, bf16[2048,768]{0,1:T(8,128)(2,1)S(1)}) fusion(f32[2048,768]{0,1:T(8,128)} %get-tuple-element.289, f32[2048,832]{0,1:T(8,128)} %copy-done.48, f32[2048,6]{0,1:T(8,128)S(1)} %get-tuple-element.186), kind=kLoop, calls=%fused_computation.70 | loop fusion | flops 40894464 | bytes 18923520 | tf_op jit(solution)/shard_map/convert.67
  272.2 5.9 convolution_convert_fusion.4
  286.5 6.2 fusion.119
  292.7 7.3 convert_multiply_fusion.3
  304.2 8.1 %fusion.13 = (bf16[2048,768]{0,1:T(8,128)(2,1)S(1)}, bf16[2048,768]{0,1:T(8,128)(2,1)S(1)}) fusion(f32[2048,768]{0,1:T(8,128)} %get-tuple-element.285, f32[2048,832]{0,1:T(8,128)} %copy-done.49, f32[2048,6]{0,1:T(8,128)S(1)} %get-tuple-element.190), kind=kLoop, calls=%fused_computation.56 | loop fusion | flops 40894464 | bytes 18923520 | tf_op jit(solution)/shard_map/convert.75
  321.5 5.9 convolution_convert_fusion.3
  335.4 9.8 %fusion.90 = f32[2048,1024]{1,0:T(8,128)} fusion(bf16[2048,6]{0,1:T(8,128)(2,1)S(1)} %copy-done.97, bf16[2048,768]{0,1:T(8,128)(2,1)} %copy-done.56, bf16[64,1024]{1,0:T(8,128)(2,1)} %copy-done.77, bf16[768,1024]{1,0:T(8,128)(2,1)S(1)} %bitcast.232), kind=kOutput, calls=%fused_computation.181 | convolution fusion | flops 3503292416 | bytes 13262848 | tf_op jit(solution)/shard_map/dot_general | solution.py:342
  348.4 17.7 %collective-permute-done.33 = bf16[400,1024]{1,0:T(8,128)(2,1)S(1)} collective-permute-done((bf16[400,1024]{1,0:T(8,128)(2,1)}, bf16[400,1024]{1,0:T(8,128)(2,1)S(1)}, u32[]{:S(2)}, u32[]{:S(2)}) %collective-permute-start.33) | collective-permute-done | bytes 819232 | tf_op jit(solution)/shard_map/ppermute | solution.py:237
  369.3 6.6 fusion.93
  375.9 9.9 %convert_multiply_fusion = (f32[2048,768]{0,1:T(8,128)}, f32[2048,768]{0,1:T(8,128)}) fusion(f32[2048,832]{0,1:T(8,128)S(1)} %fusion.93, bf16[2048,1024]{1,0:T(8,128)(2,1)S(1)} %copy-done.74, bf16[1600,1024]{1,0:T(8,128)(2,1)} %collective-permute-done.10), kind=kOutput, calls=%fused_computation.34 | convolution fusion | flops 3238526976 | bytes 24641536 | tf_op jit(solution)/shard_map/td,fd->tf/dot_general | solution.py:334
  389.9 7.9 fusion.34
  401.3 5.9 convolution_convert_fusion.2
  414.0 10.3 %fusion.82 = f32[2048,1024]{1,0:T(8,128)} fusion(bf16[2048,6]{0,1:T(8,128)(2,1)S(1)} %get-tuple-element.191, bf16[2048,768]{0,1:T(8,128)(2,1)} %copy-done.57, bf16[1600,1024]{1,0:T(8,128)(2,1)} %collective-permute-done.10), kind=kOutput, calls=%fused_computation.179 | convolution fusion | flops 3499884544 | bytes 13262848 | tf_op jit(solution)/shard_map/dot_general | solution.py:342
  424.3 11.7 %add_add_fusion = f32[2048,1024]{1,0:T(8,128)S(1)} fusion(f32[2048,1024]{1,0:T(8,128)} %fusion.82, f32[2048,1024]{1,0:T(8,128)} %fusion.90, f32[2048,1024]{1,0:T(8,128)} %fusion.87, bf16[2048,6]{0,1:T(8,128)(2,1)S(1)} %copy-done.85, bf16[2048,768]{0,1:T(8,128)(2,1)S(1)} %copy-done.25, bf16[1600,1024]{1,0:T(8,128)(2,1)} %constant_dynamic-update-slice_fusion.4), kind=kOutput, calls=%fused_computation.28 | convolution fusion | flops 3506176000 | bytes 38428672 | tf_op jit(solution)/shard_map/dot_general | solution.py:342
  440.2 8.6 %fusion.103 = f32[2048,1024]{1,0:T(8,128)} fusion(bf16[2048,768]{0,1:T(8,128)(2,1)S(1)} %copy-done.55, bf16[1600,1024]{1,0:T(8,128)(2,1)} %collective-permute-done.10), kind=kOutput, calls=%fused_computation.195 | convolution fusion | flops 3221225472 | bytes 13107200 | tf_op jit(solution)/shard_map/dot_general | solution.py:341
  448.7 12.9 %add_add_fusion.1 = f32[2048,1024]{1,0:T(8,128)} fusion(f32[2048,1024]{1,0:T(8,128)} %fusion.103, f32[2048,1024]{1,0:T(8,128)} %fusion.194, f32[2048,1024]{1,0:T(8,128)} %fusion.110, bf16[2048,768]{0,1:T(8,128)(2,1)S(1)} %copy-done.23, bf16[1600,1024]{1,0:T(8,128)(2,1)} %constant_dynamic-update-slice_fusion.4), kind=kOutput, calls=%fused_computation.29 | convolution fusion | flops 3227516928 | bytes 38273024 | tf_op jit(solution)/shard_map/dot_general | solution.py:341
  467.7 7.4 convolution_convert_fusion
  475.1 8.4 %fusion.195 = f32[1024,2560]{0,1:T(8,128)} fusion(bf16[1024,1024]{1,0:T(8,128)(2,1)S(1)} %fusion.114, bf16[2560,1024]{1,0:T(8,128)(2,1)S(1)} %bitcast.264), kind=kOutput, calls=%fused_computation.395 | convolution fusion | flops 5368709120 | bytes 17825792 | tf_op jit(solution)/shard_map/td,kd->tk/dot_general | solution.py:439
  483.5 7.3 multiply_reduce_fusion.2
  492.5 6.0 multiply_reduce_fusion.5
  498.6 7.7 multiply_reduce_fusion.4
  507.2 9.4 %multiply_convert_fusion.2 = (bf16[4,512,1024]{2,1,0:T(8,128)(2,1)}, bf16[4,512,1024]{2,1,0:T(8,128)(2,1)}) fusion(f32[4,512,1024]{2,1,0:T(8,128)} %get-tuple-element.291, f32[4,512,1024]{2,1,0:T(8,128)S(1)} %bitcast.215, f32[4,512]{1,0:T(4,128)S(1)} %get-tuple-element.290, f32[4,512]{1,0:T(4,128)S(1)} %copy-done.82, pred[512,1024]{1,0:T(8,128)(4,1)S(1)} %copy-done.13, ...), kind=kLoop, calls=%fused_computation.22 | loop fusion | flops 20971520 | bytes 43024384 | tf_op jit(solution)/shard_map/while/body/eval_jaxpr/convert_element_type | solution.py:128
  557.5 8.3 %multiply_convert_fusion = (bf16[1024,4,5,128]{0,3,2,1:T(8,128)(2,1)}, f32[1024,4,5]{0,2,1:T(8,128)S(1)}) fusion(f32[1024,4,128]{0,2,1:T(8,128)S(1)} %add_bitcast_fusion, f32[1024,4,5]{0,2,1:T(8,128)S(1)} %copy-done.64, f32[1024,4,5,128]{0,3,2,1:T(8,128)} %bitcast.219), kind=kLoop, calls=%fused_computation.2 | loop fusion | flops 10465280 | bytes 17989632 | tf_op jit(solution)/shard_map/convert_element_type | solution.py:475
  567.8 10.9 %fusion.197 = f32[1024,1024]{1,0:T(8,128)} fusion(bf16[1024,2560]{0,1:T(8,128)(2,1)} %bitcast.241, bf16[1024,2560]{1,0:T(8,128)(2,1)} %param.36), kind=kOutput, calls=%fused_computation.397 | convolution fusion | flops 5368709120 | bytes 14680064 | tf_op jit(solution)/shard_map/tk,dk->td/dot_general | solution.py:491
  581.2 9.9 %convolution_convert_fusion.1 = bf16[2560,1024]{0,1:T(8,128)(2,1)} fusion(bf16[1024,2560]{0,1:T(8,128)(2,1)} %bitcast.242, bf16[1024,1024]{1,0:T(8,128)(2,1)S(1)} %copy-done.5), kind=kOutput, calls=%fused_computation.95 | convolution fusion | flops 5371330560 | bytes 12582912 | tf_op jit(solution)/shard_map/td,tk->dk/dot_general | solution.py:478
  595.1 12.0 %concatenate.122 = bf16[16,2,32,3712]{3,2,1,0:T(8,128)(2,1)} concatenate(bf16[16,2,32,2560]{3,2,1,0:T(8,128)(2,1)} %bitcast.243, bf16[16,2,32,512]{3,2,1,0:T(8,128)(2,1)} %convolution_convert_fusion.11, bf16[16,2,32,512]{3,2,1,0:T(8,128)(2,1)} %convolution_convert_fusion.10, bf16[16,2,32,40]{3,2,1,0:T(8,128)(2,1)} %bitcast.255, bf16[16,2,32,1]{3,2,1,0:T(8,128)(2,1)S(1)} %concatenate.127, ...), dimensions={3} | concatenate | bytes 15204352 | tf_op jit(solution)/shard_map/concatenate | solution.py:499
  625.9 11.5 %add_convert_fusion.1 = (bf16[1024,1024]{1,0:T(8,128)(2,1)}, bf16[1024,1024]{1,0:T(8,128)(2,1)}) fusion(f32[1024,1024]{1,0:T(8,128)} %fusion.198, f32[1024,1024]{1,0:T(8,128)} %fusion.197, f32[1024]{0:T(1024)S(1)} %negate_multiply_fusion, bf16[1024,1024]{1,0:T(8,128)(2,1)} %copy-done.39, f32[2048,1024]{1,0:T(8,128)S(1)} %bitcast.217, ...), kind=kLoop, calls=%fused_computation.116 | loop fusion | flops 22020096 | bytes 37769216 | tf_op jit(solution)/shard_map/convert_element_type | solution.py:495
  637.4 6.4 collective-permute-done.37
  643.8 18.9 %collective-permute-done.38 = bf16[400,1024]{1,0:T(8,128)(2,1)} collective-permute-done((bf16[400,1024]{1,0:T(8,128)(2,1)}, bf16[400,1024]{1,0:T(8,128)(2,1)}, u32[]{:S(2)}, u32[]{:S(2)}) %collective-permute-start.38) | collective-permute-done | bytes 819232 | tf_op jit(solution)/shard_map/ppermute | solution.py:237
  675.0 12.8 %collective-permute-done.40 = bf16[400,1024]{1,0:T(8,128)(2,1)S(1)} collective-permute-done((bf16[400,1024]{1,0:T(8,128)(2,1)S(1)}, bf16[400,1024]{1,0:T(8,128)(2,1)S(1)}, u32[]{:S(2)}, u32[]{:S(2)}) %collective-permute-start.40) | collective-permute-done | bytes 819232 | tf_op jit(solution)/shard_map/ppermute | solution.py:237
  688.4 15.2 %collective-permute-done.41 = bf16[400,1024]{1,0:T(8,128)(2,1)S(1)} collective-permute-done((bf16[400,1024]{1,0:T(8,128)(2,1)S(1)}, bf16[400,1024]{1,0:T(8,128)(2,1)S(1)}, u32[]{:S(2)}, u32[]{:S(2)}) %collective-permute-start.41) | collective-permute-done | bytes 819232 | tf_op jit(solution)/shard_map/ppermute | solution.py:237
  738.3 15.7 %collective-permute-done.15 = bf16[128,3712]{1,0:T(8,128)(2,1)S(1)} collective-permute-done((bf16[128,3712]{1,0:T(8,128)(2,1)S(1)}, bf16[128,3712]{1,0:T(8,128)(2,1)S(1)}, u32[]{:S(2)}, u32[]{:S(2)}) %collective-permute-start.15) | collective-permute-done | bytes 950304 | tf_op jit(solution)/shard_map/ppermute | solution.py:237
  756.2 16.9 %collective-permute-done.16 = bf16[128,3712]{1,0:T(8,128)(2,1)S(1)} collective-permute-done((bf16[128,3712]{1,0:T(8,128)(2,1)S(1)}, bf16[128,3712]{1,0:T(8,128)(2,1)S(1)}, u32[]{:S(2)}, u32[]{:S(2)}) %collective-permute-start.16) | collective-permute-done | bytes 950304 | tf_op jit(solution)/shard_map/ppermute | solution.py:237
  778.4 6.0 collective-permute-done.18
  784.4 7.7 collective-permute-done.19
  (482 shorter events, 325.4 us)
Async XLA Ops:
  9.7 83.9 %collective-permute-start.2 = (bf16[400,1024]{1,0:T(8,128)(2,1)}, bf16[400,1024]{1,0:T(8,128)(2,1)}, u32[]{:S(2)}, u32[]{:S(2)}) collective-permute-start(bf16[400,1024]{1,0:T(8,128)(2,1)} %constant_dynamic-slice_fusion.21), channel_id=1, source_target_pairs={{0,4},{1,5},{2,6},{3,7},{4,0},{5,1},{6,2},{7,3},{8,12},{9,13},{10,... | collective-permute-start | bytes 2457608 | tf_op jit(solution)/shard_map/ppermute | solution.py:231
  13.7 83.5 %collective-permute-start.6 = (bf16[400,1024]{1,0:T(8,128)(2,1)}, bf16[400,1024]{1,0:T(8,128)(2,1)}, u32[]{:S(2)}, u32[]{:S(2)}) collective-permute-start(bf16[400,1024]{1,0:T(8,128)(2,1)} %constant_dynamic-slice_fusion.21), channel_id=1, source_target_pairs={{0,2},{1,3},{2,4},{3,5},{4,6},{5,7},{6,0},{7,1},{8,10},{9,11},{10,... | collective-permute-start | bytes 2457608 | tf_op jit(solution)/shard_map/ppermute | solution.py:231
  15.7 75.9 %copy-start.79 = (f32[1024]{0:T(1024)}, f32[1024]{0:T(1024)S(1)}, u32[]{:S(2)}) copy-start(f32[1024]{0:T(1024)S(1)} %broadcast_multiply_fusion) | copy-start | bytes 12292
  16.4 75.2 %copy-start.89 = (f32[1024]{0:T(1024)}, f32[1024]{0:T(1024)S(1)}, u32[]{:S(2)}) copy-start(f32[1024]{0:T(1024)S(1)} %fusion.151) | copy-start | bytes 12292
  90.7 87.0 %collective-permute-start = (bf16[1024,1024]{1,0:T(8,128)(2,1)}, bf16[1024,1024]{1,0:T(8,128)(2,1)}, u32[]{:S(2)}, u32[]{:S(2)}) collective-permute-start(bf16[1024,1024]{1,0:T(8,128)(2,1)} %get-tuple-element.280), channel_id=1, source_target_pairs={{0,1},{1,0},{2,3},{3,2},{4,5},{5,4},{6,7},{7,6},{8,9},{9,8},{10,11... | collective-permute-start | bytes 6291464 | tf_op jit(solution)/shard_map/ppermute | solution.py:225
  91.1 13.0 %collective-permute-start.1 = (bf16[1024,48]{0,1:T(8,128)(2,1)S(1)}, bf16[1024,48]{0,1:T(8,128)(2,1)S(1)}, u32[]{:S(2)}, u32[]{:S(2)}) collective-permute-start(bf16[1024,48]{0,1:T(8,128)(2,1)S(1)} %fusion.78), channel_id=1, source_target_pairs={{0,1},{1,0},{2,3},{3,2},{4,5},{5,4},{6,7},{7,6},{8,9},{9,8},{10,11... | collective-permute-start | bytes 294920 | tf_op jit(solution)/shard_map/ppermute | solution.py:225
  93.6 21.4 %collective-permute-start.3 = (bf16[400,1024]{1,0:T(8,128)(2,1)}, bf16[400,1024]{1,0:T(8,128)(2,1)}, u32[]{:S(2)}, u32[]{:S(2)}) collective-permute-start(bf16[400,1024]{1,0:T(8,128)(2,1)} %collective-permute-done.2), channel_id=1, source_target_pairs={{0,8},{8,0},{16,24},{24,16},{1,9},{9,1},{17,25},{25,17},{2,10},{10... | collective-permute-start | bytes 2457608 | tf_op jit(solution)/shard_map/ppermute | solution.py:237
  95.1 22.4 %collective-permute-start.4 = (bf16[400,1024]{1,0:T(8,128)(2,1)}, bf16[400,1024]{1,0:T(8,128)(2,1)}, u32[]{:S(2)}, u32[]{:S(2)}) collective-permute-start(bf16[400,1024]{1,0:T(8,128)(2,1)} %collective-permute-done.2), channel_id=1, source_target_pairs={{0,16},{8,24},{16,0},{24,8},{1,17},{9,25},{17,1},{25,9},{2,18},{10... | collective-permute-start | bytes 2457608 | tf_op jit(solution)/shard_map/ppermute | solution.py:237
  97.2 35.4 %collective-permute-start.7 = (bf16[400,1024]{1,0:T(8,128)(2,1)}, bf16[400,1024]{1,0:T(8,128)(2,1)}, u32[]{:S(2)}, u32[]{:S(2)}) collective-permute-start(bf16[400,1024]{1,0:T(8,128)(2,1)} %collective-permute-done.6), channel_id=1, source_target_pairs={{0,8},{8,0},{16,24},{24,16},{1,9},{9,1},{17,25},{25,17},{2,10},{10... | collective-permute-start | bytes 2457608 | tf_op jit(solution)/shard_map/ppermute | solution.py:237
  104.1 79.9 %collective-permute-start.12 = (bf16[1024,1024]{1,0:T(8,128)(2,1)S(1)}, bf16[1024,1024]{1,0:T(8,128)(2,1)}, u32[]{:S(2)}, u32[]{:S(2)}) collective-permute-start(bf16[1024,1024]{1,0:T(8,128)(2,1)S(1)} %copy-done.14), channel_id=1, source_target_pairs={{0,1},{1,0},{2,3},{3,2},{4,5},{5,4},{6,7},{7,6},{8,9},{9,8},{10,11... | collective-permute-start | bytes 6291464 | tf_op jit(solution)/shard_map/ppermute | solution.py:225
  115.1 60.4 %collective-permute-start.5 = (bf16[400,1024]{1,0:T(8,128)(2,1)}, bf16[400,1024]{1,0:T(8,128)(2,1)}, u32[]{:S(2)}, u32[]{:S(2)}) collective-permute-start(bf16[400,1024]{1,0:T(8,128)(2,1)} %collective-permute-done.2), channel_id=1, source_target_pairs={{0,24},{8,16},{16,8},{24,0},{1,25},{9,17},{17,9},{25,1},{2,26},{10... | collective-permute-start | bytes 2457608 | tf_op jit(solution)/shard_map/ppermute | solution.py:237
  117.5 53.6 %collective-permute-start.8 = (bf16[400,1024]{1,0:T(8,128)(2,1)}, bf16[400,1024]{1,0:T(8,128)(2,1)}, u32[]{:S(2)}, u32[]{:S(2)}) collective-permute-start(bf16[400,1024]{1,0:T(8,128)(2,1)} %collective-permute-done.6), channel_id=1, source_target_pairs={{0,16},{8,24},{16,0},{24,8},{1,17},{9,25},{17,1},{25,9},{2,18},{10... | collective-permute-start | bytes 2457608 | tf_op jit(solution)/shard_map/ppermute | solution.py:237
  132.6 44.0 %collective-permute-start.9 = (bf16[400,1024]{1,0:T(8,128)(2,1)}, bf16[400,1024]{1,0:T(8,128)(2,1)S(1)}, u32[]{:S(2)}, u32[]{:S(2)}) collective-permute-start(bf16[400,1024]{1,0:T(8,128)(2,1)} %collective-permute-done.6), channel_id=1, source_target_pairs={{0,24},{8,16},{16,8},{24,0},{1,25},{9,17},{17,9},{25,1},{2,26},{10... | collective-permute-start | bytes 2457608 | tf_op jit(solution)/shard_map/ppermute | solution.py:237
  171.0 198.2 %collective-permute-start.10 = (bf16[1600,1024]{1,0:T(8,128)(2,1)}, bf16[1600,1024]{1,0:T(8,128)(2,1)}, u32[]{:S(2)}, u32[]{:S(2)}) collective-permute-start(bf16[1600,1024]{1,0:T(8,128)(2,1)} %pad_maximum_fusion.1), channel_id=1, source_target_pairs={{0,6},{1,7},{2,0},{3,1},{4,2},{5,3},{6,4},{7,5},{8,14},{9,15},{10,... | collective-permute-start | bytes 9830408 | tf_op jit(solution)/shard_map/ppermute | solution.py:231
  236.7 95.7 %collective-permute-start.28 = (bf16[400,1024]{1,0:T(8,128)(2,1)}, bf16[400,1024]{1,0:T(8,128)(2,1)S(1)}, u32[]{:S(2)}, u32[]{:S(2)}) collective-permute-start(bf16[400,1024]{1,0:T(8,128)(2,1)} %get-tuple-element.210), channel_id=1, source_target_pairs={{0,8},{8,0},{16,24},{24,16},{1,9},{9,1},{17,25},{25,17},{2,10},{10... | collective-permute-start | bytes 2457608 | tf_op jit(solution)/shard_map/ppermute | solution.py:237
  237.2 96.3 %collective-permute-start.29 = (bf16[400,1024]{1,0:T(8,128)(2,1)}, bf16[400,1024]{1,0:T(8,128)(2,1)}, u32[]{:S(2)}, u32[]{:S(2)}) collective-permute-start(bf16[400,1024]{1,0:T(8,128)(2,1)} %get-tuple-element.212), channel_id=1, source_target_pairs={{0,16},{8,24},{16,0},{24,8},{1,17},{9,25},{17,1},{25,9},{2,18},{10... | collective-permute-start | bytes 2457608 | tf_op jit(solution)/shard_map/ppermute | solution.py:237
  237.7 107.4 %collective-permute-start.30 = (bf16[400,1024]{1,0:T(8,128)(2,1)}, bf16[400,1024]{1,0:T(8,128)(2,1)}, u32[]{:S(2)}, u32[]{:S(2)}) collective-permute-start(bf16[400,1024]{1,0:T(8,128)(2,1)} %get-tuple-element.211), channel_id=1, source_target_pairs={{0,24},{8,16},{16,8},{24,0},{1,25},{9,17},{17,9},{25,1},{2,26},{10... | collective-permute-start | bytes 2457608 | tf_op jit(solution)/shard_map/ppermute | solution.py:237
  286.0 62.3 %collective-permute-start.32 = (bf16[400,1024]{1,0:T(8,128)(2,1)}, bf16[400,1024]{1,0:T(8,128)(2,1)}, u32[]{:S(2)}, u32[]{:S(2)}) collective-permute-start(bf16[400,1024]{1,0:T(8,128)(2,1)} %get-tuple-element.213), channel_id=1, source_target_pairs={{0,8},{8,0},{16,24},{24,16},{1,9},{9,1},{17,25},{25,17},{2,10},{10... | collective-permute-start | bytes 2457608 | tf_op jit(solution)/shard_map/ppermute | solution.py:237
  332.4 33.6 %collective-permute-start.33 = (bf16[400,1024]{1,0:T(8,128)(2,1)}, bf16[400,1024]{1,0:T(8,128)(2,1)S(1)}, u32[]{:S(2)}, u32[]{:S(2)}) collective-permute-start(bf16[400,1024]{1,0:T(8,128)(2,1)} %get-tuple-element.215), channel_id=1, source_target_pairs={{0,16},{8,24},{16,0},{24,8},{1,17},{9,25},{17,1},{25,9},{2,18},{10... | collective-permute-start | bytes 2457608 | tf_op jit(solution)/shard_map/ppermute | solution.py:237
  333.4 32.6 %collective-permute-start.34 = (bf16[400,1024]{1,0:T(8,128)(2,1)}, bf16[400,1024]{1,0:T(8,128)(2,1)S(1)}, u32[]{:S(2)}, u32[]{:S(2)}) collective-permute-start(bf16[400,1024]{1,0:T(8,128)(2,1)} %get-tuple-element.214), channel_id=1, source_target_pairs={{0,24},{8,16},{16,8},{24,0},{1,25},{9,17},{17,9},{25,1},{2,26},{10... | collective-permute-start | bytes 2457608 | tf_op jit(solution)/shard_map/ppermute | solution.py:237
  348.4 274.0 %collective-permute-start.31 = (bf16[400,1024]{1,0:T(8,128)(2,1)}, bf16[400,1024]{1,0:T(8,128)(2,1)}, u32[]{:S(2)}, u32[]{:S(2)}) collective-permute-start(bf16[400,1024]{1,0:T(8,128)(2,1)} %add_convert_fusion.6), channel_id=1, source_target_pairs={{0,4},{1,5},{2,6},{3,7},{4,0},{5,1},{6,2},{7,3},{8,12},{9,13},{10,... | collective-permute-start | bytes 2457608 | tf_op jit(solution)/shard_map/ppermute | solution.py:231
  369.0 255.2 %collective-permute-start.35 = (bf16[400,1024]{1,0:T(8,128)(2,1)}, bf16[400,1024]{1,0:T(8,128)(2,1)}, u32[]{:S(2)}, u32[]{:S(2)}) collective-permute-start(bf16[400,1024]{1,0:T(8,128)(2,1)} %add_convert_fusion.5), channel_id=1, source_target_pairs={{0,6},{1,7},{2,0},{3,1},{4,2},{5,3},{6,4},{7,5},{8,14},{9,15},{10,... | collective-permute-start | bytes 2457608 | tf_op jit(solution)/shard_map/ppermute | solution.py:231
  412.0 203.2 %collective-permute-start.36 = (bf16[1600,1024]{1,0:T(8,128)(2,1)}, bf16[1600,1024]{1,0:T(8,128)(2,1)}, u32[]{:S(2)}, u32[]{:S(2)}) collective-permute-start(bf16[1600,1024]{1,0:T(8,128)(2,1)} %scatter.24), channel_id=1, source_target_pairs={{0,2},{1,3},{2,4},{3,5},{4,6},{5,7},{6,0},{7,1},{8,10},{9,11},{10,... | collective-permute-start | bytes 9830408 | tf_op jit(solution)/shard_map/ppermute | solution.py:231
  436.0 29.7 %copy-start.6 = (f32[2048,1024]{1,0:T(8,128)}, f32[2048,1024]{1,0:T(8,128)S(1)}, u32[]{:S(2)}) copy-start(f32[2048,1024]{1,0:T(8,128)S(1)} %add_add_fusion) | copy-start | bytes 25165828
  437.6 28.0 %collective-permute-start.13 = (bf16[1024,1024]{1,0:T(8,128)(2,1)}, bf16[1024,1024]{1,0:T(8,128)(2,1)S(1)}, u32[]{:S(2)}, u32[]{:S(2)}) collective-permute-start(bf16[1024,1024]{1,0:T(8,128)(2,1)} %slice.550), channel_id=1, source_target_pairs={{0,1},{1,0},{2,3},{3,2},{4,5},{5,4},{6,7},{7,6},{8,9},{9,8},{10,11... | collective-permute-start | bytes 6291464 | tf_op jit(solution)/shard_map/ppermute | solution.py:225
  465.7 159.0 %collective-permute-start.11 = (bf16[1024,1024]{1,0:T(8,128)(2,1)}, bf16[1024,1024]{1,0:T(8,128)(2,1)}, u32[]{:S(2)}, u32[]{:S(2)}) collective-permute-start(bf16[1024,1024]{1,0:T(8,128)(2,1)} %slice.551), channel_id=1, source_target_pairs={{0,1},{1,0},{2,3},{3,2},{4,5},{5,4},{6,7},{7,6},{8,9},{9,8},{10,11... | collective-permute-start | bytes 6291464 | tf_op jit(solution)/shard_map/ppermute | solution.py:225
  492.5 30.3 %copy-start.29 = (bf16[1024,4,128]{2,0,1:T(8,128)(2,1)}, bf16[1024,4,128]{2,0,1:T(8,128)(2,1)S(1)}, u32[]{:S(2)}) copy-start(bf16[1024,4,128]{2,0,1:T(8,128)(2,1)S(1)} %copy.165) | copy-start | bytes 3145732
  528.2 142.0 %collective-permute-start.21 = (bf16[16,32,2560]{2,1,0:T(8,128)(2,1)}, bf16[16,32,2560]{2,1,0:T(8,128)(2,1)}, u32[]{:S(2)}, u32[]{:S(2)}) collective-permute-start(bf16[16,32,2560]{2,1,0:T(8,128)(2,1)} %dynamic-slice_bitcast_fusion.1), channel_id=1, source_target_pairs={{0,1},{1,0},{2,3},{3,2},{4,5},{5,4},{6,7},{7,6},{8,9},{9,8},{10,11... | collective-permute-start | bytes 7864328 | tf_op jit(solution)/shard_map/ppermute | solution.py:225
  615.2 102.5 %collective-permute-start.14 = (bf16[16,32,3712]{2,1,0:T(8,128)(2,1)}, bf16[16,32,3712]{2,1,0:T(8,128)(2,1)}, u32[]{:S(2)}, u32[]{:S(2)}) collective-permute-start(bf16[16,32,3712]{2,1,0:T(8,128)(2,1)} %dynamic-slice_bitcast_fusion), channel_id=1, source_target_pairs={{0,1},{1,0},{2,3},{3,2},{4,5},{5,4},{6,7},{7,6},{8,9},{9,8},{10,11... | collective-permute-start | bytes 11403272 | tf_op jit(solution)/shard_map/ppermute | solution.py:225
  622.3 21.4 %collective-permute-start.37 = (bf16[400,1024]{1,0:T(8,128)(2,1)}, bf16[400,1024]{1,0:T(8,128)(2,1)}, u32[]{:S(2)}, u32[]{:S(2)}) collective-permute-start(bf16[400,1024]{1,0:T(8,128)(2,1)} %get-tuple-element.216), channel_id=1, source_target_pairs={{0,8},{8,0},{16,24},{24,16},{1,9},{9,1},{17,25},{25,17},{2,10},{10... | collective-permute-start | bytes 2457608 | tf_op jit(solution)/shard_map/ppermute | solution.py:237
  624.2 38.5 %collective-permute-start.38 = (bf16[400,1024]{1,0:T(8,128)(2,1)}, bf16[400,1024]{1,0:T(8,128)(2,1)}, u32[]{:S(2)}, u32[]{:S(2)}) collective-permute-start(bf16[400,1024]{1,0:T(8,128)(2,1)} %get-tuple-element.218), channel_id=1, source_target_pairs={{0,16},{8,24},{16,0},{24,8},{1,17},{9,25},{17,1},{25,9},{2,18},{10... | collective-permute-start | bytes 2457608 | tf_op jit(solution)/shard_map/ppermute | solution.py:237
  624.7 38.1 %collective-permute-start.39 = (bf16[400,1024]{1,0:T(8,128)(2,1)}, bf16[400,1024]{1,0:T(8,128)(2,1)}, u32[]{:S(2)}, u32[]{:S(2)}) collective-permute-start(bf16[400,1024]{1,0:T(8,128)(2,1)} %get-tuple-element.217), channel_id=1, source_target_pairs={{0,24},{8,16},{16,8},{24,0},{1,25},{9,17},{17,9},{25,1},{2,26},{10... | collective-permute-start | bytes 2457608 | tf_op jit(solution)/shard_map/ppermute | solution.py:237
  666.6 21.2 %collective-permute-start.40 = (bf16[400,1024]{1,0:T(8,128)(2,1)S(1)}, bf16[400,1024]{1,0:T(8,128)(2,1)S(1)}, u32[]{:S(2)}, u32[]{:S(2)}) collective-permute-start(bf16[400,1024]{1,0:T(8,128)(2,1)S(1)} %get-tuple-element.176), channel_id=1, source_target_pairs={{0,8},{8,0},{16,24},{24,16},{1,9},{9,1},{17,25},{25,17},{2,10},{10... | collective-permute-start | bytes 2457608 | tf_op jit(solution)/shard_map/ppermute | solution.py:237
  667.0 36.5 %collective-permute-start.41 = (bf16[400,1024]{1,0:T(8,128)(2,1)S(1)}, bf16[400,1024]{1,0:T(8,128)(2,1)S(1)}, u32[]{:S(2)}, u32[]{:S(2)}) collective-permute-start(bf16[400,1024]{1,0:T(8,128)(2,1)S(1)} %get-tuple-element.176), channel_id=1, source_target_pairs={{0,16},{8,24},{16,0},{24,8},{1,17},{9,25},{17,1},{25,9},{2,18},{10... | collective-permute-start | bytes 2457608 | tf_op jit(solution)/shard_map/ppermute | solution.py:237
  668.4 36.9 %collective-permute-start.42 = (bf16[400,1024]{1,0:T(8,128)(2,1)S(1)}, bf16[400,1024]{1,0:T(8,128)(2,1)S(1)}, u32[]{:S(2)}, u32[]{:S(2)}) collective-permute-start(bf16[400,1024]{1,0:T(8,128)(2,1)S(1)} %get-tuple-element.176), channel_id=1, source_target_pairs={{0,24},{8,16},{16,8},{24,0},{1,25},{9,17},{17,9},{25,1},{2,26},{10... | collective-permute-start | bytes 2457608 | tf_op jit(solution)/shard_map/ppermute | solution.py:237
  673.5 32.0 %copy-start.26 = (bf16[16,32,2560]{2,1,0:T(8,128)(2,1)}, bf16[16,32,2560]{2,1,0:T(8,128)(2,1)S(1)}, u32[]{:S(2)}) copy-start(bf16[16,32,2560]{2,1,0:T(8,128)(2,1)S(1)} %fusion.45) | copy-start | bytes 7864324
  674.7 50.0 %collective-permute-start.22 = (bf16[128,2560]{1,0:T(8,128)(2,1)}, bf16[128,2560]{1,0:T(8,128)(2,1)S(1)}, u32[]{:S(2)}, u32[]{:S(2)}) collective-permute-start(bf16[128,2560]{1,0:T(8,128)(2,1)} %get-tuple-element.223), channel_id=1, source_target_pairs={{0,8},{8,0},{16,24},{24,16},{1,9},{9,1},{17,25},{25,17},{2,10},{10... | collective-permute-start | bytes 1966088 | tf_op jit(solution)/shard_map/ppermute | solution.py:237
  687.8 43.9 %collective-permute-start.23 = (bf16[128,2560]{1,0:T(8,128)(2,1)S(1)}, bf16[128,2560]{1,0:T(8,128)(2,1)}, u32[]{:S(2)}, u32[]{:S(2)}) collective-permute-start(bf16[128,2560]{1,0:T(8,128)(2,1)S(1)} %get-tuple-element.225), channel_id=1, source_target_pairs={{0,16},{8,24},{16,0},{24,8},{1,17},{9,25},{17,1},{25,9},{2,18},{10... | collective-permute-start | bytes 1966088 | tf_op jit(solution)/shard_map/ppermute | solution.py:237
  703.5 30.0 %collective-permute-start.24 = (bf16[128,2560]{1,0:T(8,128)(2,1)S(1)}, bf16[128,2560]{1,0:T(8,128)(2,1)}, u32[]{:S(2)}, u32[]{:S(2)}) collective-permute-start(bf16[128,2560]{1,0:T(8,128)(2,1)S(1)} %get-tuple-element.224), channel_id=1, source_target_pairs={{0,24},{8,16},{16,8},{24,0},{1,25},{9,17},{17,9},{25,1},{2,26},{10... | collective-permute-start | bytes 1966088 | tf_op jit(solution)/shard_map/ppermute | solution.py:237
  722.0 31.9 %collective-permute-start.15 = (bf16[128,3712]{1,0:T(8,128)(2,1)S(1)}, bf16[128,3712]{1,0:T(8,128)(2,1)S(1)}, u32[]{:S(2)}, u32[]{:S(2)}) collective-permute-start(bf16[128,3712]{1,0:T(8,128)(2,1)S(1)} %get-tuple-element.205), channel_id=1, source_target_pairs={{0,8},{8,0},{16,24},{24,16},{1,9},{9,1},{17,25},{25,17},{2,10},{10... | collective-permute-start | bytes 2850824 | tf_op jit(solution)/shard_map/ppermute | solution.py:237
  724.2 48.9 %collective-permute-start.16 = (bf16[128,3712]{1,0:T(8,128)(2,1)S(1)}, bf16[128,3712]{1,0:T(8,128)(2,1)S(1)}, u32[]{:S(2)}, u32[]{:S(2)}) collective-permute-start(bf16[128,3712]{1,0:T(8,128)(2,1)S(1)} %get-tuple-element.207), channel_id=1, source_target_pairs={{0,16},{8,24},{16,0},{24,8},{1,17},{9,25},{17,1},{25,9},{2,18},{10... | collective-permute-start | bytes 2850824 | tf_op jit(solution)/shard_map/ppermute | solution.py:237
  724.6 48.5 %collective-permute-start.17 = (bf16[128,3712]{1,0:T(8,128)(2,1)S(1)}, bf16[128,3712]{1,0:T(8,128)(2,1)S(1)}, u32[]{:S(2)}, u32[]{:S(2)}) collective-permute-start(bf16[128,3712]{1,0:T(8,128)(2,1)S(1)} %get-tuple-element.206), channel_id=1, source_target_pairs={{0,24},{8,16},{16,8},{24,0},{1,25},{9,17},{17,9},{25,1},{2,26},{10... | collective-permute-start | bytes 2850824 | tf_op jit(solution)/shard_map/ppermute | solution.py:237
  735.4 41.1 %collective-permute-start.25 = (bf16[32,2560]{1,0:T(8,128)(2,1)S(1)}, bf16[32,2560]{1,0:T(8,128)(2,1)S(1)}, u32[]{:S(2)}, u32[]{:S(2)}) collective-permute-start(bf16[32,2560]{1,0:T(8,128)(2,1)S(1)} %get-tuple-element.241), channel_id=1, source_target_pairs={{0,2},{1,3},{2,4},{3,5},{4,6},{5,7},{6,0},{7,1},{8,10},{9,11},{10,... | collective-permute-start | bytes 491528 | tf_op jit(solution)/shard_map/ppermute | solution.py:231
  735.7 41.9 %collective-permute-start.26 = (bf16[32,2560]{1,0:T(8,128)(2,1)S(1)}, bf16[32,2560]{1,0:T(8,128)(2,1)S(1)}, u32[]{:S(2)}, u32[]{:S(2)}) collective-permute-start(bf16[32,2560]{1,0:T(8,128)(2,1)S(1)} %get-tuple-element.243), channel_id=1, source_target_pairs={{0,4},{1,5},{2,6},{3,7},{4,0},{5,1},{6,2},{7,3},{8,12},{9,13},{10,... | collective-permute-start | bytes 491528 | tf_op jit(solution)/shard_map/ppermute | solution.py:231
  753.9 23.6 %collective-permute-start.27 = (bf16[32,2560]{1,0:T(8,128)(2,1)S(1)}, bf16[32,2560]{1,0:T(8,128)(2,1)S(1)}, u32[]{:S(2)}, u32[]{:S(2)}) collective-permute-start(bf16[32,2560]{1,0:T(8,128)(2,1)S(1)} %get-tuple-element.242), channel_id=1, source_target_pairs={{0,6},{1,7},{2,0},{3,1},{4,2},{5,3},{6,4},{7,5},{8,14},{9,15},{10,... | collective-permute-start | bytes 491528 | tf_op jit(solution)/shard_map/ppermute | solution.py:231
  773.7 10.7 %collective-permute-start.18 = (bf16[32,3712]{1,0:T(8,128)(2,1)S(1)}, bf16[32,3712]{1,0:T(8,128)(2,1)S(1)}, u32[]{:S(2)}, u32[]{:S(2)}) collective-permute-start(bf16[32,3712]{1,0:T(8,128)(2,1)S(1)} %get-tuple-element.238), channel_id=1, source_target_pairs={{0,2},{1,3},{2,4},{3,5},{4,6},{5,7},{6,0},{7,1},{8,10},{9,11},{10,... | collective-permute-start | bytes 712712 | tf_op jit(solution)/shard_map/ppermute | solution.py:231
  774.0 18.1 %collective-permute-start.19 = (bf16[32,3712]{1,0:T(8,128)(2,1)S(1)}, bf16[32,3712]{1,0:T(8,128)(2,1)S(1)}, u32[]{:S(2)}, u32[]{:S(2)}) collective-permute-start(bf16[32,3712]{1,0:T(8,128)(2,1)S(1)} %get-tuple-element.240), channel_id=1, source_target_pairs={{0,4},{1,5},{2,6},{3,7},{4,0},{5,1},{6,2},{7,3},{8,12},{9,13},{10,... | collective-permute-start | bytes 712712 | tf_op jit(solution)/shard_map/ppermute | solution.py:231
  776.5 15.5 %collective-permute-start.20 = (bf16[32,3712]{1,0:T(8,128)(2,1)S(1)}, bf16[32,3712]{1,0:T(8,128)(2,1)S(1)}, u32[]{:S(2)}, u32[]{:S(2)}) collective-permute-start(bf16[32,3712]{1,0:T(8,128)(2,1)S(1)} %get-tuple-element.239), channel_id=1, source_target_pairs={{0,6},{1,7},{2,0},{3,1},{4,2},{5,3},{6,4},{7,5},{8,14},{9,15},{10,... | collective-permute-start | bytes 712712 | tf_op jit(solution)/shard_map/ppermute | solution.py:231
  (114 other events, 791.6 us)

commit v3 on v0

--- a/solution.py
+++ b/solution.py
@@ -1,6 +1,10 @@
+import functools
+
 import jax
 import jax.numpy as jnp
 from jax import lax
+from jax.experimental import pallas as pl
+from jax.experimental.pallas import tpu as pltpu
 from jax.sharding import PartitionSpec as P
 
 DH = 128
@@ -11,6 +15,14 @@
 ROPE_BASE = 10000.0
 MASK_FILL = -1e30
 HIGHEST = lax.Precision.HIGHEST
+ROUTER_ROWS = 64
+DIGITS = 5
+LANE = 128
+GAIN_ROWS = 16
+TILE = 256
+VMEM_BYTES = 60 << 20
+GELU_A = 0.7978845608028654
+GELU_B = 0.044715
 
 
 def layer_norm(values, gain_vec):
@@ -138,7 +150,1024 @@
     return (jnp.concatenate(grad_q_list, axis=0), grad_k, grad_v)
 
 
-def local(
+def dot_nt(left, right):
+    return lax.dot_general(left, right, (((1,), (1,)), ((), ())), preferred_element_type=jnp.float32)
+
+
+def dot_nn(left, right):
+    return lax.dot_general(left, right, (((1,), (0,)), ((), ())), preferred_element_type=jnp.float32)
+
+
+def dot_tn(left, right):
+    return lax.dot_general(left, right, (((0,), (0,)), ((), ())), preferred_element_type=jnp.float32)
+
+
+def spin(values, cos_two, sin_two):
+    return values * cos_two + pltpu.roll(values, DH // 2, 1) * sin_two
+
+
+def spin_back(values, cos_two, sin_two):
+    return values * cos_two - pltpu.roll(values, DH // 2, 1) * sin_two
+
+
+def window_mask(step, tile, start_col, keep_before, keep_now):
+    row = step * tile + lax.broadcasted_iota(jnp.int32, (tile, 2 * tile), 0)
+    col = (step - 1) * tile + lax.broadcasted_iota(jnp.int32, (tile, 2 * tile), 1)
+    keep_row = jnp.concatenate([keep_before, keep_now], axis=1)
+    return (col >= start_col) & (col <= row) & ((keep_row == 1) | (col == row))
+
+
+def neighbour(kind, amount):
+    mine, place = lax.axis_index("dp"), lax.axis_index("expert")
+    chips = lax.axis_size("expert") // 2
+    chip, core = place // 2, lax.rem(place, 2)
+    if kind == "dp":
+        flipped = [mine, mine + 1 - 2 * lax.rem(mine, 2), lax.rem(mine + 2, 4), 3 - mine]
+        return (flipped[amount], place)
+    if kind == "core":
+        return (mine, place + 1 - 2 * core)
+    return (mine, 2 * lax.rem(chip + amount + chips, chips) + core)
+
+
+def own_part(rows):
+    return lambda mine, flipped: mine * rows
+
+
+def far_part(rows):
+    return lambda mine, flipped: flipped * rows
+
+
+def fixed(start):
+    return lambda mine, flipped: start
+
+
+def shift_move(src, dst, hop, src_at, dst_at, count):
+    return [(src, dst, "chip", hop, src_at, dst_at, count)]
+
+
+def gather_moves(buf_in, buf_out, rows):
+    return [(buf_in, buf_out, "dp", flip, own_part(rows), own_part(rows), rows) for flip in (1, 2, 3)]
+
+
+def scatter_moves(src, dst, rows):
+    return [
+        (src, dst, "dp", flip, far_part(rows), fixed((flip - 1) * rows), rows) for flip in (1, 2, 3)
+    ]
+
+
+def greet(peers):
+    barrier = pltpu.get_barrier_semaphore()
+    for peer in peers:
+        pl.semaphore_signal(barrier, inc=1, device_id=peer, device_id_type=pl.DeviceIdType.MESH)
+    pl.semaphore_wait(barrier, len(peers))
+
+
+def peers_of(moves):
+    peers = []
+    for _, _, kind, amount, _, _, _ in moves:
+        peers.append(neighbour(kind, amount))
+        if kind == "chip":
+            peers.append(neighbour(kind, -amount))
+    return peers
+
+
+def copies_of(moves, ins, outs, send_sem, recv_sem):
+    mine = lax.axis_index("dp")
+    copies = []
+    for i, (src, dst, kind, amount, src_at, dst_at, count) in enumerate(moves):
+        peer = neighbour(kind, amount)
+        copies.append(
+            pltpu.make_async_remote_copy(
+                src_ref=ins[src].at[pl.ds(pl.multiple_of(src_at(mine, peer[0]), 16), count)],
+                dst_ref=outs[dst].at[pl.ds(pl.multiple_of(dst_at(mine, peer[0]), 16), count)],
+                send_sem=send_sem.at[i],
+                recv_sem=recv_sem.at[i],
+                device_id=peer,
+                device_id_type=pl.DeviceIdType.MESH,
+            )
+        )
+    return copies
+
+
+ANYWHERE = pl.BlockSpec(memory_space=pl.ANY)
+
+
+def tile_rows(index, tile):
+    return pl.ds(pl.multiple_of(index * tile, tile), tile)
+
+
+def forward_body(heads, tile, steps, *refs):
+    (
+        own_any,
+        cot_any,
+        x_ref,
+        start_ref,
+        keep_ref,
+        cos_ref,
+        sin_ref,
+        mask_ref,
+        gain_ref,
+        wqk_ref,
+        wsel_ref,
+        wval_ref,
+        wout_ref,
+        chunk_any,
+        cot_far_any,
+        sent_far_any,
+        hid_ref,
+        norm_ref,
+        q_ref,
+        k_ref,
+        v_ref,
+        val_ref,
+        att_ref,
+        sig_ref,
+        lse_ref,
+        mix_ref,
+        sent_all,
+        send_sem,
+        recv_sem,
+        tile_send,
+        tile_recv,
+    ) = refs
+    step = pl.program_id(0)
+    rows = steps * tile
+    quarter = own_any.shape[0] // 4
+    moves = shift_move(0, 0, -2, own_part(quarter), own_part(quarter), quarter)
+    moves = moves + [(1, 1, "core", 1, fixed(0), fixed(0), rows)]
+    partner = neighbour("core", 1)
+    copies = copies_of(moves, [own_any, cot_any], [chunk_any, cot_far_any], send_sem, recv_sem)
+
+    def tile_copy(index):
+        return pltpu.make_async_remote_copy(
+            src_ref=sent_all.at[pl.ds(index * tile, tile)],
+            dst_ref=sent_far_any.at[pl.ds(index * tile, tile)],
+            send_sem=tile_send.at[index],
+            recv_sem=tile_recv.at[index],
+            device_id=partner,
+            device_id_type=pl.DeviceIdType.MESH,
+        )
+
+
+    @pl.when(step == 0)
+    def _():
+        greet(peers_of(moves))
+        for copy in copies:
+            copy.start()
+
+    now = tile_rows(step, tile)
+    before = tile_rows(jnp.maximum(step - 1, 0), tile)
+    x = x_ref[...]
+    x_f = x.astype(jnp.float32)
+    center = x_f - jnp.mean(x_f, axis=1, keepdims=True)
+    spread = jnp.mean(center * center, axis=1, keepdims=True)
+    normed = (center * lax.rsqrt(spread + NORM_EPS) * gain_ref[...]).astype(jnp.bfloat16)
+    norm_ref[...] = normed
+    sig = 1.0 / (1.0 + jnp.exp(-dot_nn(x, wsel_ref[...])))
+    sig_ref[...] = sig
+    gates = sig * mask_ref[...].astype(jnp.float32)
+    cos_two, sin_two = cos_ref[...], sin_ref[...]
+    allowed = window_mask(step, tile, start_ref[...], keep_ref[:, before], keep_ref[:, now])
+    scale = DH ** (-0.5)
+    lanes = lax.broadcasted_iota(jnp.int32, (tile, LANE), 1)
+    lse = jnp.zeros((tile, LANE), jnp.float32)
+    for head in range(heads):
+        cols = slice(head * DH, (head + 1) * DH)
+        value = dot_nn(x, wval_ref[:, head * VEXP * DH : (head + 1) * VEXP * DH])
+        val_ref[:, head * VEXP * DH : (head + 1) * VEXP * DH] = value.astype(jnp.bfloat16)
+        total = jnp.zeros((tile, DH), jnp.float32)
+        for e in range(VEXP):
+            at = head * VEXP + e
+            total = total + gates[:, at : at + 1] * value[:, e * DH : (e + 1) * DH]
+        v_ref[now, cols] = total.astype(jnp.bfloat16)
+    qk = dot_nn(normed, wqk_ref[...])
+    for head in range(heads):
+        cols = slice(head * DH, (head + 1) * DH)
+        q_head = (spin(qk[:, cols], cos_two, sin_two) * scale).astype(jnp.bfloat16)
+        k_head = spin(
+            qk[:, (heads + head) * DH : (heads + head + 1) * DH], cos_two, sin_two
+        ).astype(jnp.bfloat16)
+        q_ref[:, cols] = q_head
+        k_ref[now, cols] = k_head
+        scores = jnp.concatenate(
+            [dot_nt(q_head, k_ref[before, cols]), dot_nt(q_head, k_head)], axis=1
+        )
+        scores = jnp.where(allowed, scores, MASK_FILL)
+        row_max = jnp.max(scores, axis=1, keepdims=True)
+        terms = jnp.exp(scores - row_max)
+        row_sum = jnp.sum(terms, axis=1, keepdims=True)
+        probs = (terms * (1.0 / row_sum)).astype(jnp.bfloat16)
+        attended = dot_nn(probs[:, :tile], v_ref[before, cols]) + dot_nn(
+            probs[:, tile:], v_ref[now, cols]
+        )
+        att_ref[:, cols] = attended
+        lse = jnp.where(lanes == head, row_max + jnp.log(row_sum), lse)
+        for e in range(VEXP):
+            at = head * VEXP + e
+            gate = gates[:, heads * VEXP + at : heads * VEXP + at + 1]
+            mix_ref[:, at * DH : (at + 1) * DH] = (gate * attended).astype(jnp.bfloat16)
+    lse_ref[...] = lse
+    hidden = x_f + dot_nn(mix_ref[...], wout_ref[...])
+    hid_ref[...] = hidden
+    sent_all[now, :] = hidden.astype(jnp.bfloat16)
+    for index in range(steps):
+
+        @pl.when(step == index)
+        def _(index=index):
+            tile_copy(index).start()
+
+    @pl.when(step == steps - 1)
+    def _():
+        for copy in copies:
+            copy.wait()
+        for index in range(steps):
+            tile_copy(index).wait()
+
+
+def whole_block(shape):
+    return pl.BlockSpec(shape, lambda step: (0,) * len(shape), pipeline_mode=pl.Buffered(1))
+
+
+def attention_forward(own, cot, x, start, keep, cos_two, sin_two, mask, gain, wqk, wsel, wval, wout, tile):
+    rows, model = x.shape
+    heads = wqk.shape[1] // (2 * DH)
+    per_tile = lambda width: pl.BlockSpec((tile, width), lambda step: (step, 0))
+    full = lambda arr: whole_block(arr.shape)
+    narrow, wide = heads * DH, heads * VEXP * DH
+    shapes = [
+        (model, jnp.float32, False),
+        (model, jnp.bfloat16, False),
+        (narrow, jnp.bfloat16, False),
+        (narrow, jnp.bfloat16, True),
+        (narrow, jnp.bfloat16, True),
+        (wide, jnp.bfloat16, False),
+        (narrow, jnp.float32, False),
+        (LANE, jnp.float32, False),
+        (LANE, jnp.float32, False),
+        (wide, jnp.bfloat16, False),
+        (model, jnp.bfloat16, True),
+    ]
+    return pl.pallas_call(
+        functools.partial(forward_body, heads, tile, rows // tile),
+        grid=(rows // tile,),
+        in_specs=[
+            ANYWHERE,
+            ANYWHERE,
+            per_tile(model),
+            per_tile(1),
+            full(keep),
+            per_tile(LANE),
+            per_tile(LANE),
+            per_tile(LANE),
+            full(gain),
+            full(wqk),
+            full(wsel),
+            full(wval),
+            full(wout),
+        ],
+        out_specs=[ANYWHERE] * 3
+        + [whole_block((rows, width)) if whole else per_tile(width) for width, _, whole in shapes],
+        out_shape=[
+            jax.ShapeDtypeStruct(own.shape, jnp.bfloat16),
+            jax.ShapeDtypeStruct((rows, model), jnp.bfloat16),
+            jax.ShapeDtypeStruct((rows, model), jnp.bfloat16),
+        ]
+        + [jax.ShapeDtypeStruct((rows, width), kind) for width, kind, _ in shapes],
+        scratch_shapes=[
+            pltpu.SemaphoreType.DMA((2,)),
+            pltpu.SemaphoreType.DMA((2,)),
+            pltpu.SemaphoreType.DMA((rows // tile,)),
+            pltpu.SemaphoreType.DMA((rows // tile,)),
+        ],
+        compiler_params=pltpu.CompilerParams(
+            vmem_limit_bytes=VMEM_BYTES, collective_id=1, has_side_effects=True
+        ),
+        cost_estimate=pl.CostEstimate(
+            flops=2 * rows * model * (2 * narrow + 2 * wide), bytes_accessed=40 << 20, transcendentals=0
+        ),
+    )(own, cot, x, start, keep, cos_two, sin_two, mask, gain, wqk, wsel, wval, wout)
+
+
+def backward_body(heads, tile, steps, moves, n_in, n_out, *refs):
+    ins, refs = refs[:n_in], refs[n_in:]
+    (
+        dy_ref,
+        q_ref,
+        k_ref,
+        v_ref,
+        att_ref,
+        lse_ref,
+        start_ref,
+        keep_ref,
+        sig_now_ref,
+        mask_now_ref,
+        cos_now_ref,
+        sin_now_ref,
+        sig_old_ref,
+        mask_old_ref,
+        cos_old_ref,
+        sin_old_ref,
+        x_ref,
+        val_ref,
+        dhid_ref,
+        gain_ref,
+        wqk_ref,
+        wsel_ref,
+        wval_ref,
+        wout_ref,
+        *outs_and_rest,
+    ) = refs
+    outs, rest = outs_and_rest[:n_out], outs_and_rest[n_out:]
+    (
+        gin_ref,
+        dqk_ref,
+        dval_ref,
+        dlog_ref,
+        ggain_ref,
+        dk_acc,
+        dv_acc,
+        dq_keep,
+        dgate_keep,
+        gain_acc,
+        send_sem,
+        recv_sem,
+    ) = rest
+    step = pl.program_id(0)
+    copies = copies_of(moves, ins, outs, send_sem, recv_sem)
+
+    @pl.when(step == 0)
+    def _():
+        greet(peers_of(moves))
+        for copy in copies:
+            copy.start()
+
+    slot = lax.rem(step, 2)
+    old = 1 - slot
+    lanes = lax.broadcasted_iota(jnp.int32, (tile, LANE), 1)
+    scale = DH ** (-0.5)
+    narrow = heads * DH
+
+    @pl.when(step == 0)
+    def _():
+        gain_acc[...] = jnp.zeros_like(gain_acc)
+        dk_acc[...] = jnp.zeros_like(dk_acc)
+        dv_acc[...] = jnp.zeros_like(dv_acc)
+
+    @pl.when(step < steps)
+    def _():
+        now = tile_rows(jnp.minimum(step, steps - 1), tile)
+        before = tile_rows(jnp.maximum(step - 1, 0), tile)
+        allowed = window_mask(step, tile, start_ref[...], keep_ref[:, before], keep_ref[:, now])
+        gates = sig_now_ref[...] * mask_now_ref[...].astype(jnp.float32)
+        dy = dy_ref[...]
+        dgate = jnp.zeros((tile, LANE), jnp.float32)
+        for head in range(heads):
+            cols = slice(head * DH, (head + 1) * DH)
+            dmixed = dot_nt(dy, wout_ref[head * VEXP * DH : (head + 1) * VEXP * DH, :])
+            attended = att_ref[:, cols]
+            dattend = jnp.zeros((tile, DH), jnp.float32)
+            for e in range(VEXP):
+                at = (heads + head) * VEXP + e
+                part = dmixed[:, e * DH : (e + 1) * DH]
+                dattend = dattend + gates[:, at : at + 1] * part
+                dgate = jnp.where(
+                    lanes == at, jnp.sum(part * attended, axis=1, keepdims=True), dgate
+                )
+            dattend = dattend.astype(jnp.bfloat16)
+            q_head = q_ref[:, cols]
+            k_old, k_now = k_ref[before, cols], k_ref[now, cols]
+            v_old, v_now = v_ref[before, cols], v_ref[now, cols]
+            scores = jnp.concatenate([dot_nt(q_head, k_old), dot_nt(q_head, k_now)], axis=1)
+            scores = jnp.where(allowed, scores, MASK_FILL)
+            probs = jnp.exp(scores - lse_ref[:, head : head + 1])
+            dprob = jnp.concatenate([dot_nt(dattend, v_old), dot_nt(dattend, v_now)], axis=1)
+            delta = jnp.sum(probs * dprob, axis=1, keepdims=True)
+            dscore = (probs * (dprob - delta)).astype(jnp.bfloat16)
+            probs = probs.astype(jnp.bfloat16)
+            dv_acc[old, :, cols] += dot_tn(probs[:, :tile], dattend)
+            dv_acc[slot, :, cols] = dot_tn(probs[:, tile:], dattend)
+            dk_acc[old, :, cols] += dot_tn(dscore[:, :tile], q_head)
+            dk_acc[slot, :, cols] = dot_tn(dscore[:, tile:], q_head)
+            dq = dot_nn(dscore[:, :tile], k_old) + dot_nn(dscore[:, tile:], k_now)
+            dq_keep[slot, :, cols] = (
+                spin_back(dq, cos_now_ref[...], sin_now_ref[...]) * scale
+            ).astype(jnp.bfloat16)
+        dgate_keep[slot] = dgate
+
+    @pl.when(step > 0)
+    def _():
+        sig = sig_old_ref[...]
+        mask = mask_old_ref[...].astype(jnp.float32)
+        gates = sig * mask
+        dgate = dgate_keep[old]
+        for head in range(heads):
+            cols = slice(head * DH, (head + 1) * DH)
+            dqk_ref[:, cols] = dq_keep[old, :, cols]
+            dqk_ref[:, narrow + head * DH : narrow + (head + 1) * DH] = spin_back(
+                dk_acc[old, :, cols], cos_old_ref[...], sin_old_ref[...]
+            ).astype(jnp.bfloat16)
+            dvalue = dv_acc[old, :, cols]
+            for e in range(VEXP):
+                at = head * VEXP + e
+                wide = slice(at * DH, (at + 1) * DH)
+                val = val_ref[:, wide].astype(jnp.float32)
+                dgate = jnp.where(lanes == at, jnp.sum(dvalue * val, axis=1, keepdims=True), dgate)
+                dval_ref[:, wide] = (gates[:, at : at + 1] * dvalue).astype(jnp.bfloat16)
+        dlog = (dgate * gates * (1.0 - sig)).astype(jnp.bfloat16)
+        dlog_ref[...] = dlog
+        dnormed = dot_nt(dqk_ref[...], wqk_ref[...])
+        x_f = x_ref[...].astype(jnp.float32)
+        center = x_f - jnp.mean(x_f, axis=1, keepdims=True)
+        inv = lax.rsqrt(jnp.mean(center * center, axis=1, keepdims=True) + NORM_EPS)
+        x_hat = center * inv
+        gain_acc[...] += jnp.sum(dnormed * x_hat, axis=0, keepdims=True)
+        grad = dnormed * gain_ref[...]
+        dx = inv * (
+            grad
+            - jnp.mean(grad, axis=1, keepdims=True)
+            - x_hat * jnp.mean(grad * x_hat, axis=1, keepdims=True)
+        )
+        dx = dx + dhid_ref[...] + dot_nt(dval_ref[...], wval_ref[...]) + dot_nt(dlog, wsel_ref[...])
+        gin_ref[...] = dx.astype(jnp.bfloat16)
+
+    @pl.when(step == steps)
+    def _():
+        gain = gain_acc[...]
+        high = gain.astype(jnp.bfloat16).astype(jnp.float32)
+        row = lax.broadcasted_iota(jnp.int32, (GAIN_ROWS, gain.shape[1]), 0)
+        split = jnp.where(row == 0, high, jnp.where(row == 1, gain - high, 0.0))
+        ggain_ref[...] = split.astype(jnp.bfloat16)
+        for copy in copies:
+            copy.wait()
+
+
+def attention_backward(
+    sources, results, moves, dy, q, k, v, att, lse, start, keep, sig, mask, cos_two, sin_two, x, val, dhid, gain, wqk, wsel, wval, wout, tile
+):
+    rows, model = x.shape
+    heads = wqk.shape[1] // (2 * DH)
+    steps = rows // tile
+    narrow, wide = heads * DH, heads * VEXP * DH
+    at_now = lambda width: pl.BlockSpec((tile, width), lambda step: (jnp.minimum(step, steps - 1), 0))
+    at_old = lambda width: pl.BlockSpec((tile, width), lambda step: (jnp.maximum(step - 1, 0), 0))
+    full = lambda arr: whole_block(arr.shape)
+    return pl.pallas_call(
+        functools.partial(backward_body, heads, tile, steps, moves, len(sources), len(results)),
+        grid=(steps + 1,),
+        in_specs=[ANYWHERE] * len(sources)
+        + [
+            at_now(model),
+            at_now(narrow),
+            full(k),
+            full(v),
+            at_now(narrow),
+            at_now(LANE),
+            at_now(1),
+            full(keep),
+            at_now(LANE),
+            at_now(LANE),
+            at_now(LANE),
+            at_now(LANE),
+            at_old(LANE),
+            at_old(LANE),
+            at_old(LANE),
+            at_old(LANE),
+            at_old(model),
+            at_old(wide),
+            at_old(model),
+            full(gain),
+            full(wqk),
+            full(wsel),
+            full(wval),
+            full(wout),
+        ],
+        out_specs=[ANYWHERE] * len(results)
+        + [
+            at_old(model),
+            at_old(2 * narrow),
+            at_old(wide),
+            at_old(LANE),
+            whole_block((GAIN_ROWS, model)),
+        ],
+        out_shape=[jax.ShapeDtypeStruct(shape, jnp.bfloat16) for shape in results]
+        + [
+            jax.ShapeDtypeStruct((rows, model), jnp.bfloat16),
+            jax.ShapeDtypeStruct((rows, 2 * narrow), jnp.bfloat16),
+            jax.ShapeDtypeStruct((rows, wide), jnp.bfloat16),
+            jax.ShapeDtypeStruct((rows, LANE), jnp.bfloat16),
+            jax.ShapeDtypeStruct((GAIN_ROWS, model), jnp.bfloat16),
+        ],
+        scratch_shapes=[
+            pltpu.VMEM((2, tile, narrow), jnp.float32),
+            pltpu.VMEM((2, tile, narrow), jnp.float32),
+            pltpu.VMEM((2, tile, narrow), jnp.bfloat16),
+            pltpu.VMEM((2, tile, LANE), jnp.float32),
+            pltpu.VMEM((1, model), jnp.float32),
+            pltpu.SemaphoreType.DMA((len(moves),)),
+            pltpu.SemaphoreType.DMA((len(moves),)),
+        ],
+        compiler_params=pltpu.CompilerParams(
+            vmem_limit_bytes=VMEM_BYTES, collective_id=6, has_side_effects=True
+        ),
+        cost_estimate=pl.CostEstimate(
+            flops=2 * rows * model * (2 * narrow + 2 * wide), bytes_accessed=50 << 20, transcendentals=0
+        ),
+    )(
+        *sources, dy, q, k, v, att, lse, start, keep, sig, mask, cos_two, sin_two, sig, mask, cos_two, sin_two,
+        x, val, dhid, gain, wqk, wsel, wval, wout,
+    )
+
+
+def outer_body(groups, *refs):
+    out_ref = refs[-1]
+    at = 0
+    for pairs in groups:
+        total = sum(dot_tn(refs[left][...], refs[right][...]) for left, right in pairs)
+        out_ref[:, at : at + total.shape[1]] = total.astype(jnp.bfloat16)
+        at += total.shape[1]
+
+
+def outer_products(arrays, groups, lefts, block):
+    rows, model = arrays[0].shape
+    width = sum(arrays[pairs[0][1]].shape[1] for pairs in groups)
+    return pl.pallas_call(
+        functools.partial(outer_body, groups),
+        grid=(model // block,),
+        in_specs=[
+            pl.BlockSpec((arr.shape[0], block), lambda step: (0, step))
+            if i < lefts
+            else whole_block(arr.shape)
+            for i, arr in enumerate(arrays)
+        ],
+        out_specs=pl.BlockSpec((block, width), lambda step: (step, 0)),
+        out_shape=jax.ShapeDtypeStruct((model, width), jnp.bfloat16),
+        compiler_params=pltpu.CompilerParams(vmem_limit_bytes=VMEM_BYTES),
+        cost_estimate=pl.CostEstimate(
+            flops=2 * rows * model * width, bytes_accessed=20 << 20, transcendentals=0
+        ),
+    )(*arrays)
+
+
+def expert_body(first, last, exp_local, ff_dim, tile, steps, moves, n_in, n_out, *refs):
+    ins, refs = refs[:n_in], refs[n_in:]
+    x_own, x_far, c_own, c_far, w_ref, mask_ref, digit_ref = refs[:7]
+    at = 7
+    if not first:
+        out_in, grad_in = refs[at : at + 2]
+        at += 2
+    if last:
+        hid_ref = refs[at]
+        at += 1
+    outs = refs[at : at + n_out]
+    at += n_out
+    results = refs[at : at + 3]
+    g_ref = refs[at + 3 if last else at + 2]
+    at += 4 if last else 3
+    act_all, dpre_all, x_ref, c_ref, load_sem, send_sem, recv_sem = refs[at : at + 7]
+    wide = exp_local * ff_dim
+    back = wide + ROUTER_ROWS
+    half = steps // 2
+    step = pl.program_id(0)
+    copies = copies_of(moves, ins, outs, send_sem, recv_sem)
+    peers = peers_of(moves)
+    if last:
+        given, taken, tile_send, tile_recv = refs[at + 7 :]
+        partner = neighbour("core", 1)
+        peers.append(partner)
+
+        def tile_copy(index, kind):
+            return pltpu.make_async_remote_copy(
+                src_ref=given.at[kind, pl.ds(index * tile, tile)],
+                dst_ref=taken.at[kind, pl.ds(index * tile, tile)],
+                send_sem=tile_send.at[kind, index],
+                recv_sem=tile_recv.at[kind, index],
+                device_id=partner,
+                device_id_type=pl.DeviceIdType.MESH,
+            )
+
+    def load(index, kind):
+        near, far, whole = ((x_own, x_far, x_ref), (c_own, c_far, c_ref))[kind]
+        source = near if index < half else far
+        return pltpu.make_async_copy(
+            source.at[pl.ds(index % half * tile, tile)],
+            whole.at[pl.ds(index * tile, tile)],
+            load_sem.at[kind, index],
+        )
+
+    @pl.when(step == 0)
+    def _():
+        for turn in range(steps):
+            for kind in range(2):
+                load((turn + half) % steps if last else turn, kind).start()
+        greet(peers)
+        for copy in copies:
+            copy.start()
+
+    for turn in range(steps):
+
+        @pl.when(step == turn)
+        def _(turn=turn):
+            for kind in range(2):
+                load((turn + half) % steps if last else turn, kind).wait()
+
+    rows = tile_rows(lax.rem(step + half, steps) if last else step, tile)
+    x, c = x_ref[rows, :], c_ref[rows, :]
+    sig = 1.0 / (1.0 + jnp.exp(-dot_nt(x, w_ref[wide:back, :])))
+    gate = sig * mask_ref[:, :ROUTER_ROWS].astype(jnp.float32)
+    lanes = lax.broadcasted_iota(jnp.int32, (tile, ROUTER_ROWS), 1)
+    dgate = jnp.zeros((tile, ROUTER_ROWS), jnp.float32)
+    for pair in range(exp_local // 2):
+        lo, hi = 2 * pair * ff_dim, 2 * (pair + 1) * ff_dim
+        pre_two = dot_nt(x, w_ref[lo:hi, :])
+        raw_two = dot_nt(c, w_ref[back + lo : back + hi, :])
+        for side in range(2):
+            e = 2 * pair + side
+            pre = pre_two[:, side * ff_dim : (side + 1) * ff_dim]
+            raw = raw_two[:, side * ff_dim : (side + 1) * ff_dim]
+            square = pre * pre
+            bend = jnp.tanh(pre * (GELU_A + GELU_A * GELU_B * square))
+            upper = 0.5 * bend + 0.5
+            act = (pre * upper).astype(jnp.bfloat16).astype(jnp.float32)
+            slope = upper + (0.5 * pre) * (1.0 - bend * bend) * (GELU_A + 3 * GELU_A * GELU_B * square)
+            gate_col = gate[:, e : e + 1]
+            act_all[rows, e * ff_dim : (e + 1) * ff_dim] = (gate_col * act).astype(jnp.bfloat16)
+            dpre_all[rows, e * ff_dim : (e + 1) * ff_dim] = (gate_col * raw * slope).astype(
+                jnp.bfloat16
+            )
+            dgate = jnp.where(lanes == e, jnp.sum(act * raw, axis=1, keepdims=True), dgate)
+    dpre_all[rows, wide:back] = (dgate * gate * (1.0 - sig)).astype(jnp.bfloat16)
+    out_new = dot_nn(act_all[rows, :], w_ref[back:, :])
+    grad_new = dot_nn(dpre_all[rows, :], w_ref[:back, :])
+    if not first:
+        out_new = out_new + out_in[...]
+        grad_new = grad_new + grad_in[...]
+    if last:
+
+        @pl.when(step < half)
+        def _():
+            mine = tile_rows(jnp.minimum(step, half - 1), tile)
+            given[0, mine, :] = out_new.astype(jnp.bfloat16)
+            given[1, mine, :] = grad_new.astype(jnp.bfloat16)
+
+        for index in range(half):
+
+            @pl.when(step == index)
+            def _(index=index):
+                tile_copy(index, 0).start()
+                tile_copy(index, 1).start()
+
+            @pl.when(step == index + half)
+            def _(index=index):
+                tile_copy(index, 0).wait_recv()
+                tile_copy(index, 1).wait_recv()
+
+        @pl.when(step >= half)
+        def _():
+            mine = tile_rows(jnp.maximum(step - half, 0), tile)
+            total = hid_ref[...] + out_new + taken[0, mine, :].astype(jnp.float32)
+            results[0][...] = total.astype(jnp.bfloat16)
+            dhidden = c.astype(jnp.float32) + grad_new + taken[1, mine, :].astype(jnp.float32)
+            results[1][...] = dhidden
+            results[2][...] = dhidden.astype(jnp.bfloat16)
+
+    else:
+        results[0][...] = out_new
+        results[1][...] = grad_new
+
+    @pl.when(step == steps - 1)
+    def _():
+        for lo in range(0, wide, 2 * ff_dim):
+            g_ref[lo : lo + 2 * ff_dim, :] = dot_tn(
+                dpre_all[:, lo : lo + 2 * ff_dim], x_ref[...]
+            ).astype(jnp.bfloat16)
+            g_ref[back + lo : back + lo + 2 * ff_dim, :] = dot_tn(
+                act_all[:, lo : lo + 2 * ff_dim], c_ref[...]
+            ).astype(jnp.bfloat16)
+        extra = dot_tn(dpre_all[:, wide:back], x_ref[...])
+        g_ref[wide:back, :LANE] = (extra[:, :LANE] + digit_ref[...]).astype(jnp.bfloat16)
+        g_ref[wide:back, LANE:] = extra[:, LANE:].astype(jnp.bfloat16)
+        for copy in copies:
+            copy.wait()
+        if last:
+            for index in range(half):
+                tile_copy(index, 0).wait_send()
+                tile_copy(index, 1).wait_send()
+
+
+def expert_chunk(
+    sources, results, aliases, moves, tokens, weights, masks, digits, hop, sums, hidden, exp_local, ff_dim, tile
+):
+    rows, model = 2 * tokens[0].shape[0], tokens[0].shape[1]
+    steps = rows // tile
+    half = steps // 2
+    first, last = sums is None, hidden is not None
+    turn = (lambda step: lax.rem(step + half, steps)) if last else (lambda step: step)
+    per_tile = lambda: pl.BlockSpec((tile, model), lambda step: (turn(step), 0))
+    late = lambda: pl.BlockSpec((tile, model), lambda step: (jnp.maximum(step - half, 0), 0))
+    in_specs = [ANYWHERE] * (len(sources) + 4) + [
+        whole_block(weights.shape),
+        pl.BlockSpec((tile, LANE), lambda step: (turn(step), hop)),
+        pl.BlockSpec((ROUTER_ROWS, LANE), lambda step: (0, hop)),
+    ]
+    args = list(sources) + list(tokens) + [weights, masks, digits]
+    if not first:
+        in_specs += [per_tile(), per_tile()]
+        args += list(sums)
+    wide = exp_local * ff_dim
+    scratch = [
+        pltpu.VMEM((rows, wide), jnp.bfloat16),
+        pltpu.VMEM((rows, wide + ROUTER_ROWS), jnp.bfloat16),
+        pltpu.VMEM((rows, model), jnp.bfloat16),
+        pltpu.VMEM((rows, model), jnp.bfloat16),
+        pltpu.SemaphoreType.DMA((2, steps)),
+        pltpu.SemaphoreType.DMA((len(moves),)),
+        pltpu.SemaphoreType.DMA((len(moves),)),
+    ]
+    if last:
+        in_specs.append(late())
+        args.append(hidden)
+        out_specs = [late(), late(), late()]
+        out_shape = [
+            jax.ShapeDtypeStruct((rows // 2, model), kind)
+            for kind in (jnp.bfloat16, jnp.float32, jnp.bfloat16)
+        ]
+        scratch += [
+            pltpu.VMEM((2, rows // 2, model), jnp.bfloat16),
+            pltpu.VMEM((2, rows // 2, model), jnp.bfloat16),
+            pltpu.SemaphoreType.DMA((2, half)),
+            pltpu.SemaphoreType.DMA((2, half)),
+        ]
+    else:
+        out_specs = [per_tile(), per_tile()]
+        out_shape = [jax.ShapeDtypeStruct((rows, model), jnp.float32)] * 2
+    outs = pl.pallas_call(
+        functools.partial(
+            expert_body, first, last, exp_local, ff_dim, tile, steps, moves, len(sources), len(results)
+        ),
+        grid=(steps,),
+        in_specs=in_specs,
+        out_specs=[ANYWHERE] * len(results) + out_specs + [whole_block(weights.shape)],
+        out_shape=[jax.ShapeDtypeStruct(shape, jnp.bfloat16) for shape in results]
+        + out_shape
+        + [jax.ShapeDtypeStruct(weights.shape, jnp.bfloat16)],
+        input_output_aliases=aliases,
+        scratch_shapes=scratch,
+        compiler_params=pltpu.CompilerParams(
+            vmem_limit_bytes=VMEM_BYTES, collective_id=2 + hop, has_side_effects=True
+        ),
+        cost_estimate=pl.CostEstimate(
+            flops=12 * rows * model * wide, bytes_accessed=40 << 20, transcendentals=rows * wide
+        ),
+    )(*args)
+    return outs[: len(results)], outs[len(results) : -1], outs[-1]
+
+
+def core_swap(arr):
+    size = lax.axis_size("expert")
+    return lax.ppermute(arr, "expert", [(i, i ^ 1) for i in range(size)])
+
+
+def chip_shift(arr, hop):
+    size = lax.axis_size("expert")
+    chips = size // 2
+    return lax.ppermute(
+        arr, "expert", [(i, (i // 2 + hop) % chips * 2 + i % 2) for i in range(size)]
+    )
+
+
+def dp_swap(arr, flip):
+    return lax.ppermute(arr, "dp", [(i, i ^ flip) for i in range(lax.axis_size("dp"))])
+
+
+def row_part(arr, index, count):
+    return lax.dynamic_slice_in_dim(arr, index * (arr.shape[0] // count), arr.shape[0] // count, 0)
+
+
+def dp_gather(part):
+    mine = lax.axis_index("dp")
+    rows = part.shape[0]
+    whole = jnp.zeros((4 * rows,) + part.shape[1:], part.dtype)
+    for flip in range(4):
+        piece = part if flip == 0 else dp_swap(part, flip)
+        whole = lax.dynamic_update_slice_in_dim(whole, piece, (mine ^ flip) * rows, 0)
+    return whole
+
+
+def dp_scatter(whole):
+    mine = lax.axis_index("dp")
+    total = row_part(whole, mine, 4).astype(jnp.float32)
+    for flip in range(1, 4):
+        total = total + dp_swap(row_part(whole, mine ^ flip, 4), flip).astype(jnp.float32)
+    return total
+
+
+def scatter_rows(whole):
+    dev_count = lax.axis_size("expert")
+    chips = dev_count // 2
+    rows, width = whole.shape
+    mine = lax.axis_index("expert")
+    chip, core = mine // 2, mine % 2
+    by_core = whole.reshape(4 * chips, 2, rows // (8 * chips), width)
+    kept = lax.dynamic_index_in_dim(by_core, core, 1, keepdims=False)
+    given = lax.dynamic_index_in_dim(by_core, 1 - core, 1, keepdims=False)
+    pair = (kept.astype(jnp.float32) + core_swap(given).astype(jnp.float32)).astype(jnp.bfloat16)
+    quarter = dp_scatter(pair.reshape(rows // 2, width)).astype(jnp.bfloat16)
+    total = row_part(quarter, chip, chips).astype(jnp.float32)
+    for hop in range(1, chips):
+        piece = row_part(quarter, (chip + hop) % chips, chips)
+        total = total + chip_shift(piece, hop).astype(jnp.float32)
+    return total
+
+
+def own_weights(w_router, w_in, w_out):
+    exp_local, model_dim, ff_dim = w_in.shape
+    router_rows = jnp.zeros((ROUTER_ROWS, model_dim), jnp.bfloat16).at[:exp_local].set(w_router)
+    return jnp.concatenate(
+        [
+            jnp.swapaxes(w_in, 1, 2).reshape(exp_local * ff_dim, model_dim),
+            router_rows,
+            w_out.reshape(exp_local * ff_dim, model_dim),
+        ]
+    )
+
+
+def block_dense(
+    layer_input,
+    segments,
+    keep_mask,
+    att_routes,
+    moe_routes,
+    expert_counts,
+    norm_gain,
+    w_query,
+    w_key,
+    w_select,
+    w_value,
+    w_output,
+    w_router,
+    w_in,
+    w_out,
+    cotangent,
+):
+    rows, model = layer_input.shape
+    seqs, seq_len = segments.shape
+    exp_local, _, ff_dim = w_in.shape
+    heads = w_query.shape[1] // DH
+    chips = lax.axis_size("expert") // 2
+    wide, narrow, gates = heads * VEXP * DH, heads * DH, 2 * heads * VEXP
+    moe_wide = exp_local * ff_dim
+    mine = lax.axis_index("expert")
+    chip, core = mine // 2, mine % 2
+
+    own = own_weights(w_router, w_in, w_out)
+    exp_total = 2 * chips * exp_local
+    named = jnp.sum(
+        (moe_routes[..., None] == jnp.arange(exp_total, dtype=jnp.int32)).astype(jnp.bfloat16), axis=1
+    )
+    named = jnp.concatenate([named, core_swap(named)])
+
+    column = jnp.arange(seq_len, dtype=jnp.int32)
+    changed = jnp.concatenate(
+        [jnp.ones((seqs, 1), jnp.bool_), segments[:, 1:] != segments[:, :-1]], axis=1
+    )
+    start = lax.cummax(jnp.where(changed, column, 0), axis=1)
+    cos_tab, sin_tab = rope_tables((column - start).reshape(-1), DH)
+    cos_two = jnp.concatenate([cos_tab, cos_tab], axis=1)
+    sin_two = jnp.concatenate([-sin_tab, sin_tab], axis=1)
+    start = (start + seq_len * jnp.arange(seqs, dtype=jnp.int32)[:, None]).reshape(rows, 1)
+    keep = keep_mask.reshape(1, rows)
+    att_mask = jnp.sum(
+        (att_routes[..., None] == jnp.arange(VEXP, dtype=jnp.int32)).astype(jnp.bfloat16), axis=2
+    ).reshape(rows, gates)
+    att_mask = jnp.pad(att_mask, ((0, 0), (0, LANE - gates)))
+    gain_row = norm_gain.reshape(1, model)
+    wqk = jnp.concatenate([w_query, w_key], axis=1)
+    wsel = jnp.pad(w_select, ((0, 0), (0, LANE - gates)))
+
+    second, cot_far, sent_far, hidden, normed, q_rot, k_rot, value_bf, value_all, attended, sig, lse, mixed, sent = (
+        attention_forward(
+            own, cotangent, layer_input, start, keep, cos_two, sin_two, att_mask, gain_row, wqk, wsel, w_value, w_output, TILE
+        )
+    )
+
+    lane = jnp.arange(chips * LANE, dtype=jnp.int32)
+    owner = ((chip + lane // LANE) % chips * 2 + core) * exp_local + lane % LANE
+    pick = (lane % LANE < exp_local) & (jnp.arange(exp_total, dtype=jnp.int32)[:, None] == owner)
+    masks = jnp.dot(named, pick.astype(jnp.bfloat16), preferred_element_type=jnp.float32)
+    counts = jnp.sum(masks, axis=0).astype(jnp.int32)
+    masks = masks.astype(jnp.bfloat16)
+    place = jnp.arange(ROUTER_ROWS, dtype=jnp.int32)[:, None] - exp_local
+    digits = jnp.where(
+        (place >= 0) & (place < DIGITS), (counts >> (2 * jnp.clip(place, 0, DIGITS))) & 3, 0
+    ).astype(jnp.float32)
+
+    part = own.shape[0] // 4
+    shape, three = own.shape, (3 * part, model)
+
+    def run(hop, sources, results, aliases, moves, weights, sums, last_hidden):
+        return expert_chunk(
+            sources, results, aliases, moves, (sent, sent_far, cotangent, cot_far), weights, masks, digits, hop, sums,
+            last_hidden, exp_local, ff_dim, TILE,
+        )
+
+    def sum_parts(whole, three_parts):
+        total = row_part(whole, lax.axis_index("dp"), 4).astype(jnp.float32)
+        for flip in range(3):
+            total = total + three_parts[flip * part : (flip + 1) * part].astype(jnp.float32)
+        return total
+
+    (second, third, first), sums, grad_0 = run(
+        0,
+        [second, own],
+        [shape, shape, shape],
+        {0: 0},
+        gather_moves(0, 0, part)
+        + shift_move(1, 1, -3, own_part(part), own_part(part), part)
+        + shift_move(1, 2, -1, fixed(0), fixed(0), part),
+        own,
+        None,
+        None,
+    )
+    (third, first), sums, grad_2 = run(
+        2,
+        [third, first, own],
+        [shape, shape],
+        {0: 0, 1: 1},
+        gather_moves(0, 0, part) + shift_move(2, 1, -1, fixed(part), fixed(part), 2 * part),
+        second,
+        sums,
+        None,
+    )
+    (first, from_2), sums, grad_3 = run(
+        3,
+        [first, own, grad_2],
+        [shape, three],
+        {0: 0},
+        shift_move(1, 0, -1, fixed(3 * part), fixed(3 * part), part) + scatter_moves(2, 1, part),
+        third,
+        sums,
+        None,
+    )
+    part_2 = sum_parts(grad_2, from_2).astype(jnp.bfloat16)
+    (from_3, got_2), (layer_output, dhidden, dy), grad_1 = run(
+        1,
+        [grad_3, part_2],
+        [three, (part, model)],
+        {},
+        scatter_moves(0, 0, part) + shift_move(1, 1, 2, fixed(0), fixed(0), part),
+        first,
+        sums,
+        hidden,
+    )
+    part_3 = sum_parts(grad_3, from_3).astype(jnp.bfloat16)
+    out_joined = outer_products([dy, mixed], [[(0, 1)]], 1, TILE)
+    from_0, got_3, grad_input, dqk, dval, dlog, gain_rows = attention_backward(
+        [grad_0, part_3],
+        [three, (part, model)],
+        scatter_moves(0, 0, part) + shift_move(1, 1, 3, fixed(0), fixed(0), part),
+        dy, q_rot, k_rot, value_bf, attended, lse, start, keep, sig, att_mask, cos_two, sin_two,
+        layer_input, value_all, dhidden, gain_row, wqk, wsel, w_value, w_output, TILE,
+    )
+    out_sum = scatter_rows(out_joined).T
+    part_1 = dp_scatter(grad_1).astype(jnp.bfloat16)
+    total = sum_parts(grad_0, from_0) + got_2.astype(jnp.float32) + got_3.astype(jnp.float32)
+    total = total + chip_shift(part_1, 1).astype(jnp.float32)
+    summed = dp_gather(total.astype(jnp.bfloat16)).astype(jnp.float32)
+    grad_w_in = jnp.swapaxes(summed[:moe_wide].reshape(exp_local, ff_dim, model), 1, 2)
+    extra = summed[moe_wide : moe_wide + ROUTER_ROWS]
+    grad_router = extra[:exp_local]
+    parts = extra[exp_local : exp_local + DIGITS, :exp_local].astype(jnp.int32)
+    tally = sum(parts[i] << (2 * i) for i in range(DIGITS))
+    grad_w_out = summed[moe_wide + ROUTER_ROWS :].reshape(exp_local, ff_dim, model)
+
+    unit = (
+        (jnp.arange(GAIN_ROWS)[:, None] < 2) & (jnp.arange(LANE)[None, :] == gates)
+    ).astype(jnp.bfloat16)
+    joined = outer_products(
+        [layer_input, normed, gain_rows, dval, dlog, dqk, unit],
+        [[(0, 3)], [(0, 4), (2, 6)], [(1, 5)]],
+        3,
+        TILE,
+    )
+    summed = scatter_rows(joined)
+    at_qk = wide + LANE
+    return (
+        layer_output,
+        grad_input,
+        summed[:, wide + gates],
+        summed[:, at_qk : at_qk + narrow],
+        summed[:, at_qk + narrow : at_qk + 2 * narrow],
+        summed[:, wide : wide + gates],
+        summed[:, :wide],
+        out_sum,
+        grad_router,
+        grad_w_in,
+        grad_w_out,
+        expert_counts + tally,
+    )
+
+
+def block_dispatched(
     layer_input,
     segments,
     keep_mask,
@@ -355,6 +1384,15 @@
     )
 
 
+def local(*args):
+    rows, top_k = args[4].shape
+    experts, _, ff_dim = args[13].shape
+    exp_total = lax.axis_size("expert") * experts
+    capacity = 10 * rows * top_k // (7 * exp_total) + 1
+    regular = lax.axis_size("dp") == 4 and lax.axis_size("expert") == 8 and experts % 2 == 0 and ff_dim == LANE
+    return (block_dense if regular and 4 * capacity > rows else block_dispatched)(*args)
+
+
 def solution(mesh):
     placed = (
         P(("dp", "expert"), None),

time: 5440 us -> 520 us (0.10)
  the two profiles are of different devices: /device:TPU:0 before, /device:TPU:12 now
where the time goes in v3:
time: 520 us; the launch traced here: 512 us
  Pallas kernels  304 us (58%)
  waiting for transfers between devices  101 us (19%)
  local copies, waits for them, and re-layouts  37.6 us (7%)
  other arithmetic  34 us (7%)
  starting transfers between devices  31.2 us (6%)
    pallas_call x4, Pallas kernels, expert_chunk(): pl.pallas_call(functools.partial(expert_body, first, last, exp_local, ff_...  178 us
    ppermute x12, waiting for transfers between devices, dp_swap(): lax.ppermute(arr, 'dp', [(i, i ^ flip) for i in range(lax.axis_size('dp'))])  84.3 us
    pallas_call x1, Pallas kernels, attention_backward(): pl.pallas_call(functools.partial(backward_body, heads, tile, steps, moves...  53.6 us
    pallas_call x1, Pallas kernels, attention_forward(): pl.pallas_call(functools.partial(forward_body, heads, tile, rows // tile)...  47.5 us
    pallas_call x2, Pallas kernels, outer_products(): pl.pallas_call(functools.partial(outer_body, groups), grid=(model // bloc...  24.3 us
    ppermute x7, starting transfers between devices, chip_shift(): lax.ppermute(arr, 'expert', [(i, (i // 2 + hop) % chips * 2 + i % 2) for...  17.3 us
    ppermute x7, waiting for transfers between devices, chip_shift(): lax.ppermute(arr, 'expert', [(i, (i // 2 + hop) % chips * 2 + i % 2) for...  17.2 us
    ppermute x12, starting transfers between devices, dp_swap(): lax.ppermute(arr, 'dp', [(i, i ^ flip) for i in range(lax.axis_size('dp'))])  13.8 us
  transfers between devices with their start and end apart: 22, of which 10 were waited for; matrix products, arithmetic and copies ran while one was open for 11% of the time, Pallas kernels for 25%

profile of v3, /device:TPU:12, one launch (start us, length us, event | category | flops | bytes accessed | tf_op | source)
XLA Modules:
  0.0 511.6 jit_solution(2902918307071478539)
XLA Ops:
  4.9 1.7 copy.60
  9.8 1.9 fusion.13
  11.7 2.3 constant_dynamic-update-slice_fusion.4.refs_9_.refs_22_
  14.7 1.4 pad_maximum_fusion
  16.0 1.9 fusion.5.refs_0_.refs_1_.refs_6_.refs_2_
  18.0 47.5 %shard_map.247 = (bf16[1600,1024]{1,0:T(8,128)(2,1)}, bf16[1024,1024]{1,0:T(8,128)(2,1)}, bf16[1024,1024]{1,0:T(8,128)(2,1)}, f32[1024,1024]{1,0:T(8,128)}, bf16...) custom-call(bf16[1600,1024]{1,0:T(8,128)(2,1)} %fusion.5.refs_0_.ref, ...), custom_call_target="tpu_custom_call" | custom-call | flops 12884901888 | bytes 41943040 | tf_op jit(solution)/shard_map/pallas_call | solution.py:410
  65.5 2.1 fusion.34
  68.3 44.8 %shard_map.248 = (bf16[1600,1024]{1,0:T(8,128)(2,1)}, bf16[1600,1024]{1,0:T(8,128)(2,1)}, bf16[1600,1024]{1,0:T(8,128)(2,1)}, f32[2048,1024]{1,0:T(8,128)}, f32[...) custom-call(bf16[1600,1024]{1,0:T(8,128)(2,1)} %get-tuple-element.67.refs_0_, ...), custom_call_target="tpu_custom_call", output_to_operand_aliasing={{0}: (0, {})} | custom-call | flops 19327352832 | bytes 41943040 | tf_op jit(solution)/shard_map/pallas_call | solution.py:903
  113.1 45.0 %shard_map.249 = (bf16[1600,1024]{1,0:T(8,128)(2,1)}, bf16[1600,1024]{1,0:T(8,128)(2,1)}, f32[2048,1024]{1,0:T(8,128)}, f32[2048,1024]{1,0:T(8,128)}, bf16[1600,1024]{1,0:T(8,128)(2,1)}) custom-call(bf16[1600,1024]{1,0:T(8,128)(2,1)} %get-tuple-element.71.refs_0_, ...), custom_call_target="tpu_custom_call", output_to_operand_aliasing={{0}: (0, {}), {1}: (1, {})} | custom-call | flops 19327352832 | bytes 41943040 | tf_op jit(solution)/shard_map/pallas_call | solution.py:903
  158.1 44.1 %shard_map.250 = (bf16[1600,1024]{1,0:T(8,128)(2,1)}, bf16[1200,1024]{1,0:T(8,128)(2,1)}, f32[2048,1024]{1,0:T(8,128)}, f32[2048,1024]{1,0:T(8,128)}, bf16[1600,1024]{1,0:T(8,128)(2,1)}) custom-call(bf16[1600,1024]{1,0:T(8,128)(2,1)} %get-tuple-element.76.refs_0_, ...), custom_call_target="tpu_custom_call", output_to_operand_aliasing={{0}: (0, {})} | custom-call | flops 19327352832 | bytes 41943040 | tf_op jit(solution)/shard_map/pallas_call | solution.py:903
  202.2 3.4 add_convert_fusion.4.refs_1_
  205.7 44.4 %shard_map.251 = (bf16[1200,1024]{1,0:T(8,128)(2,1)}, bf16[400,1024]{1,0:T(8,128)(2,1)}, bf16[1024,1024]{1,0:T(8,128)(2,1)}, f32[1024,1024]{1,0:T(8,128)}, bf16[...) custom-call(bf16[1600,1024]{1,0:T(8,128)(2,1)} %get-tuple-element.81.refs_0_, ...), custom_call_target="tpu_custom_call" | custom-call | flops 19327352832 | bytes 41943040 | tf_op jit(solution)/shard_map/pallas_call | solution.py:903
  250.1 2.9 constant_dynamic-slice_fusion.2
  253.6 1.5 collective-permute-start.16
  255.1 1.4 collective-permute-start.17
  256.5 2.7 add_convert_fusion.3.refs_1_
  259.2 10.0 %shard_map.254 = bf16[1024,2560]{1,0:T(8,128)(2,1)} custom-call(bf16[1024,1024]{1,0:T(8,128)(2,1)} %get-tuple-element.90.refs_2_.refs_0_, bf16[1024,2560]{1,0:T(8,128)(2,1)} %get-tuple-element.105.refs_1_), custom_call_target="tpu_custom_call" | custom-call | flops 5368709120 | bytes 20971520 | tf_op jit(solution)/shard_map/pallas_call | solution.py:693
  269.2 3.4 dynamic-slice_bitcast_fusion.1
  272.6 53.6 %shard_map.252 = (bf16[1200,1024]{1,0:T(8,128)(2,1)}, bf16[400,1024]{1,0:T(8,128)(2,1)}, bf16[1024,1024]{1,0:T(8,128)(2,1)}, bf16[1024,1024]{1,0:T(8,128)(2,1)},...) custom-call(bf16[1600,1024]{1,0:T(8,128)(2,1)} %get-tuple-element.88.refs_0_, ...), custom_call_target="tpu_custom_call" | custom-call | flops 12884901888 | bytes 52428800 | tf_op jit(solution)/shard_map/pallas_call | solution.py:614
  326.3 1.8 add_convert_fusion.2
  328.1 2.1 collective-permute-start.18
  330.2 14.3 %shard_map.253 = bf16[1024,3712]{1,0:T(8,128)(2,1)} custom-call(bf16[1024,1024]{1,0:T(8,128)(2,1)} %refs_0_.1, bf16[1024,1024]{1,0:T(8,128)(2,1)} %get-tuple-element.100.refs_1_, bf16[16,1024]{1,0:T(8,128)(2,1)} %get-tuple-element.101.refs_2_, bf16[1024,2560]{1,0:T(8,128)(2,1)} %get-tuple-element.102.refs_3_, bf16[1024,128]{1,0:T(8,128)(2,1)} %get-tuple-element.103.refs_4_, ...), custom_call_target="tpu_custom_call" | custom-call | flops 7784628224 | bytes 20971520 | tf_op jit(solution)/shard_map/pallas_call | solution.py:693
  344.6 4.3 dynamic-slice_bitcast_fusion
  348.9 1.9 collective-permute-done.18
  352.1 3.6 constant_dynamic-update-slice_fusion.3
  356.7 2.5 collective-permute-start.21
  359.2 18.0 %collective-permute-done.19 = bf16[400,1024]{1,0:T(8,128)(2,1)} collective-permute-done((bf16[400,1024]{1,0:T(8,128)(2,1)}, bf16[400,1024]{1,0:T(8,128)(2,1)}, u32[]{:S(2)}, u32[]{:S(2)}) %collective-permute-start.19) | collective-permute-done | bytes 819232 | tf_op jit(solution)/shard_map/ppermute | solution.py:939
  378.4 14.7 %collective-permute-done.20 = bf16[400,1024]{1,0:T(8,128)(2,1)} collective-permute-done((bf16[400,1024]{1,0:T(8,128)(2,1)}, bf16[400,1024]{1,0:T(8,128)(2,1)}, u32[]{:S(2)}, u32[]{:S(2)}) %collective-permute-start.20) | collective-permute-done | bytes 819232 | tf_op jit(solution)/shard_map/ppermute | solution.py:939
  395.5 3.6 convert_element_type.246
  399.7 3.6 fusion.35
  403.3 3.7 copy.67
  408.2 3.5 fusion.3
  412.1 3.0 collective-permute-start.11
  415.4 3.0 fusion
  418.6 1.8 collective-permute-start.2
  420.7 21.3 %collective-permute-done.10 = bf16[128,2560]{1,0:T(8,128)(2,1)S(1)} collective-permute-done((bf16[128,2560]{1,0:T(8,128)(2,1)S(1)}, bf16[128,2560]{1,0:T(8,128)(2,1)S(1)}, u32[]{:S(2)}, u32[]{:S(2)}) %collective-permute-start.10) | collective-permute-done | bytes 655392 | tf_op jit(solution)/shard_map/ppermute | solution.py:939
  443.2 1.9 collective-permute-done.9
  445.5 2.2 collective-permute-start.12
  447.7 3.4 collective-permute-start.13
  451.1 14.3 %collective-permute-done.2 = bf16[128,3712]{1,0:T(8,128)(2,1)S(1)} collective-permute-done((bf16[128,3712]{1,0:T(8,128)(2,1)S(1)}, bf16[128,3712]{1,0:T(8,128)(2,1)S(1)}, u32[]{:S(2)}, u32[]{:S(2)}) %collective-permute-start.2) | collective-permute-done | bytes 950304 | tf_op jit(solution)/shard_map/ppermute | solution.py:939
  465.4 3.2 collective-permute-start.14
  468.7 14.0 %collective-permute-done.4 = bf16[128,3712]{1,0:T(8,128)(2,1)S(1)} collective-permute-done((bf16[128,3712]{1,0:T(8,128)(2,1)S(1)}, bf16[128,3712]{1,0:T(8,128)(2,1)S(1)}, u32[]{:S(2)}, u32[]{:S(2)}) %collective-permute-start.4) | collective-permute-done | bytes 950304 | tf_op jit(solution)/shard_map/ppermute | solution.py:939
  483.3 2.5 collective-permute-start.5
  485.8 2.8 collective-permute-start.6
  490.4 10.2 %collective-permute-done.5 = bf16[32,3712]{1,0:T(8,128)(2,1)S(1)} collective-permute-done((bf16[32,3712]{1,0:T(8,128)(2,1)S(1)}, bf16[32,3712]{1,0:T(8,128)(2,1)S(1)}, u32[]{:S(2)}, u32[]{:S(2)}) %collective-permute-start.5) | collective-permute-done | bytes 237600 | tf_op jit(solution)/shard_map/ppermute | solution.py:933
  500.6 2.5 collective-permute-done.6
  503.2 2.5 collective-permute-done.7
  508.6 1.3 copy.79
  (105 shorter events, 26.4 us)
Async XLA Ops:
  0.6 6.1 %copy-start.5 = (bf16[1024,512]{1,0:T(8,128)(2,1)S(1)}, bf16[1024,512]{1,0:T(8,128)(2,1)}, u32[]{:S(2)}) copy-start(bf16[1024,512]{1,0:T(8,128)(2,1)} %param.25) | copy-start | bytes 3145732
  1.9 63.6 %collective-permute-start = (bf16[1024,48]{0,1:T(8,128)(2,1)S(1)}, bf16[1024,48]{0,1:T(8,128)(2,1)S(1)}, u32[]{:S(2)}, u32[]{:S(2)}) collective-permute-start(bf16[1024,48]{0,1:T(8,128)(2,1)S(1)} %fusion.7), channel_id=1, source_target_pairs={{0,1},{1,0},{2,3},{3,2},{4,5},{5,4},{6,7},{7,6},{8,9},{9,8},{10,11... | collective-permute-start | bytes 294920 | tf_op jit(solution)/shard_map/ppermute | solution.py:927
  4.9 2.8 copy-start.10
  4.9 3.2 copy-start.9
  11.7 4.3 copy-start.11
  14.0 2.0 copy-start.4
  250.1 6.4 %copy-start = (bf16[1200,1024]{1,0:T(8,128)(2,1)S(1)}, bf16[1200,1024]{1,0:T(8,128)(2,1)}, u32[]{:S(2)}) copy-start(bf16[1200,1024]{1,0:T(8,128)(2,1)} %get-tuple-element.89) | copy-start | bytes 7372804
  253.0 73.2 %collective-permute-start.15 = (bf16[400,1024]{1,0:T(8,128)(2,1)}, bf16[400,1024]{1,0:T(8,128)(2,1)S(1)}, u32[]{:S(2)}, u32[]{:S(2)}) collective-permute-start(bf16[400,1024]{1,0:T(8,128)(2,1)} %get-tuple-element.167), channel_id=1, source_target_pairs={{0,8},{8,0},{16,24},{24,16},{1,9},{9,1},{17,25},{25,17},{2,10},{10... | collective-permute-start | bytes 2457608 | tf_op jit(solution)/shard_map/ppermute | solution.py:939
  253.6 72.7 %collective-permute-start.16 = (bf16[400,1024]{1,0:T(8,128)(2,1)S(1)}, bf16[400,1024]{1,0:T(8,128)(2,1)S(1)}, u32[]{:S(2)}, u32[]{:S(2)}) collective-permute-start(bf16[400,1024]{1,0:T(8,128)(2,1)S(1)} %get-tuple-element.169), channel_id=1, source_target_pairs={{0,16},{8,24},{16,0},{24,8},{1,17},{9,25},{17,1},{25,9},{2,18},{10... | collective-permute-start | bytes 2457608 | tf_op jit(solution)/shard_map/ppermute | solution.py:939
  255.1 71.1 %collective-permute-start.17 = (bf16[400,1024]{1,0:T(8,128)(2,1)S(1)}, bf16[400,1024]{1,0:T(8,128)(2,1)S(1)}, u32[]{:S(2)}, u32[]{:S(2)}) collective-permute-start(bf16[400,1024]{1,0:T(8,128)(2,1)S(1)} %get-tuple-element.168), channel_id=1, source_target_pairs={{0,24},{8,16},{16,8},{24,0},{1,25},{9,17},{17,9},{25,1},{2,26},{10... | collective-permute-start | bytes 2457608 | tf_op jit(solution)/shard_map/ppermute | solution.py:939
  272.6 135.6 %collective-permute-start.8 = (bf16[16,32,2560]{2,1,0:T(8,128)(2,1)}, bf16[16,32,2560]{2,1,0:T(8,128)(2,1)}, u32[]{:S(2)}, u32[]{:S(2)}) collective-permute-start(bf16[16,32,2560]{2,1,0:T(8,128)(2,1)} %dynamic-slice_bitcast_fusion.1), channel_id=1, source_target_pairs={{0,1},{1,0},{2,3},{3,2},{4,5},{5,4},{6,7},{7,6},{8,9},{9,8},{10,11... | collective-permute-start | bytes 7864328 | tf_op jit(solution)/shard_map/ppermute | solution.py:927
  328.1 22.7 %collective-permute-start.18 = (bf16[400,1024]{1,0:T(8,128)(2,1)S(1)}, bf16[400,1024]{1,0:T(8,128)(2,1)S(1)}, u32[]{:S(2)}, u32[]{:S(2)}) collective-permute-start(bf16[400,1024]{1,0:T(8,128)(2,1)S(1)} %add_convert_fusion.2), channel_id=1, source_target_pairs={{0,2},{1,3},{2,4},{3,5},{4,6},{5,7},{6,0},{7,1},{8,10},{9,11},{10,... | collective-permute-start | bytes 2457608 | tf_op jit(solution)/shard_map/ppermute | solution.py:933
  344.6 7.5 %copy-start.7 = (bf16[400,1024]{1,0:T(8,128)(2,1)S(1)}, bf16[400,1024]{1,0:T(8,128)(2,1)}, u32[]{:S(2)}) copy-start(bf16[400,1024]{1,0:T(8,128)(2,1)} %get-tuple-element.108) | copy-start | bytes 2457604
  348.9 3.2 copy-start.1
  348.9 3.2 copy-start.6
  348.9 66.5 %collective-permute-start.1 = (bf16[16,32,3712]{2,1,0:T(8,128)(2,1)}, bf16[16,32,3712]{2,1,0:T(8,128)(2,1)}, u32[]{:S(2)}, u32[]{:S(2)}) collective-permute-start(bf16[16,32,3712]{2,1,0:T(8,128)(2,1)} %dynamic-slice_bitcast_fusion), channel_id=1, source_target_pairs={{0,1},{1,0},{2,3},{3,2},{4,5},{5,4},{6,7},{7,6},{8,9},{9,8},{10,11... | collective-permute-start | bytes 11403272 | tf_op jit(solution)/shard_map/ppermute | solution.py:927
  350.8 0.9 copy-start.8
  355.7 21.5 %collective-permute-start.19 = (bf16[400,1024]{1,0:T(8,128)(2,1)}, bf16[400,1024]{1,0:T(8,128)(2,1)}, u32[]{:S(2)}, u32[]{:S(2)}) collective-permute-start(bf16[400,1024]{1,0:T(8,128)(2,1)} %get-tuple-element.159), channel_id=1, source_target_pairs={{0,8},{8,0},{16,24},{24,16},{1,9},{9,1},{17,25},{25,17},{2,10},{10... | collective-permute-start | bytes 2457608 | tf_op jit(solution)/shard_map/ppermute | solution.py:939
  356.0 37.1 %collective-permute-start.20 = (bf16[400,1024]{1,0:T(8,128)(2,1)}, bf16[400,1024]{1,0:T(8,128)(2,1)}, u32[]{:S(2)}, u32[]{:S(2)}) collective-permute-start(bf16[400,1024]{1,0:T(8,128)(2,1)} %get-tuple-element.159), channel_id=1, source_target_pairs={{0,16},{8,24},{16,0},{24,8},{1,17},{9,25},{17,1},{25,9},{2,18},{10... | collective-permute-start | bytes 2457608 | tf_op jit(solution)/shard_map/ppermute | solution.py:939
  356.7 37.6 %collective-permute-start.21 = (bf16[400,1024]{1,0:T(8,128)(2,1)}, bf16[400,1024]{1,0:T(8,128)(2,1)}, u32[]{:S(2)}, u32[]{:S(2)}) collective-permute-start(bf16[400,1024]{1,0:T(8,128)(2,1)} %get-tuple-element.159), channel_id=1, source_target_pairs={{0,24},{8,16},{16,8},{24,0},{1,25},{9,17},{17,9},{25,1},{2,26},{10... | collective-permute-start | bytes 2457608 | tf_op jit(solution)/shard_map/ppermute | solution.py:939
  403.3 4.4 copy-start.12
  403.3 12.1 %slice-start = ((s8[7602176]{0:T(1024)(128)(4,1)}), s8[3407872]{0:T(1024)(128)(4,1)S(1)}, s32[]{:S(2)}) async-start(s8[7602176]{0:T(1024)(128)(4,1)} %bitcast.49), calls=%async_computation | async-start | bytes 6815744
  408.2 7.2 %slice-start.1 = ((s8[7602176]{0:T(1024)(128)(4,1)}), s8[4194304]{0:T(1024)(128)(4,1)S(1)}, s32[]{:S(2)}) async-start(s8[7602176]{0:T(1024)(128)(4,1)} %bitcast.49), calls=%async_computation.1 | async-start | bytes 8388608
  411.8 30.2 %collective-permute-start.10 = (bf16[128,2560]{1,0:T(8,128)(2,1)S(1)}, bf16[128,2560]{1,0:T(8,128)(2,1)S(1)}, u32[]{:S(2)}, u32[]{:S(2)}) collective-permute-start(bf16[128,2560]{1,0:T(8,128)(2,1)S(1)} %get-tuple-element.172), channel_id=1, source_target_pairs={{0,16},{8,24},{16,0},{24,8},{1,17},{9,25},{17,1},{25,9},{2,18},{10... | collective-permute-start | bytes 1966088 | tf_op jit(solution)/shard_map/ppermute | solution.py:939
  412.1 31.0 %collective-permute-start.11 = (bf16[128,2560]{1,0:T(8,128)(2,1)S(1)}, bf16[128,2560]{1,0:T(8,128)(2,1)S(1)}, u32[]{:S(2)}, u32[]{:S(2)}) collective-permute-start(bf16[128,2560]{1,0:T(8,128)(2,1)S(1)} %get-tuple-element.171), channel_id=1, source_target_pairs={{0,24},{8,16},{16,8},{24,0},{1,25},{9,17},{17,9},{25,1},{2,26},{10... | collective-permute-start | bytes 1966088 | tf_op jit(solution)/shard_map/ppermute | solution.py:939
  415.1 30.0 %collective-permute-start.9 = (bf16[128,2560]{1,0:T(8,128)(2,1)S(1)}, bf16[128,2560]{1,0:T(8,128)(2,1)S(1)}, u32[]{:S(2)}, u32[]{:S(2)}) collective-permute-start(bf16[128,2560]{1,0:T(8,128)(2,1)S(1)} %get-tuple-element.170), channel_id=1, source_target_pairs={{0,8},{8,0},{16,24},{24,16},{1,9},{9,1},{17,25},{25,17},{2,10},{10... | collective-permute-start | bytes 1966088 | tf_op jit(solution)/shard_map/ppermute | solution.py:939
  418.6 46.9 %collective-permute-start.2 = (bf16[128,3712]{1,0:T(8,128)(2,1)S(1)}, bf16[128,3712]{1,0:T(8,128)(2,1)S(1)}, u32[]{:S(2)}, u32[]{:S(2)}) collective-permute-start(bf16[128,3712]{1,0:T(8,128)(2,1)S(1)} %get-tuple-element.162), channel_id=1, source_target_pairs={{0,8},{8,0},{16,24},{24,16},{1,9},{9,1},{17,25},{25,17},{2,10},{10... | collective-permute-start | bytes 2850824 | tf_op jit(solution)/shard_map/ppermute | solution.py:939
  420.4 48.3 %collective-permute-start.3 = (bf16[128,3712]{1,0:T(8,128)(2,1)S(1)}, bf16[128,3712]{1,0:T(8,128)(2,1)S(1)}, u32[]{:S(2)}, u32[]{:S(2)}) collective-permute-start(bf16[128,3712]{1,0:T(8,128)(2,1)S(1)} %get-tuple-element.164), channel_id=1, source_target_pairs={{0,16},{8,24},{16,0},{24,8},{1,17},{9,25},{17,1},{25,9},{2,18},{10... | collective-permute-start | bytes 2850824 | tf_op jit(solution)/shard_map/ppermute | solution.py:939
  442.0 40.6 %collective-permute-start.4 = (bf16[128,3712]{1,0:T(8,128)(2,1)S(1)}, bf16[128,3712]{1,0:T(8,128)(2,1)S(1)}, u32[]{:S(2)}, u32[]{:S(2)}) collective-permute-start(bf16[128,3712]{1,0:T(8,128)(2,1)S(1)} %get-tuple-element.163), channel_id=1, source_target_pairs={{0,24},{8,16},{16,8},{24,0},{1,25},{9,17},{17,9},{25,1},{2,26},{10... | collective-permute-start | bytes 2850824 | tf_op jit(solution)/shard_map/ppermute | solution.py:939
  445.5 43.1 %collective-permute-start.12 = (bf16[32,2560]{1,0:T(8,128)(2,1)S(1)}, bf16[32,2560]{1,0:T(8,128)(2,1)S(1)}, u32[]{:S(2)}, u32[]{:S(2)}) collective-permute-start(bf16[32,2560]{1,0:T(8,128)(2,1)S(1)} %get-tuple-element.176), channel_id=1, source_target_pairs={{0,2},{1,3},{2,4},{3,5},{4,6},{5,7},{6,0},{7,1},{8,10},{9,11},{10,... | collective-permute-start | bytes 491528 | tf_op jit(solution)/shard_map/ppermute | solution.py:933
  447.7 42.0 %collective-permute-start.13 = (bf16[32,2560]{1,0:T(8,128)(2,1)S(1)}, bf16[32,2560]{1,0:T(8,128)(2,1)S(1)}, u32[]{:S(2)}, u32[]{:S(2)}) collective-permute-start(bf16[32,2560]{1,0:T(8,128)(2,1)S(1)} %get-tuple-element.178), channel_id=1, source_target_pairs={{0,4},{1,5},{2,6},{3,7},{4,0},{5,1},{6,2},{7,3},{8,12},{9,13},{10,... | collective-permute-start | bytes 491528 | tf_op jit(solution)/shard_map/ppermute | solution.py:933
  465.4 24.2 %collective-permute-start.14 = (bf16[32,2560]{1,0:T(8,128)(2,1)S(1)}, bf16[32,2560]{1,0:T(8,128)(2,1)S(1)}, u32[]{:S(2)}, u32[]{:S(2)}) collective-permute-start(bf16[32,2560]{1,0:T(8,128)(2,1)S(1)} %get-tuple-element.177), channel_id=1, source_target_pairs={{0,6},{1,7},{2,0},{3,1},{4,2},{5,3},{6,4},{7,5},{8,14},{9,15},{10,... | collective-permute-start | bytes 491528 | tf_op jit(solution)/shard_map/ppermute | solution.py:933
  483.2 25.4 %copy-start.2 = (bf16[1024,1024]{1,0:T(8,128)(2,1)S(1)}, bf16[1024,1024]{1,0:T(8,128)(2,1)}, u32[]{:S(2)}) copy-start(bf16[1024,1024]{1,0:T(8,128)(2,1)} %get-tuple-element.199) | copy-start | bytes 6291460
  483.3 17.3 %collective-permute-start.5 = (bf16[32,3712]{1,0:T(8,128)(2,1)S(1)}, bf16[32,3712]{1,0:T(8,128)(2,1)S(1)}, u32[]{:S(2)}, u32[]{:S(2)}) collective-permute-start(bf16[32,3712]{1,0:T(8,128)(2,1)S(1)} %get-tuple-element.173), channel_id=1, source_target_pairs={{0,2},{1,3},{2,4},{3,5},{4,6},{5,7},{6,0},{7,1},{8,10},{9,11},{10,... | collective-permute-start | bytes 712712 | tf_op jit(solution)/shard_map/ppermute | solution.py:933
  485.8 17.4 %collective-permute-start.6 = (bf16[32,3712]{1,0:T(8,128)(2,1)S(1)}, bf16[32,3712]{1,0:T(8,128)(2,1)S(1)}, u32[]{:S(2)}, u32[]{:S(2)}) collective-permute-start(bf16[32,3712]{1,0:T(8,128)(2,1)S(1)} %get-tuple-element.175), channel_id=1, source_target_pairs={{0,4},{1,5},{2,6},{3,7},{4,0},{5,1},{6,2},{7,3},{8,12},{9,13},{10,... | collective-permute-start | bytes 712712 | tf_op jit(solution)/shard_map/ppermute | solution.py:933
  488.6 17.1 %collective-permute-start.7 = (bf16[32,3712]{1,0:T(8,128)(2,1)S(1)}, bf16[32,3712]{1,0:T(8,128)(2,1)S(1)}, u32[]{:S(2)}, u32[]{:S(2)}) collective-permute-start(bf16[32,3712]{1,0:T(8,128)(2,1)S(1)} %get-tuple-element.174), channel_id=1, source_target_pairs={{0,6},{1,7},{2,0},{3,1},{4,2},{5,3},{6,4},{7,5},{8,14},{9,15},{10,... | collective-permute-start | bytes 712712 | tf_op jit(solution)/shard_map/ppermute | solution.py:933
  505.8 4.0 copy-start.3

commit v4 on v3

--- a/solution.py
+++ b/solution.py
@@ -193,26 +193,12 @@
     return lambda mine, flipped: mine * rows
 
 
-def far_part(rows):
-    return lambda mine, flipped: flipped * rows
-
-
 def fixed(start):
     return lambda mine, flipped: start
 
 
 def shift_move(src, dst, hop, src_at, dst_at, count):
     return [(src, dst, "chip", hop, src_at, dst_at, count)]
-
-
-def gather_moves(buf_in, buf_out, rows):
-    return [(buf_in, buf_out, "dp", flip, own_part(rows), own_part(rows), rows) for flip in (1, 2, 3)]
-
-
-def scatter_moves(src, dst, rows):
-    return [
-        (src, dst, "dp", flip, far_part(rows), fixed((flip - 1) * rows), rows) for flip in (1, 2, 3)
-    ]
 
 
 def greet(peers):
@@ -256,7 +242,182 @@
     return pl.ds(pl.multiple_of(index * tile, tile), tile)
 
 
-def forward_body(heads, tile, steps, *refs):
+def flips():
+    mine = lax.axis_index("dp")
+    return [mine, mine + 1 - 2 * lax.rem(mine, 2), lax.rem(mine + 2, 4), 3 - mine]
+
+
+def remote(src, dst, sems, index, peer):
+    return pltpu.make_async_remote_copy(
+        src_ref=src,
+        dst_ref=dst,
+        send_sem=sems.at[0, index],
+        recv_sem=sems.at[1, index],
+        device_id=peer,
+        device_id_type=pl.DeviceIdType.MESH,
+    )
+
+
+def span(start, count):
+    return pl.ds(pl.multiple_of(start, 16), count)
+
+
+def halving_first(source, near, far, part, cut, sems, at):
+    dp = flips()
+    low = part - cut
+    copies = []
+    for slot, owner in enumerate((1, 3)):
+        copies.append(
+            remote(
+                source.at[span(dp[owner] * part, cut)],
+                near.at[pl.ds(slot * cut, cut)],
+                sems,
+                at + slot,
+                neighbour("dp", 1),
+            )
+        )
+    for slot, owner in enumerate((2, 3)):
+        copies.append(
+            remote(
+                source.at[span(dp[owner] * part + cut, low)],
+                far.at[pl.ds(slot * low, low)],
+                sems,
+                at + 2 + slot,
+                neighbour("dp", 2),
+            )
+        )
+    return copies
+
+
+def halving_second(send, land, part, cut, sems, at):
+    low = part - cut
+    return [
+        remote(send.at[pl.ds(0, cut)], land.at[pl.ds(0, cut)], sems, at, neighbour("dp", 2)),
+        remote(send.at[pl.ds(cut, low)], land.at[pl.ds(cut, low)], sems, at + 1, neighbour("dp", 1)),
+    ]
+
+
+def as_f32(ref, start, count):
+    return ref[pl.ds(start, count), :].astype(jnp.float32)
+
+
+def spread_first(source, target, part, cut, sems, at):
+    mine = lax.axis_index("dp")
+    return [
+        remote(
+            source.at[pl.ds(0, cut)],
+            target.at[span(mine * part, cut)],
+            sems,
+            at,
+            neighbour("dp", 1),
+        ),
+        remote(
+            source.at[pl.ds(cut, part - cut)],
+            target.at[span(mine * part + cut, part - cut)],
+            sems,
+            at + 1,
+            neighbour("dp", 2),
+        ),
+    ]
+
+
+def spread_second(source, target, part, cut, sems, at):
+    dp = flips()
+    low = part - cut
+    mine_up, mine_down = span(dp[0] * part, cut), span(dp[0] * part + cut, low)
+    got_up, got_down = span(dp[1] * part, cut), span(dp[2] * part + cut, low)
+    return [
+        remote(source.at[pl.ds(0, cut)], target.at[mine_up], sems, at, neighbour("dp", 2)),
+        remote(target.at[got_up], target.at[got_up], sems, at + 1, neighbour("dp", 2)),
+        remote(source.at[pl.ds(cut, low)], target.at[mine_down], sems, at + 2, neighbour("dp", 1)),
+        remote(target.at[got_down], target.at[got_down], sems, at + 3, neighbour("dp", 1)),
+    ]
+
+
+def load_own(source, own, part, cut, sems):
+    dp = flips()
+    low = part - cut
+    return [
+        pltpu.make_async_copy(
+            source.at[span(dp[owner] * part + start, count)], own.at[pl.ds(at, count)], sems.at[i]
+        )
+        for i, (owner, start, count, at) in enumerate(
+            [(0, 0, cut, 0), (2, 0, cut, cut), (0, cut, low, 2 * cut), (1, cut, low, 2 * cut + low)]
+        )
+    ]
+
+
+class Halving:
+    def __init__(self, source, total, buffers, part, cut):
+        own, near, far, send, land, load_sems, sems = buffers
+        self.source, self.total, self.part, self.cut = source, total, part, cut
+        self.own, self.near, self.far, self.send, self.land = own, near, far, send, land
+        self.loads = load_own(source, own, part, cut, load_sems)
+        self.first = halving_first(source, near, far, part, cut, sems, 0)
+        self.second = halving_second(send, land, part, cut, sems, 4)
+
+    def start(self):
+        for copy in self.first + self.loads:
+            copy.start()
+
+    def turn(self):
+        part, cut = self.part, self.cut
+        low = part - cut
+        for copy in self.first + self.loads:
+            copy.wait()
+        up = as_f32(self.own, cut, cut) + as_f32(self.near, cut, cut)
+        down = as_f32(self.own, 2 * cut + low, low) + as_f32(self.far, low, low)
+        self.send[:cut, :] = up.astype(jnp.bfloat16)
+        self.send[cut:, :] = down.astype(jnp.bfloat16)
+        for copy in self.second:
+            copy.start()
+
+    def finish(self):
+        part, cut = self.part, self.cut
+        low = part - cut
+        for copy in self.second:
+            copy.wait()
+        up = as_f32(self.own, 0, cut) + as_f32(self.near, 0, cut) + as_f32(self.land, 0, cut)
+        down = as_f32(self.own, 2 * cut, low) + as_f32(self.far, 0, low) + as_f32(self.land, cut, low)
+        self.total[:cut, :] = up.astype(jnp.bfloat16)
+        self.total[cut:, :] = down.astype(jnp.bfloat16)
+
+
+def halving_buffers(part, cut, model):
+    bf16 = lambda rows: pltpu.VMEM((rows, model), jnp.bfloat16)
+    return [
+        bf16(2 * part),
+        bf16(2 * cut),
+        bf16(2 * (part - cut)),
+        bf16(part),
+        bf16(part),
+        pltpu.SemaphoreType.DMA((4,)),
+        pltpu.SemaphoreType.DMA((2, 6)),
+    ]
+
+
+class Spreading:
+    def __init__(self, target, part, cut, sems):
+        mine = target.at[span(lax.axis_index("dp") * part, part)]
+        self.first = spread_first(mine, target, part, cut, sems, 0)
+        self.second = spread_second(mine, target, part, cut, sems, 2)
+
+    def start(self):
+        for copy in self.first:
+            copy.start()
+
+    def turn(self):
+        for copy in self.first:
+            copy.wait()
+        for copy in self.second:
+            copy.start()
+
+    def finish(self):
+        for copy in self.second:
+            copy.wait()
+
+
+def forward_body(heads, tile, steps, ahead, *refs):
     (
         own_any,
         cot_any,
@@ -272,6 +433,7 @@
         wval_ref,
         wout_ref,
         chunk_any,
+        near_any,
         cot_far_any,
         sent_far_any,
         hid_ref,
@@ -293,10 +455,11 @@
     step = pl.program_id(0)
     rows = steps * tile
     quarter = own_any.shape[0] // 4
-    moves = shift_move(0, 0, -2, own_part(quarter), own_part(quarter), quarter)
-    moves = moves + [(1, 1, "core", 1, fixed(0), fixed(0), rows)]
+    moves = shift_move(0, 0, -3, own_part(quarter), own_part(quarter), quarter)
+    moves = moves + shift_move(0, 1, -1, fixed(0), fixed(0), ahead)
+    moves = moves + [(1, 2, "core", 1, fixed(0), fixed(0), rows)]
     partner = neighbour("core", 1)
-    copies = copies_of(moves, [own_any, cot_any], [chunk_any, cot_far_any], send_sem, recv_sem)
+    copies = copies_of(moves, [own_any, cot_any], [chunk_any, near_any, cot_far_any], send_sem, recv_sem)
 
     def tile_copy(index):
         return pltpu.make_async_remote_copy(
@@ -388,7 +551,7 @@
     return pl.BlockSpec(shape, lambda step: (0,) * len(shape), pipeline_mode=pl.Buffered(1))
 
 
-def attention_forward(own, cot, x, start, keep, cos_two, sin_two, mask, gain, wqk, wsel, wval, wout, tile):
+def attention_forward(ahead, own, cot, x, start, keep, cos_two, sin_two, mask, gain, wqk, wsel, wval, wout, tile):
     rows, model = x.shape
     heads = wqk.shape[1] // (2 * DH)
     per_tile = lambda width: pl.BlockSpec((tile, width), lambda step: (step, 0))
@@ -408,7 +571,7 @@
         (model, jnp.bfloat16, True),
     ]
     return pl.pallas_call(
-        functools.partial(forward_body, heads, tile, rows // tile),
+        functools.partial(forward_body, heads, tile, rows // tile, ahead),
         grid=(rows // tile,),
         in_specs=[
             ANYWHERE,
@@ -425,17 +588,18 @@
             full(wval),
             full(wout),
         ],
-        out_specs=[ANYWHERE] * 3
+        out_specs=[ANYWHERE] * 4
         + [whole_block((rows, width)) if whole else per_tile(width) for width, _, whole in shapes],
         out_shape=[
+            jax.ShapeDtypeStruct(own.shape, jnp.bfloat16),
             jax.ShapeDtypeStruct(own.shape, jnp.bfloat16),
             jax.ShapeDtypeStruct((rows, model), jnp.bfloat16),
             jax.ShapeDtypeStruct((rows, model), jnp.bfloat16),
         ]
         + [jax.ShapeDtypeStruct((rows, width), kind) for width, kind, _ in shapes],
         scratch_shapes=[
-            pltpu.SemaphoreType.DMA((2,)),
-            pltpu.SemaphoreType.DMA((2,)),
+            pltpu.SemaphoreType.DMA((3,)),
+            pltpu.SemaphoreType.DMA((3,)),
             pltpu.SemaphoreType.DMA((rows // tile,)),
             pltpu.SemaphoreType.DMA((rows // tile,)),
         ],
@@ -448,7 +612,7 @@
     )(own, cot, x, start, keep, cos_two, sin_two, mask, gain, wqk, wsel, wval, wout)
 
 
-def backward_body(heads, tile, steps, moves, n_in, n_out, *refs):
+def backward_body(heads, tile, steps, moves, halve, part, n_in, n_out, *refs):
     ins, refs = refs[:n_in], refs[n_in:]
     (
         dy_ref,
@@ -484,6 +648,10 @@
         dval_ref,
         dlog_ref,
         ggain_ref,
+        *totals_and_rest,
+    ) = rest
+    totals, rest = totals_and_rest[: len(halve)], totals_and_rest[len(halve) :]
+    (
         dk_acc,
         dv_acc,
         dq_keep,
@@ -491,15 +659,26 @@
         gain_acc,
         send_sem,
         recv_sem,
+        *buffers,
     ) = rest
     step = pl.program_id(0)
     copies = copies_of(moves, ins, outs, send_sem, recv_sem)
+    riders = [
+        Halving(ins[source], totals[i], buffers[7 * i : 7 * i + 7], part, part // 32 * 16)
+        for i, source in enumerate(halve)
+    ]
 
     @pl.when(step == 0)
     def _():
-        greet(peers_of(moves))
+        greet(peers_of(moves) + [neighbour("dp", 1), neighbour("dp", 2)])
         for copy in copies:
             copy.start()
+        for rider in riders:
+            rider.start()
+
+    @pl.when(step == steps - 1)
+    def _():
+        riders[0].turn()
 
     slot = lax.rem(step, 2)
     old = 1 - slot
@@ -597,12 +776,16 @@
         row = lax.broadcasted_iota(jnp.int32, (GAIN_ROWS, gain.shape[1]), 0)
         split = jnp.where(row == 0, high, jnp.where(row == 1, gain - high, 0.0))
         ggain_ref[...] = split.astype(jnp.bfloat16)
+        for rider in riders[1:]:
+            rider.turn()
+        for rider in riders:
+            rider.finish()
         for copy in copies:
             copy.wait()
 
 
 def attention_backward(
-    sources, results, moves, dy, q, k, v, att, lse, start, keep, sig, mask, cos_two, sin_two, x, val, dhid, gain, wqk, wsel, wval, wout, tile
+    sources, results, moves, halve, part, dy, q, k, v, att, lse, start, keep, sig, mask, cos_two, sin_two, x, val, dhid, gain, wqk, wsel, wval, wout, tile
 ):
     rows, model = x.shape
     heads = wqk.shape[1] // (2 * DH)
@@ -612,7 +795,9 @@
     at_old = lambda width: pl.BlockSpec((tile, width), lambda step: (jnp.maximum(step - 1, 0), 0))
     full = lambda arr: whole_block(arr.shape)
     return pl.pallas_call(
-        functools.partial(backward_body, heads, tile, steps, moves, len(sources), len(results)),
+        functools.partial(
+            backward_body, heads, tile, steps, moves, halve, part, len(sources), len(results)
+        ),
         grid=(steps + 1,),
         in_specs=[ANYWHERE] * len(sources)
         + [
@@ -648,7 +833,8 @@
             at_old(wide),
             at_old(LANE),
             whole_block((GAIN_ROWS, model)),
-        ],
+        ]
+        + [whole_block((part, model))] * len(halve),
         out_shape=[jax.ShapeDtypeStruct(shape, jnp.bfloat16) for shape in results]
         + [
             jax.ShapeDtypeStruct((rows, model), jnp.bfloat16),
@@ -656,7 +842,8 @@
             jax.ShapeDtypeStruct((rows, wide), jnp.bfloat16),
             jax.ShapeDtypeStruct((rows, LANE), jnp.bfloat16),
             jax.ShapeDtypeStruct((GAIN_ROWS, model), jnp.bfloat16),
-        ],
+        ]
+        + [jax.ShapeDtypeStruct((part, model), jnp.bfloat16)] * len(halve),
         scratch_shapes=[
             pltpu.VMEM((2, tile, narrow), jnp.float32),
             pltpu.VMEM((2, tile, narrow), jnp.float32),
@@ -665,7 +852,8 @@
             pltpu.VMEM((1, model), jnp.float32),
             pltpu.SemaphoreType.DMA((len(moves),)),
             pltpu.SemaphoreType.DMA((len(moves),)),
-        ],
+        ]
+        + halving_buffers(part, part // 32 * 16, model) * len(halve),
         compiler_params=pltpu.CompilerParams(
             vmem_limit_bytes=VMEM_BYTES, collective_id=6, has_side_effects=True
         ),
@@ -678,37 +866,243 @@
     )
 
 
-def outer_body(groups, *refs):
-    out_ref = refs[-1]
-    at = 0
-    for pairs in groups:
-        total = sum(dot_tn(refs[left][...], refs[right][...]) for left, right in pairs)
-        out_ref[:, at : at + total.shape[1]] = total.astype(jnp.bfloat16)
-        at += total.shape[1]
-
-
-def outer_products(arrays, groups, lefts, block):
-    rows, model = arrays[0].shape
-    width = sum(arrays[pairs[0][1]].shape[1] for pairs in groups)
+def tail_body(blocks, chips, part, cut, *refs):
+    (
+        part_1,
+        part_0,
+        got_2,
+        got_3,
+        dy_ref,
+        x_ref,
+        norm_ref,
+        gain_ref,
+        mix_ref,
+        dval_ref,
+        dlog_ref,
+        dqk_ref,
+        unit_ref,
+        dense_ref,
+        whole_any,
+        came,
+        quarter,
+        product,
+        pair,
+        near,
+        far,
+        send,
+        land,
+        sums,
+        last,
+        link,
+        core_sems,
+        xy_sems,
+        z_sems,
+        local_sem,
+    ) = refs
+    place = lax.axis_index("expert")
+    chip, core = place // 2, lax.rem(place, 2)
+    model = x_ref.shape[1]
+    piece = model // 4 // chips // 2
+    quart = chips * piece
+    halfway = quart // 2
+    rights = {"out": mix_ref, "val": dval_ref, "log": dlog_ref, "qk": dqk_ref}
+    lefts = {"out": dy_ref, "val": x_ref, "log": x_ref, "qk": norm_ref}
+
+    peers = [neighbour("core", 1)] + [neighbour("dp", flip) for flip in (1, 2)]
+    for hop in range(1, chips):
+        peers.append(neighbour("chip", hop))
+    greet(peers)
+    first = remote(part_1, came, link, 0, neighbour("chip", 1))
+    first.start()
+
+    def width_of(b):
+        return sum(hi - lo for _, lo, hi in blocks[b])
+
+    def core_copy(b):
+        width = width_of(b)
+        return remote(
+            product.at[b % 2, :, span((1 - core) * piece, piece), pl.ds(0, width)],
+            pair.at[b, :, :, pl.ds(0, width)],
+            core_sems,
+            b,
+            neighbour("core", 1),
+        )
+
+    def compute(b):
+        if b >= 2:
+            core_copy(b - 2).wait_send()
+        at = 0
+        for name, lo, hi in blocks[b]:
+            total = dot_tn(lefts[name][...], rights[name][:, lo:hi])
+            if name == "log":
+                total = total + dot_tn(gain_ref[...], unit_ref[...])
+            product[b % 2, :, :, at : at + hi - lo] = total.astype(jnp.bfloat16).reshape(
+                4 * chips, 2 * piece, hi - lo
+            )
+            at += hi - lo
+        core_copy(b).start()
+
+    def pair_rows(b):
+        return pair.at[b].reshape(4 * quart, pair.shape[3])
+
+    def first_copies(b):
+        return halving_first(pair_rows(b), near.at[b], far.at[b], quart, halfway, xy_sems.at[b], 0)
+
+    def second_copies(b):
+        return halving_second(send.at[b], land.at[b], quart, halfway, xy_sems.at[b], 4)
+
+    def chip_copies(b):
+        copies = []
+        for hop in range(1, chips):
+            target = lax.rem(chip + hop, chips)
+            copies.append(
+                remote(
+                    sums.at[b, span(target * piece, piece)],
+                    last.at[b, hop - 1],
+                    z_sems.at[b],
+                    hop - 1,
+                    neighbour("chip", hop),
+                )
+            )
+        return copies
+
+    def stage_1(b):
+        core_copy(b).wait_recv()
+        kept = product[b % 2, :, span(core * piece, piece), :].astype(jnp.float32)
+        pair[b] = (kept + pair[b].astype(jnp.float32)).astype(jnp.bfloat16)
+        for copy in first_copies(b):
+            copy.start()
+
+    def own_rows(b, owner, start):
+        return as_f32(pair_rows(b), pl.multiple_of(flips()[owner] * quart + start, 16), halfway)
+
+    def stage_2(b):
+        for copy in first_copies(b):
+            copy.wait()
+        send[b, :halfway, :] = (own_rows(b, 2, 0) + as_f32(near.at[b], halfway, halfway)).astype(
+            jnp.bfloat16
+        )
+        send[b, halfway:, :] = (own_rows(b, 1, halfway) + as_f32(far.at[b], halfway, halfway)).astype(
+            jnp.bfloat16
+        )
+        for copy in second_copies(b):
+            copy.start()
+
+    def stage_3(b):
+        for copy in second_copies(b):
+            copy.wait()
+        up = own_rows(b, 0, 0) + as_f32(near.at[b], 0, halfway) + as_f32(land.at[b], 0, halfway)
+        down = own_rows(b, 0, halfway) + as_f32(far.at[b], 0, halfway)
+        down = down + as_f32(land.at[b], halfway, halfway)
+        sums[b, :halfway, :] = up.astype(jnp.bfloat16)
+        sums[b, halfway:, :] = down.astype(jnp.bfloat16)
+        for copy in chip_copies(b):
+            copy.start()
+
+    def stage_4(b):
+        for copy in chip_copies(b):
+            copy.wait()
+        total = sums[b, span(chip * piece, piece), :].astype(jnp.float32)
+        for hop in range(chips - 1):
+            total = total + last[b, hop].astype(jnp.float32)
+        start = sum(width_of(i) for i in range(b))
+        dense_ref[:, start : start + width_of(b)] = total[:, : width_of(b)]
+
+    def spread_1():
+        return spread_first(quarter, whole_any, part, cut, link, 1)
+
+    def spread_2():
+        return spread_second(quarter, whole_any, part, cut, link, 3)
+
+    mine = lax.axis_index("dp")
+    keep = pltpu.make_async_copy(quarter, whole_any.at[span(mine * part, part)], local_sem)
+    count = len(blocks)
+    compute(0)
+    compute(1)
+    for b in range(count):
+        stage_1(b)
+        if b + 2 < count:
+            compute(b + 2)
+    first.wait()
+    quarter[...] = sum(
+        ref[...].astype(jnp.float32) for ref in (part_0, got_2, got_3, came)
+    ).astype(jnp.bfloat16)
+    keep.start()
+    for copy in spread_1():
+        copy.start()
+    for b in range(count):
+        stage_2(b)
+    for copy in spread_1():
+        copy.wait()
+    for copy in spread_2():
+        copy.start()
+    for b in range(count):
+        stage_3(b)
+    for b in range(count):
+        stage_4(b)
+    for copy in spread_2():
+        copy.wait()
+    keep.wait()
+    for b in range(max(0, count - 2), count):
+        core_copy(b).wait_send()
+
+
+def tail(part_1, part_0, got_2, got_3, dy, x, normed, gain_rows, mixed, dval, dlog, dqk, unit, shape, chips):
+    rows, model = x.shape
+    part = shape[0] // 4
+    cut = part // 32 * 16
+    wide, narrow = mixed.shape[1], dqk.shape[1]
+    half = wide // 2
+    blocks = [
+        [("out", 0, half)],
+        [("out", half, wide)],
+        [("val", 0, half)],
+        [("val", half, wide)],
+        [("log", 0, LANE), ("qk", 0, narrow)],
+    ]
+    width = max(half, LANE + narrow)
+    total = 2 * wide + LANE + narrow
+    count = len(blocks)
+    piece = model // 4 // chips // 2
+    quart = chips * piece
+    bf16 = lambda *shape: pltpu.VMEM(shape, jnp.bfloat16)
+    dma = lambda *shape: pltpu.SemaphoreType.DMA(shape)
+    vmem = pl.BlockSpec(memory_space=pltpu.VMEM)
     return pl.pallas_call(
-        functools.partial(outer_body, groups),
-        grid=(model // block,),
-        in_specs=[
-            pl.BlockSpec((arr.shape[0], block), lambda step: (0, step))
-            if i < lefts
-            else whole_block(arr.shape)
-            for i, arr in enumerate(arrays)
+        functools.partial(tail_body, blocks, chips, part, cut),
+        in_specs=[vmem] * 13,
+        out_specs=[vmem, ANYWHERE],
+        out_shape=[
+            jax.ShapeDtypeStruct((piece, total), jnp.float32),
+            jax.ShapeDtypeStruct(shape, jnp.bfloat16),
         ],
-        out_specs=pl.BlockSpec((block, width), lambda step: (step, 0)),
-        out_shape=jax.ShapeDtypeStruct((model, width), jnp.bfloat16),
-        compiler_params=pltpu.CompilerParams(vmem_limit_bytes=VMEM_BYTES),
+        scratch_shapes=[
+            bf16(part, model),
+            bf16(part, model),
+            bf16(2, 4 * chips, 2 * piece, width),
+            bf16(count, 4 * chips, piece, width),
+            bf16(count, quart, width),
+            bf16(count, quart, width),
+            bf16(count, quart, width),
+            bf16(count, quart, width),
+            bf16(count, quart, width),
+            bf16(count, chips - 1, piece, width),
+            dma(2, 7),
+            dma(2, count),
+            dma(count, 2, 6),
+            dma(count, 2, chips - 1),
+            dma(),
+        ],
+        compiler_params=pltpu.CompilerParams(
+            vmem_limit_bytes=VMEM_BYTES, collective_id=7, has_side_effects=True
+        ),
         cost_estimate=pl.CostEstimate(
-            flops=2 * rows * model * width, bytes_accessed=20 << 20, transcendentals=0
+            flops=2 * rows * model * total, bytes_accessed=20 << 20, transcendentals=0
         ),
-    )(*arrays)
-
-
-def expert_body(first, last, exp_local, ff_dim, tile, steps, moves, n_in, n_out, *refs):
+    )(part_1, part_0, got_2, got_3, dy, x, normed, gain_rows, mixed, dval, dlog, dqk, unit)
+
+
+def expert_body(first, last, exp_local, ff_dim, tile, steps, moves, spread, halve, n_in, n_out, *refs):
     ins, refs = refs[:n_in], refs[n_in:]
     x_own, x_far, c_own, c_far, w_ref, mask_ref, digit_ref = refs[:7]
     at = 7
@@ -721,8 +1115,12 @@
     outs = refs[at : at + n_out]
     at += n_out
     results = refs[at : at + 3]
-    g_ref = refs[at + 3 if last else at + 2]
-    at += 4 if last else 3
+    at += 3 if last else 2
+    if halve is not None:
+        total = refs[at]
+        at += 1
+    g_ref = refs[at]
+    at += 1
     act_all, dpre_all, x_ref, c_ref, load_sem, send_sem, recv_sem = refs[at : at + 7]
     wide = exp_local * ff_dim
     back = wide + ROUTER_ROWS
@@ -730,8 +1128,20 @@
     step = pl.program_id(0)
     copies = copies_of(moves, ins, outs, send_sem, recv_sem)
     peers = peers_of(moves)
+    at += 7
+    part = w_ref.shape[0] // 4
+    cut = part // 32 * 16
+    riders = []
+    if spread is not None:
+        riders.append((Spreading(outs[spread], part, cut, refs[at]), steps // 2 - 1))
+        at += 1
+    if halve is not None:
+        riders.append((Halving(ins[halve], total, refs[at : at + 7], part, cut), steps - 2))
+        at += 7
+    if riders:
+        peers += [neighbour("dp", 1), neighbour("dp", 2)]
     if last:
-        given, taken, tile_send, tile_recv = refs[at + 7 :]
+        given, taken, tile_send, tile_recv = refs[at:]
         partner = neighbour("core", 1)
         peers.append(partner)
 
@@ -762,11 +1172,16 @@
         greet(peers)
         for copy in copies:
             copy.start()
+        for rider, _ in riders:
+            rider.start()
 
     for turn in range(steps):
 
         @pl.when(step == turn)
         def _(turn=turn):
+            for rider, at_step in riders:
+                if at_step == turn:
+                    rider.turn()
             for kind in range(2):
                 load((turn + half) % steps if last else turn, kind).wait()
 
@@ -846,6 +1261,8 @@
         extra = dot_tn(dpre_all[:, wide:back], x_ref[...])
         g_ref[wide:back, :LANE] = (extra[:, :LANE] + digit_ref[...]).astype(jnp.bfloat16)
         g_ref[wide:back, LANE:] = extra[:, LANE:].astype(jnp.bfloat16)
+        for rider, _ in riders:
+            rider.finish()
         for copy in copies:
             copy.wait()
         if last:
@@ -855,7 +1272,7 @@
 
 
 def expert_chunk(
-    sources, results, aliases, moves, tokens, weights, masks, digits, hop, sums, hidden, exp_local, ff_dim, tile
+    sources, results, aliases, moves, spread, halve, tokens, weights, masks, digits, hop, sums, hidden, exp_local, ff_dim, tile
 ):
     rows, model = 2 * tokens[0].shape[0], tokens[0].shape[1]
     steps = rows // tile
@@ -874,15 +1291,21 @@
         in_specs += [per_tile(), per_tile()]
         args += list(sums)
     wide = exp_local * ff_dim
+    part = weights.shape[0] // 4
+    cut = part // 32 * 16
     scratch = [
         pltpu.VMEM((rows, wide), jnp.bfloat16),
         pltpu.VMEM((rows, wide + ROUTER_ROWS), jnp.bfloat16),
         pltpu.VMEM((rows, model), jnp.bfloat16),
         pltpu.VMEM((rows, model), jnp.bfloat16),
         pltpu.SemaphoreType.DMA((2, steps)),
-        pltpu.SemaphoreType.DMA((len(moves),)),
-        pltpu.SemaphoreType.DMA((len(moves),)),
+        pltpu.SemaphoreType.DMA((max(1, len(moves)),)),
+        pltpu.SemaphoreType.DMA((max(1, len(moves)),)),
     ]
+    if spread is not None:
+        scratch.append(pltpu.SemaphoreType.DMA((2, 6)))
+    if halve is not None:
+        scratch += halving_buffers(part, cut, model)
     if last:
         in_specs.append(late())
         args.append(hidden)
@@ -900,9 +1323,12 @@
     else:
         out_specs = [per_tile(), per_tile()]
         out_shape = [jax.ShapeDtypeStruct((rows, model), jnp.float32)] * 2
+    if halve is not None:
+        out_specs.append(whole_block((part, model)))
+        out_shape.append(jax.ShapeDtypeStruct((part, model), jnp.bfloat16))
     outs = pl.pallas_call(
         functools.partial(
-            expert_body, first, last, exp_local, ff_dim, tile, steps, moves, len(sources), len(results)
+            expert_body, first, last, exp_local, ff_dim, tile, steps, moves, spread, halve, len(sources), len(results)
         ),
         grid=(steps,),
         in_specs=in_specs,
@@ -927,56 +1353,8 @@
     return lax.ppermute(arr, "expert", [(i, i ^ 1) for i in range(size)])
 
 
-def chip_shift(arr, hop):
-    size = lax.axis_size("expert")
-    chips = size // 2
-    return lax.ppermute(
-        arr, "expert", [(i, (i // 2 + hop) % chips * 2 + i % 2) for i in range(size)]
-    )
-
-
-def dp_swap(arr, flip):
-    return lax.ppermute(arr, "dp", [(i, i ^ flip) for i in range(lax.axis_size("dp"))])
-
-
 def row_part(arr, index, count):
     return lax.dynamic_slice_in_dim(arr, index * (arr.shape[0] // count), arr.shape[0] // count, 0)
-
-
-def dp_gather(part):
-    mine = lax.axis_index("dp")
-    rows = part.shape[0]
-    whole = jnp.zeros((4 * rows,) + part.shape[1:], part.dtype)
-    for flip in range(4):
-        piece = part if flip == 0 else dp_swap(part, flip)
-        whole = lax.dynamic_update_slice_in_dim(whole, piece, (mine ^ flip) * rows, 0)
-    return whole
-
-
-def dp_scatter(whole):
-    mine = lax.axis_index("dp")
-    total = row_part(whole, mine, 4).astype(jnp.float32)
-    for flip in range(1, 4):
-        total = total + dp_swap(row_part(whole, mine ^ flip, 4), flip).astype(jnp.float32)
-    return total
-
-
-def scatter_rows(whole):
-    dev_count = lax.axis_size("expert")
-    chips = dev_count // 2
-    rows, width = whole.shape
-    mine = lax.axis_index("expert")
-    chip, core = mine // 2, mine % 2
-    by_core = whole.reshape(4 * chips, 2, rows // (8 * chips), width)
-    kept = lax.dynamic_index_in_dim(by_core, core, 1, keepdims=False)
-    given = lax.dynamic_index_in_dim(by_core, 1 - core, 1, keepdims=False)
-    pair = (kept.astype(jnp.float32) + core_swap(given).astype(jnp.float32)).astype(jnp.bfloat16)
-    quarter = dp_scatter(pair.reshape(rows // 2, width)).astype(jnp.bfloat16)
-    total = row_part(quarter, chip, chips).astype(jnp.float32)
-    for hop in range(1, chips):
-        piece = row_part(quarter, (chip + hop) % chips, chips)
-        total = total + chip_shift(piece, hop).astype(jnp.float32)
-    return total
 
 
 def own_weights(w_router, w_in, w_out):
@@ -1044,9 +1422,13 @@
     wqk = jnp.concatenate([w_query, w_key], axis=1)
     wsel = jnp.pad(w_select, ((0, 0), (0, LANE - gates)))
 
-    second, cot_far, sent_far, hidden, normed, q_rot, k_rot, value_bf, value_all, attended, sig, lse, mixed, sent = (
+    shape = own.shape
+    part = shape[0] // 4
+    ahead = part // 80 * 64
+    third, first, cot_far, sent_far, hidden, normed, q_rot, k_rot, value_bf, value_all, attended, sig, lse, mixed, sent = (
         attention_forward(
-            own, cotangent, layer_input, start, keep, cos_two, sin_two, att_mask, gain_row, wqk, wsel, w_value, w_output, TILE
+            ahead, own, cotangent, layer_input, start, keep, cos_two, sin_two, att_mask, gain_row, wqk, wsel, w_value,
+            w_output, TILE,
         )
     )
 
@@ -1061,78 +1443,78 @@
         (place >= 0) & (place < DIGITS), (counts >> (2 * jnp.clip(place, 0, DIGITS))) & 3, 0
     ).astype(jnp.float32)
 
-    part = own.shape[0] // 4
-    shape, three = own.shape, (3 * part, model)
-
-    def run(hop, sources, results, aliases, moves, weights, sums, last_hidden):
+    def run(hop, sources, results, aliases, moves, spread, halve, weights, sums, last_hidden):
         return expert_chunk(
-            sources, results, aliases, moves, (sent, sent_far, cotangent, cot_far), weights, masks, digits, hop, sums,
-            last_hidden, exp_local, ff_dim, TILE,
-        )
-
-    def sum_parts(whole, three_parts):
-        total = row_part(whole, lax.axis_index("dp"), 4).astype(jnp.float32)
-        for flip in range(3):
-            total = total + three_parts[flip * part : (flip + 1) * part].astype(jnp.float32)
-        return total
-
-    (second, third, first), sums, grad_0 = run(
+            sources, results, aliases, moves, spread, halve, (sent, sent_far, cotangent, cot_far), weights,
+            masks, digits, hop, sums, last_hidden, exp_local, ff_dim, TILE,
+        )
+
+    middle = (ahead + shape[0]) // 32 * 16
+    (third, second), sums, grad_0 = run(
         0,
-        [second, own],
-        [shape, shape, shape],
+        [third, own],
+        [shape, shape],
         {0: 0},
-        gather_moves(0, 0, part)
-        + shift_move(1, 1, -3, own_part(part), own_part(part), part)
-        + shift_move(1, 2, -1, fixed(0), fixed(0), part),
+        shift_move(1, 1, -2, own_part(part), own_part(part), part),
+        0,
+        None,
         own,
         None,
         None,
     )
-    (third, first), sums, grad_2 = run(
-        2,
-        [third, first, own],
+    (second, first), sums, grad_3 = run(
+        3,
+        [second, first, own],
         [shape, shape],
         {0: 0, 1: 1},
-        gather_moves(0, 0, part) + shift_move(2, 1, -1, fixed(part), fixed(part), 2 * part),
+        shift_move(2, 1, -1, fixed(ahead), fixed(ahead), middle - ahead),
+        0,
+        None,
+        third,
+        sums,
+        None,
+    )
+    (first,), (*sums, part_3), grad_2 = run(
+        2,
+        [first, own, grad_3],
+        [shape],
+        {0: 0},
+        shift_move(1, 0, -1, fixed(middle), fixed(middle), shape[0] - middle),
+        None,
+        2,
         second,
         sums,
         None,
     )
-    (first, from_2), sums, grad_3 = run(
-        3,
-        [first, own, grad_2],
-        [shape, three],
-        {0: 0},
-        shift_move(1, 0, -1, fixed(3 * part), fixed(3 * part), part) + scatter_moves(2, 1, part),
-        third,
-        sums,
+    (got_3,), (layer_output, dhidden, dy, part_2), grad_1 = run(
+        1,
+        [grad_2, part_3],
+        [(part, model)],
+        {},
+        shift_move(1, 0, 3, fixed(0), fixed(0), part),
         None,
-    )
-    part_2 = sum_parts(grad_2, from_2).astype(jnp.bfloat16)
-    (from_3, got_2), (layer_output, dhidden, dy), grad_1 = run(
-        1,
-        [grad_3, part_2],
-        [three, (part, model)],
-        {},
-        scatter_moves(0, 0, part) + shift_move(1, 1, 2, fixed(0), fixed(0), part),
+        0,
         first,
         sums,
         hidden,
     )
-    part_3 = sum_parts(grad_3, from_3).astype(jnp.bfloat16)
-    out_joined = outer_products([dy, mixed], [[(0, 1)]], 1, TILE)
-    from_0, got_3, grad_input, dqk, dval, dlog, gain_rows = attention_backward(
-        [grad_0, part_3],
-        [three, (part, model)],
-        scatter_moves(0, 0, part) + shift_move(1, 1, 3, fixed(0), fixed(0), part),
+    got_2, grad_input, dqk, dval, dlog, gain_rows, part_1, part_0 = attention_backward(
+        [grad_1, grad_0, part_2],
+        [(part, model)],
+        shift_move(2, 0, 2, fixed(0), fixed(0), part),
+        (0, 1),
+        part,
         dy, q_rot, k_rot, value_bf, attended, lse, start, keep, sig, att_mask, cos_two, sin_two,
         layer_input, value_all, dhidden, gain_row, wqk, wsel, w_value, w_output, TILE,
     )
-    out_sum = scatter_rows(out_joined).T
-    part_1 = dp_scatter(grad_1).astype(jnp.bfloat16)
-    total = sum_parts(grad_0, from_0) + got_2.astype(jnp.float32) + got_3.astype(jnp.float32)
-    total = total + chip_shift(part_1, 1).astype(jnp.float32)
-    summed = dp_gather(total.astype(jnp.bfloat16)).astype(jnp.float32)
+    unit = (
+        (jnp.arange(GAIN_ROWS)[:, None] < 2) & (jnp.arange(LANE)[None, :] == gates)
+    ).astype(jnp.bfloat16)
+    dense, summed = tail(
+        part_1, part_0, got_2, got_3, dy, layer_input, normed, gain_rows, mixed, dval, dlog, dqk, unit, shape, chips
+    )
+    summed = summed.astype(jnp.float32)
+    out_sum, dense = dense[:, :wide].T, dense[:, wide:]
     grad_w_in = jnp.swapaxes(summed[:moe_wide].reshape(exp_local, ff_dim, model), 1, 2)
     extra = summed[moe_wide : moe_wide + ROUTER_ROWS]
     grad_router = extra[:exp_local]
@@ -1140,25 +1522,15 @@
     tally = sum(parts[i] << (2 * i) for i in range(DIGITS))
     grad_w_out = summed[moe_wide + ROUTER_ROWS :].reshape(exp_local, ff_dim, model)
 
-    unit = (
-        (jnp.arange(GAIN_ROWS)[:, None] < 2) & (jnp.arange(LANE)[None, :] == gates)
-    ).astype(jnp.bfloat16)
-    joined = outer_products(
-        [layer_input, normed, gain_rows, dval, dlog, dqk, unit],
-        [[(0, 3)], [(0, 4), (2, 6)], [(1, 5)]],
-        3,
-        TILE,
-    )
-    summed = scatter_rows(joined)
     at_qk = wide + LANE
     return (
         layer_output,
         grad_input,
-        summed[:, wide + gates],
-        summed[:, at_qk : at_qk + narrow],
-        summed[:, at_qk + narrow : at_qk + 2 * narrow],
-        summed[:, wide : wide + gates],
-        summed[:, :wide],
+        dense[:, wide + gates],
+        dense[:, at_qk : at_qk + narrow],
+        dense[:, at_qk + narrow : at_qk + 2 * narrow],
+        dense[:, wide : wide + gates],
+        dense[:, :wide],
         out_sum,
         grad_router,
         grad_w_in,

time: 520 us -> 428 us (0.82)
  the two profiles are of different devices: /device:TPU:12 before, /device:TPU:0 now
where the time goes in v4:
time: 428 us; the launch traced here: 419 us
  Pallas kernels  378 us (88%)
  local copies, waits for them, and re-layouts  23 us (5%)
  other arithmetic  14.3 us (3%)
    pallas_call x4, Pallas kernels, expert_chunk(): pl.pallas_call(functools.partial(expert_body, first, last, exp_local, ff_...  164 us
    pallas_call x1, Pallas kernels, tail(): pl.pallas_call(functools.partial(tail_body, blocks, chips, part, cut), in...  102 us
    pallas_call x1, Pallas kernels, attention_backward(): pl.pallas_call(functools.partial(backward_body, heads, tile, steps, moves...  65.9 us
    pallas_call x1, Pallas kernels, attention_forward(): pl.pallas_call(functools.partial(forward_body, heads, tile, rows // tile,...  46.2 us
  transfers between devices with their start and end apart: 1, of which 0 were waited for; matrix products, arithmetic and copies ran while one was open for 4% of the time, Pallas kernels for 11%

profile of v4, /device:TPU:0, one launch (start us, length us, event | category | flops | bytes accessed | tf_op | source)
XLA Modules:
  0.0 419.4 jit_solution(15751506653237873934)
XLA Ops:
  0.7 1.3 fusion.5
  1.9 0.5 collective-permute-start
  2.5 0.8 slice_compare_fusion
  3.4 0.1 add_reduce_fusion
  3.5 0.3 reduce-window.6
  3.7 0.2 slice_reduce_fusion.1
  3.9 0.2 reduce-window.9
  4.1 0.1 fusion.18
  4.2 0.1 broadcast.244
  4.3 1.0 copy.66.refs_3_.refs_9_
  5.3 1.7 copy.61
  7.1 0.0 copy-done.3
  7.1 1.0 constant_dynamic-update-slice_fusion.1
  8.2 0.1 copy.63
  8.3 0.2 copy.64
  8.5 0.0 copy-done.5
  8.5 0.2 copy.65
  8.7 0.8 pad.10.refs_7_.refs_12_.refs_16_
  9.4 0.8 pad.11.refs_10_.refs_24_
  10.2 1.9 fusion.11
  12.1 2.3 constant_dynamic-update-slice_fusion.refs_9_.refs_23_
  14.4 0.7 and_convert_fusion.refs_12_
  15.0 1.3 pad_maximum_fusion
  16.3 0.0 copy-done.2
  16.3 2.0 fusion.3.refs_0_.refs_1_.refs_6_.refs_2_
  18.3 46.2 %shard_map.247 = (bf16[1600,1024]{1,0:T(8,128)(2,1)}, bf16[1600,1024]{1,0:T(8,128)(2,1)}, bf16[1024,1024]{1,0:T(8,128)(2,1)}, bf16[1024,1024]{1,0:T(8,128)(2,1)}...) custom-call(bf16[1600,1024]{1,0:T(8,128)(2,1)} %fusion.3.refs_0_.ref, ...), custom_call_target="tpu_custom_call" | custom-call | flops 12884901888 | bytes 41943040 | tf_op jit(solution)/shard_map/pallas_call | solution.py:573
  64.5 0.0 collective-permute-done
  64.5 2.0 fusion.32
  66.6 0.7 select_convert_fusion.refs_8_.refs_9_
  67.3 43.5 %shard_map.248 = (bf16[1600,1024]{1,0:T(8,128)(2,1)}, bf16[1600,1024]{1,0:T(8,128)(2,1)}, f32[2048,1024]{1,0:T(8,128)}, f32[2048,1024]{1,0:T(8,128)}, bf16[1600,1024]{1,0:T(8,128)(2,1)}) custom-call(bf16[1600,1024]{1,0:T(8,128)(2,1)} %get-tuple-element.70.refs_0_, ...), custom_call_target="tpu_custom_call", output_to_operand_aliasing={{0}: (0, {})} | custom-call | flops 19327352832 | bytes 41943040 | tf_op jit(solution)/shard_map/pallas_call | solution.py:1329
  110.7 39.9 %shard_map.249 = (bf16[1600,1024]{1,0:T(8,128)(2,1)}, bf16[1600,1024]{1,0:T(8,128)(2,1)}, f32[2048,1024]{1,0:T(8,128)}, f32[2048,1024]{1,0:T(8,128)}, bf16[1600,1024]{1,0:T(8,128)(2,1)}) custom-call(bf16[1600,1024]{1,0:T(8,128)(2,1)} %get-tuple-element.74.refs_0_, ...), custom_call_target="tpu_custom_call", output_to_operand_aliasing={{0}: (0, {}), {1}: (1, {})} | custom-call | flops 19327352832 | bytes 41943040 | tf_op jit(solution)/shard_map/pallas_call | solution.py:1329
  150.7 40.1 %shard_map.250 = (bf16[1600,1024]{1,0:T(8,128)(2,1)}, f32[2048,1024]{1,0:T(8,128)}, f32[2048,1024]{1,0:T(8,128)}, bf16[400,1024]{1,0:T(8,128)(2,1)}, bf16[1600,1024]{1,0:T(8,128)(2,1)}) custom-call(bf16[1600,1024]{1,0:T(8,128)(2,1)} %get-tuple-element.79.refs_0_, ...), custom_call_target="tpu_custom_call", output_to_operand_aliasing={{0}: (0, {})} | custom-call | flops 19327352832 | bytes 41943040 | tf_op jit(solution)/shard_map/pallas_call | solution.py:1329
  190.8 40.4 %shard_map.251 = (bf16[400,1024]{1,0:T(8,128)(2,1)}, bf16[1024,1024]{1,0:T(8,128)(2,1)}, f32[1024,1024]{1,0:T(8,128)}, bf16[1024,1024]{1,0:T(8,128)(2,1)}, bf16[...) custom-call(bf16[1600,1024]{1,0:T(8,128)(2,1)} %get-tuple-element.84.refs_0_, ...), custom_call_target="tpu_custom_call" | custom-call | flops 19327352832 | bytes 41943040 | tf_op jit(solution)/shard_map/pallas_call | solution.py:1329
  231.2 65.9 %shard_map.252 = (bf16[400,1024]{1,0:T(8,128)(2,1)}, bf16[1024,1024]{1,0:T(8,128)(2,1)}, bf16[1024,1024]{1,0:T(8,128)(2,1)}, bf16[1024,2560]{1,0:T(8,128)(2,1)},...) custom-call(bf16[1600,1024]{1,0:T(8,128)(2,1)} %get-tuple-element.91, ...), custom_call_target="tpu_custom_call" | custom-call | flops 12884901888 | bytes 52428800 | tf_op jit(solution)/shard_map/pallas_call | solution.py:797
  297.1 102.3 %shard_map.253 = (f32[32,6272]{1,0:T(8,128)}, bf16[1600,1024]{1,0:T(8,128)(2,1)}) custom-call(bf16[400,1024]{1,0:T(8,128)(2,1)} %get-tuple-element.104.refs_0_, bf16[400,1024]{1,0:T(8,128)(2,1)} %get-tuple-element.105.refs_1_, bf16[400,1024]{1,0:T(8,128)(2,1)} %get-tuple-element.106.refs_2_, bf16[400,1024]{1,0:T(8,128)(2,1)} %get-tuple-element.107.refs_3_, ...), custom_call_target="tpu_custom_call" | custom-call | flops 13153337344 | bytes 20971520 | tf_op jit(solution)/shard_map/pallas_call | solution.py:1071
  399.4 4.4 %fusion.33 = (f32[768,1024]{1,0:T(8,128)}, f32[768,1024]{1,0:T(8,128)S(1)}) fusion(bf16[1600,1024]{1,0:T(8,128)(2,1)} %get-tuple-element.115), kind=kLoop, calls=%fused_computation.69 | loop fusion | bytes 12582912 | tf_op jit(solution)/shard_map/slice | solution.py:1523
  403.8 3.5 convert_element_type.50
  407.3 0.9 slice_bitcast_fusion
  408.2 0.7 fusion.34
  408.8 0.6 slice.101
  409.4 0.6 slice.89
  410.0 0.7 slice_reduce_fusion
  410.7 2.4 copy.68
  413.1 0.9 slice_convert_fusion
  413.9 0.0 copy-done.8
  413.9 0.5 bitcast_add_fusion
  414.5 3.1 copy.76
  417.6 1.3 copy.77
  (28 shorter events, 0.2 us)
Async XLA Ops:
  0.6 6.4 %copy-start.3 = (bf16[1024,512]{1,0:T(8,128)(2,1)S(1)}, bf16[1024,512]{1,0:T(8,128)(2,1)}, u32[]{:S(2)}) copy-start(bf16[1024,512]{1,0:T(8,128)(2,1)} %param.25) | copy-start | bytes 3145732
  0.7 7.5 %copy-start.6 = (s32[1024,8,2]{0,2,1:T(2,128)S(1)}, s32[1024,8,2]{0,2,1:T(2,128)}, u32[]{:S(2)}) copy-start(s32[1024,8,2]{0,2,1:T(2,128)} %param.21) | copy-start | bytes 196612
  1.9 62.6 %collective-permute-start = (bf16[1024,48]{0,1:T(8,128)(2,1)S(1)}, bf16[1024,48]{0,1:T(8,128)(2,1)S(1)}, u32[]{:S(2)}, u32[]{:S(2)}) collective-permute-start(bf16[1024,48]{0,1:T(8,128)(2,1)S(1)} %fusion.5), channel_id=1, source_target_pairs={{0,1},{1,0},{2,3},{3,2},{4,5},{5,4},{6,7},{7,6},{8,9},{9,8},{10,11... | collective-permute-start | bytes 294920 | tf_op jit(solution)/shard_map/ppermute | solution.py:1353
  5.3 3.2 copy-start.5
  10.2 6.2 %copy-start.2 = (bf16[6,128,1024]{2,1,0:T(8,128)(2,1)S(1)}, bf16[6,128,1024]{2,1,0:T(8,128)(2,1)}, u32[]{:S(2)}) copy-start(bf16[6,128,1024]{2,1,0:T(8,128)(2,1)} %param.32) | copy-start | bytes 4718596
  10.2 6.2 %copy-start.7 = (bf16[6,1024]{1,0:T(8,128)(2,1)S(1)}, bf16[6,1024]{1,0:T(8,128)(2,1)}, u32[]{:S(2)}) copy-start(bf16[6,1024]{1,0:T(8,128)(2,1)} %param.30) | copy-start | bytes 36868
  399.4 4.4 %copy-start = (bf16[1600,1024]{1,0:T(8,128)(2,1)S(1)}, bf16[1600,1024]{1,0:T(8,128)(2,1)}, u32[]{:S(2)}) copy-start(bf16[1600,1024]{1,0:T(8,128)(2,1)} %get-tuple-element.115) | copy-start | bytes 9830404
  403.8 3.5 copy-start.4
  408.8 5.1 %copy-start.8 = (s32[6]{0:T(128)S(1)}, s32[6]{0:T(128)}, u32[]{:S(2)}) copy-start(s32[6]{0:T(128)} %param.23) | copy-start | bytes 76
  413.1 4.5 %copy-start.1 = (bf16[1024,1024]{1,0:T(8,128)(2,1)S(1)}, bf16[1024,1024]{1,0:T(8,128)(2,1)}, u32[]{:S(2)}) copy-start(bf16[1024,1024]{1,0:T(8,128)(2,1)} %get-tuple-element.143) | copy-start | bytes 6291460
